TPU v7x, 512 devices: a whole 4x4x16 slice. The times are simulated.
512 devices in a mesh: grid: 64 (over z_lo, y, core), orb: 8 (over z_hi, x).
Axes of the slice: x: 4, y: 4, z: 16 (z_hi: 2, z_lo: 8; z = z_hi * 8 + z_lo), core: 2. Of those that a mesh axis runs over, the one named last changes fastest.
Arguments:
- occupied: bfloat16 [80, 6400, 1024], P(None, 'grid', 'orb'), may hold values from -6 to 6
- virtual: bfloat16 [80, 6400, 1024], P(None, 'grid', 'orb'), may hold values from -6 to 6
- points: int32 [128], replicated, may hold values from 0 to 511999, as said below
- panels: int32 [2, 64], replicated, may hold values from 0 to 127, as said below
Outputs:
- projection: float32 [64, 64], P('orb')
Inputs may be any that keep to these rules, and one draw needn't show every extreme that they name: `points`: the 128 cells are distinct. Every index of points appears exactly once in panels, so the two panels are disjoint.
All inputs are finite; a program needn't handle non-finite values.
Results may differ from a plain program's by a relative error of at most 0.0003.
Values may be sent and summed in bfloat16 or wider, within the bound.
No kernel may reach another device: no remote copies, remote signals or barrier semaphores. Data moves between devices by JAX's collectives and lax.ppermute only.
A program may use at most 64 MiB of HBM per device.

v0:
```python
import math

import jax
import jax.numpy as jnp
from jax import lax
from jax.sharding import PartitionSpec as P

NB = 80
NC = 80


FOUR_PI = 4.0 * math.pi
TWO_PI = 2.0 * math.pi


def wave_table(length):
    steps = jnp.arange(length, dtype=jnp.int32)
    angle = TWO_PI / length * (steps[:, None] * steps[None, :] % length).astype(jnp.float32)
    return (jnp.cos(angle), jnp.sin(angle))


def signed_square(steps, length):
    shifted = jnp.where(steps > length // 2, steps - length, steps).astype(jnp.float32)
    wave = TWO_PI / length * shifted
    return wave * wave


def apply_table(form, table, values):
    return jnp.einsum(
        form, table, values, precision=lax.Precision.HIGHEST, preferred_element_type=jnp.float32
    )


def gram_solve(factor, values):
    lowered = lax.linalg.triangular_solve(factor, values, left_side=True, lower=True)
    return lax.linalg.triangular_solve(
        factor, lowered, left_side=True, lower=True, transpose_a=True
    )


def plane_spectra(spec_real, spec_imag):
    field_count, first_len, slab_width = spec_real.shape
    stacked = jnp.stack([spec_real, spec_imag]).reshape(2, field_count * first_len, slab_width)
    planes = lax.all_to_all(stacked, "grid", split_axis=1, concat_axis=2, tiled=True)
    plane_count = planes.shape[1]
    real_part = planes[0].reshape(plane_count, NB, NC)
    imag_part = planes[1].reshape(plane_count, NB, NC)
    cos_b, sin_b = wave_table(NB)
    cos_c, sin_c = wave_table(NC)
    real_part, imag_part = (
        apply_table("pb,tbc->tpc", cos_b, real_part) + apply_table("pb,tbc->tpc", sin_b, imag_part),
        apply_table("pb,tbc->tpc", cos_b, imag_part) - apply_table("pb,tbc->tpc", sin_b, real_part),
    )
    real_part, imag_part = (
        apply_table("qc,tbc->tbq", cos_c, real_part) + apply_table("qc,tbc->tbq", sin_c, imag_part),
        apply_table("qc,tbc->tbq", cos_c, imag_part) - apply_table("qc,tbc->tbq", sin_c, real_part),
    )
    plane_ids = lax.axis_index("grid") * plane_count + jnp.arange(plane_count, dtype=jnp.int32)
    squared = (
        signed_square(plane_ids % first_len, first_len)[:, None, None]
        + signed_square(jnp.arange(NB, dtype=jnp.int32), NB)[None, :, None]
        + signed_square(jnp.arange(NC, dtype=jnp.int32), NC)[None, None, :]
    )
    positive = jnp.where(squared > 0, squared, 1.0)
    kernel = jnp.where(squared > 0, FOUR_PI / positive, 0.0) / (first_len * NB * NC)
    real_part = real_part * kernel
    imag_part = imag_part * kernel
    real_part, imag_part = (
        apply_table("qc,tbc->tbq", cos_c, real_part) - apply_table("qc,tbc->tbq", sin_c, imag_part),
        apply_table("qc,tbc->tbq", cos_c, imag_part) + apply_table("qc,tbc->tbq", sin_c, real_part),
    )
    real_part, imag_part = (
        apply_table("pb,tbc->tpc", cos_b, real_part) - apply_table("pb,tbc->tpc", sin_b, imag_part),
        apply_table("pb,tbc->tpc", cos_b, imag_part) + apply_table("pb,tbc->tpc", sin_b, real_part),
    )
    restacked = jnp.stack([real_part, imag_part]).reshape(2, plane_count, NB * NC)
    returned = lax.all_to_all(restacked, "grid", split_axis=2, concat_axis=1, tiled=True)
    return (
        returned[0].reshape(field_count, first_len, slab_width),
        returned[1].reshape(field_count, first_len, slab_width),
    )


def shards(occupied, virtual, points, panels):
    grid_rank = lax.axis_index("grid")
    orb_count = lax.axis_size("orb")
    first_len, slab_width, occ_local = occupied.shape
    vir_local = virtual.shape[2]
    row_count = first_len * slab_width
    part_rows = row_count // orb_count
    plane_width = slab_width * lax.axis_size("grid")
    panel_size = panels.shape[1]
    chosen = points[panels.reshape(-1)]
    plane_of = chosen // plane_width
    within = chosen % plane_width - grid_rank * slab_width
    inside = (within >= 0) & (within < slab_width)
    local_rows = jnp.where(inside, plane_of * slab_width + within, 0)
    flat_occ = occupied.reshape(row_count, occ_local)
    flat_vir = virtual.reshape(row_count, vir_local)
    occ_here = jnp.where(inside[:, None], flat_occ[local_rows].astype(jnp.float32), 0.0)
    vir_here = jnp.where(inside[:, None], flat_vir[local_rows].astype(jnp.float32), 0.0)
    occ_sum, vir_sum = lax.psum((occ_here, vir_here), "grid")
    occ_pts, vir_pts = (
        lax.all_gather(occ_sum.astype(jnp.bfloat16), "orb", axis=1, tiled=True),
        lax.all_gather(vir_sum.astype(jnp.bfloat16), "orb", axis=1, tiled=True),
    )

    def hadamard_gram(start):
        occ_part = occ_pts[start : start + panel_size]
        vir_part = vir_pts[start : start + panel_size]
        return jnp.dot(occ_part, occ_part.T, preferred_element_type=jnp.float32) * jnp.dot(
            vir_part, vir_part.T, preferred_element_type=jnp.float32
        )

    chol_fit = jnp.linalg.cholesky(hadamard_gram(0))
    chol_bra = jnp.linalg.cholesky(hadamard_gram(panel_size))
    occ_side = jnp.dot(
        lax.all_to_all(
            flat_occ.reshape(orb_count, part_rows, occ_local),
            "orb",
            split_axis=0,
            concat_axis=2,
            tiled=True,
        )[0],
        occ_pts.T,
        preferred_element_type=jnp.float32,
    )
    vir_side = jnp.dot(
        lax.all_to_all(
            flat_vir.reshape(orb_count, part_rows, vir_local),
            "orb",
            split_axis=0,
            concat_axis=2,
            tiled=True,
        )[0],
        vir_pts.T,
        preferred_element_type=jnp.float32,
    )
    pairs = (occ_side * vir_side)[None][0]
    fit_cols = gram_solve(chol_fit, pairs[:, :panel_size].T)
    bra_cols = gram_solve(chol_bra, pairs[:, panel_size:].T)
    slab_cols = lax.all_to_all(fit_cols, "orb", split_axis=0, concat_axis=1, tiled=True)
    column_count = slab_cols.shape[0]
    slab_cols = slab_cols.reshape(column_count, first_len, slab_width)
    cos_a, sin_a = wave_table(first_len)
    spec_real = apply_table("fa,kaj->kfj", cos_a, slab_cols)
    spec_imag = -apply_table("fa,kaj->kfj", sin_a, slab_cols)
    back_real, back_imag = plane_spectra(spec_real, spec_imag)
    potential = apply_table("fa,kaj->kfj", cos_a, back_real) - apply_table(
        "fa,kaj->kfj", sin_a, back_imag
    )
    pot_rows = lax.all_to_all(
        potential.reshape(column_count, row_count), "orb", split_axis=1, concat_axis=0, tiled=True
    )
    partial_value = 32.0 * jnp.dot(
        bra_cols, pot_rows.T, precision=lax.Precision.HIGHEST, preferred_element_type=jnp.float32
    )
    summed = lax.psum(partial_value, "grid")
    return lax.psum_scatter(summed, "orb", scatter_dimension=0, tiled=True)


def solution(mesh):
    in_specs = (P(None, "grid", "orb"), P(None, "grid", "orb"), P(), P())
    out_specs = P("orb", None)
    return jax.shard_map(shards, mesh=mesh, in_specs=in_specs, out_specs=out_specs, check_vma=False)
```

profile of v0, /device:TPU:1, one launch (start us, length us, event | category | flops | bytes accessed | tf_op | source)
XLA Modules:
  0.0 1210.4 jit_solution(18314718947268039931)
XLA Ops:
  0.0 2.1 copy.57
  3.6 18.1 %all-to-all-start = ((bf16[8,1000,128]{2,1,0:T(8,128)(2,1)}), bf16[8,1000,128]{2,1,0:T(8,128)(2,1)}, u32[]{:S(2)}, u32[]{:S(2)}) async-start(bf16[8,1000,128]{2,1,0:T(8,128)(2,1)} %reshape_reshape.6), calls=%async_computation | async-start | bytes 4096000 | tf_op jit(solution)/shard_map/all_to_all | solution.py:118
  21.7 3.5 copy.58
  25.2 3.8 reshape_reshape.7
  29.0 37.0 %all-to-all-done = bf16[8,1000,128]{2,1,0:T(8,128)(2,1)} async-done(((bf16[8,1000,128]{2,1,0:T(8,128)(2,1)}), bf16[8,1000,128]{2,1,0:T(8,128)(2,1)}, u32[]{:S(2)}, u32[]{:S(2)}) %all-to-all-start) | async-done | bytes 2048032 | tf_op jit(solution)/shard_map/all_to_all | solution.py:118
  66.0 6.5 all-to-all-start.1
  72.5 3.9 reshape.237
  79.3 2.5 gather_fusion.2
  81.7 2.5 gather_fusion.1
  84.3 507.5 %all-reduce.3 = (bf16[128,128]{1,0:T(8,128)(2,1)S(1)}, bf16[128,128]{1,0:T(8,128)(2,1)S(1)}) all-reduce(f32[128,128]{1,0:T(8,128)S(1)} %get-tuple-element.15, f32[128,128]{1,0:T(8,128)S(1)} %get-tuple-element.14), channel_id=1, replica_groups=mesh['grid'=64,'orb'=8] {'grid'}, use_global_device_ids=true, to_apply=%region_0.1 | all-reduce | flops 32768 | bytes 196608 | tf_op jit(solution)/shard_map/psum | solution.py:102
  591.9 60.8 %all_gather.6 = bf16[128,1024]{1,0:T(8,128)(2,1)S(1)} all-gather(bf16[128,128]{1,0:T(8,128)(2,1)S(1)} %get-tuple-element.6), channel_id=1, replica_groups=mesh['grid'=64,'orb'=8] {'orb'}, dimensions={1}, use_global_device_ids=true | all-gather | bytes 294912 | tf_op jit(solution)/shard_map/all_gather | solution.py:104
  652.7 54.7 %all_gather.7 = bf16[128,1024]{1,0:T(8,128)(2,1)S(1)} all-gather(bf16[128,128]{1,0:T(8,128)(2,1)S(1)} %get-tuple-element.8), channel_id=1, replica_groups=mesh['grid'=64,'orb'=8] {'orb'}, dimensions={1}, use_global_device_ids=true | all-gather | bytes 294912 | tf_op jit(solution)/shard_map/all_gather | solution.py:105
  707.9 5.8 cholesky.55
  715.0 4.9 custom-call.13
  719.9 2.9 copy.63
  723.8 2.9 copy.65
  728.7 26.5 %all_to_all.95 = f32[8,8,1000]{2,1,0:T(8,128)S(1)} all-to-all(f32[8,8,1000]{2,1,0:T(8,128)S(1)} %convolution_bitcast_fusion), channel_id=1, replica_groups=mesh['grid'=64,'orb'=8] {'orb'}, dimensions={0} | all-to-all | bytes 512000 | tf_op jit(solution)/shard_map/all_to_all | solution.py:142
  758.4 23.2 %all-to-all-start.3 = ((f32[2,640,100]{2,0,1:T(2,128)}), f32[2,640,100]{2,0,1:T(2,128)S(1)}, u32[]{:S(2)}, u32[]{:S(2)}) async-start(f32[2,640,100]{2,0,1:T(2,128)} %pad_maximum_fusion.1), calls=%async_computation.3 | async-start | bytes 1310720 | tf_op jit(solution)/shard_map/all_to_all | solution.py:44
  781.7 35.4 %all-to-all-done.3 = f32[2,640,100]{2,0,1:T(2,128)S(1)} async-done(((f32[2,640,100]{2,0,1:T(2,128)}), f32[2,640,100]{2,0,1:T(2,128)S(1)}, u32[]{:S(2)}, u32[]{:S(2)}) %all-to-all-start.3) | async-done | bytes 512032 | tf_op jit(solution)/shard_map/all_to_all | solution.py:44
  832.6 5.9 copy.88
  838.5 10.2 reshape.278
  848.7 7.3 all-to-all-start.4
  856.5 5.8 cholesky.44
  862.4 23.7 %all-to-all-done.4 = f32[64,1,2000]{2,1,0:T(1,128)S(1)} async-done(((f32[64,1,2000]{2,1,0:T(1,128)}), f32[64,1,2000]{2,1,0:T(1,128)S(1)}, u32[]{:S(2)}, u32[]{:S(2)}) %all-to-all-start.4) | async-done | bytes 512032 | tf_op jit(solution)/shard_map/all_to_all | solution.py:77
  886.6 1.9 reduce.4
  888.5 10.5 reshape.279
  899.0 6.4 copy.109
  908.2 3.4 all-to-all-start.5
  912.9 4.9 custom-call.11
  921.0 5.5 all-to-all-done.5
  926.9 65.1 %all-reduce = f32[64,64]{1,0:T(8,128)S(1)} all-reduce(f32[64,64]{1,0:T(8,128)S(1)} %convolution_multiply_fusion.3), channel_id=2, replica_groups=mesh['grid'=64,'orb'=8] {'orb'}, use_global_device_ids=true, to_apply=%region_5.9.clone | all-reduce | flops 4096 | bytes 32768
  992.0 218.1 %psum.24 = f32[8,64]{1,0:T(8,128)} all-reduce(f32[8,64]{1,0:T(8,128)S(1)} %constant_dynamic-slice_fusion), channel_id=1, replica_groups=mesh['grid'=64,'orb'=8] {'grid'}, use_global_device_ids=true, to_apply=%region_4.8 | all-reduce | flops 512 | bytes 4096 | tf_op jit(solution)/shard_map/psum | solution.py:158
  (86 shorter events, 35.8 us)
Async XLA Ops:
  0.0 78.0 %copy-start = (s32[128]{0:T(128)S(1)}, s32[128]{0:T(128)}, u32[]{:S(2)}) copy-start(s32[128]{0:T(128)} %param.11) | copy-start | bytes 1540
  3.6 62.4 %all-to-all-start = ((bf16[8,1000,128]{2,1,0:T(8,128)(2,1)}), bf16[8,1000,128]{2,1,0:T(8,128)(2,1)}, u32[]{:S(2)}, u32[]{:S(2)}) async-start(bf16[8,1000,128]{2,1,0:T(8,128)(2,1)} %reshape_reshape.6), calls=%async_computation | async-start | bytes 4096000 | tf_op jit(solution)/shard_map/all_to_all | solution.py:118
  66.0 657.8 %all-to-all-start.1 = ((bf16[8,1000,128]{2,1,0:T(8,128)(2,1)}), bf16[8,1000,128]{2,1,0:T(8,128)(2,1)}, u32[]{:S(2)}, u32[]{:S(2)}) async-start(bf16[8,1000,128]{2,1,0:T(8,128)(2,1)} %reshape_reshape.7), calls=%async_computation.1 | async-start | bytes 4096000 | tf_op jit(solution)/shard_map/all_to_all | solution.py:129
  76.4 1.5 copy-start.3
  652.7 70.2 %copy-start.1 = (bf16[128,1024]{1,0:T(8,128)(2,1)}, bf16[128,1024]{1,0:T(8,128)(2,1)S(1)}, u32[]{:S(2)}) copy-start(bf16[128,1024]{1,0:T(8,128)(2,1)S(1)} %all_gather.6) | copy-start | bytes 786436
  758.4 58.7 %all-to-all-start.3 = ((f32[2,640,100]{2,0,1:T(2,128)}), f32[2,640,100]{2,0,1:T(2,128)S(1)}, u32[]{:S(2)}, u32[]{:S(2)}) async-start(f32[2,640,100]{2,0,1:T(2,128)} %pad_maximum_fusion.1), calls=%async_computation.3 | async-start | bytes 1310720 | tf_op jit(solution)/shard_map/all_to_all | solution.py:44
  838.5 17.6 %copy-start.2 = (bf16[128,1024]{1,0:T(8,128)(2,1)S(1)}, bf16[128,1024]{1,0:T(8,128)(2,1)}, u32[]{:S(2)}) copy-start(bf16[128,1024]{1,0:T(8,128)(2,1)} %copy-done.1) | copy-start | bytes 786436
  848.7 37.4 %all-to-all-start.4 = ((f32[64,1,2000]{2,1,0:T(1,128)}), f32[64,1,2000]{2,1,0:T(1,128)S(1)}, u32[]{:S(2)}, u32[]{:S(2)}) async-start(f32[64,1,2000]{2,1,0:T(1,128)} %reshape.278), calls=%async_computation.4 | async-start | bytes 1048576 | tf_op jit(solution)/shard_map/all_to_all | solution.py:77
  908.2 18.3 %all-to-all-start.5 = ((f32[8,8,1000]{2,0,1:T(8,128)}), f32[8,8,1000]{2,0,1:T(8,128)S(1)}, u32[]{:S(2)}, u32[]{:S(2)}) async-start(f32[8,8,1000]{2,0,1:T(8,128)} %copy.92), calls=%async_computation.5 | async-start | bytes 524288 | tf_op jit(solution)/shard_map/all_to_all | solution.py:152
where the time goes:
time: 1220 us; the launch traced here: 1210 us
  blocking collectives  933 us (76%)
  waiting for transfers between devices  102 us (8%)
  local copies, waits for them, and re-layouts  67.1 us (5%)
  starting transfers between devices  58.5 us (5%)
  other arithmetic  27.9 us (2%)
  matrix products  21 us (2%)
    psum x1, blocking collectives, shards(): occ_sum, vir_sum = lax.psum((occ_here, vir_here), 'grid')  508 us
    psum x1, blocking collectives, shards(): summed = lax.psum(partial_value, 'grid')  218 us
    unnamed x1, blocking collectives  65.1 us
    all_gather x1, blocking collectives, shards(): lax.all_gather(occ_sum.astype(jnp.bfloat16), 'orb', axis=1, tiled=True)  60.8 us
    all_gather x1, blocking collectives, shards(): lax.all_gather(vir_sum.astype(jnp.bfloat16), 'orb', axis=1, tiled=True)  54.7 us
    all_to_all x1, waiting for transfers between devices, shards(): lax.all_to_all(flat_occ.reshape(orb_count, part_rows, occ_local), 'orb',...  37 us
    all_to_all x1, waiting for transfers between devices, plane_spectra(): lax.all_to_all(stacked, 'grid', split_axis=1, concat_axis=2, tiled=True)  35.4 us
    unnamed x14, local copies, waits for them, and re-layouts  27.6 us
  transfers between devices with their start and end apart: 5, of which 4 were waited for; matrix products, arithmetic and copies ran while one was open for 4% of the time, Pallas kernels for 0%

commit v1 on v0

v1 whole, which is shorter than its diff:
```python
import math

import jax
import jax.numpy as jnp
import numpy as np
from jax import lax
from jax.sharding import Mesh, PartitionSpec as P

N = 80
PANEL = 64
GRID = ("zl", "yh", "yl", "c")
ORB = ("zh", "x")
PLANE = ("yl", "c", "x")
RING = ("yh", "zl", "zh")
BF16 = jnp.bfloat16
F32 = jnp.float32
FOUR_PI = 4.0 * math.pi
TWO_PI = 2.0 * math.pi


def real_basis():
    steps = np.arange(N)
    freqs = np.concatenate([np.arange(N // 2 + 1), np.arange(1, N // 2)])
    angle = TWO_PI / N * (freqs[:, None] * steps[None, :] % N)
    table = np.where(np.arange(N)[:, None] <= N // 2, np.cos(angle), np.sin(angle)) * math.sqrt(2.0 / N)
    table[0] /= math.sqrt(2.0)
    table[N // 2] /= math.sqrt(2.0)
    return table.astype(np.float32)


def freq_square(index):
    freq = jnp.where(index > N // 2, index - N // 2, index).astype(F32)
    wave = TWO_PI / N * freq
    return wave * wave


def mix(form, left, right):
    return jnp.einsum(form, left, right, precision=lax.Precision.HIGHEST, preferred_element_type=F32)


def swap(values, axes):
    return lax.all_to_all(values, axes, 0, 0, tiled=True)


def shards(occupied, virtual, points, panels):
    x_rank = lax.axis_index("x")
    zh_rank = lax.axis_index("zh")
    grid_rank = lax.axis_index(GRID)
    columns = occupied.shape[1]
    width = occupied.shape[2]
    per_x = columns // 4

    chosen = points[panels.reshape(-1)]
    plane_of = chosen // (N * N)
    within = chosen % (N * N) - grid_rank * columns
    inside = (within >= 0) & (within < columns)
    column_of = jnp.where(inside, within, 0)
    here = jnp.concatenate([occupied[plane_of, column_of], virtual[plane_of, column_of]], axis=1)
    here = jnp.where(inside[:, None], here, jnp.zeros((), BF16))
    two_rows = jnp.sum(swap(here.reshape(64, 2, 2 * width), GRID).astype(F32), axis=0).astype(BF16)
    gathered = swap(jnp.broadcast_to(two_rows[None], (256, 2, 2 * width)), GRID + ("x",))
    pts = gathered.reshape(64, 4, 2, 2 * width).transpose(1, 0, 2, 3).reshape(4, 2 * PANEL, 2 * width)

    def spread(array):
        parts = array.reshape(N, 4, per_x, width).transpose(1, 2, 0, 3).reshape(4, per_x * N, width)
        blocks = [lax.dynamic_index_in_dim(parts, x_rank, 0, keepdims=False)]
        for shift in (1, 3, 2):
            out = lax.dynamic_index_in_dim(parts, (x_rank + shift) % 4, 0, keepdims=False)
            blocks.append(lax.ppermute(out, "x", [(i, (i + shift) % 4) for i in range(4)]))
        return blocks

    occ_blocks = spread(occupied)
    vir_blocks = spread(virtual)
    pts_blocks = [lax.dynamic_index_in_dim(pts, (x_rank - shift) % 4, 0, keepdims=False) for shift in (0, 1, 3, 2)]

    def side_sums(start):
        rows = [lax.dynamic_slice_in_dim(block, start, PANEL, 0) for block in pts_blocks]

        def total(blocks, low):
            cells = jnp.concatenate(
                [jnp.concatenate([b, r[:, low : low + width]], axis=0) for b, r in zip(blocks, rows)], axis=1
            )
            weights = jnp.concatenate([r[:, low : low + width] for r in rows], axis=1)
            return jnp.dot(cells, weights.T, preferred_element_type=F32)

        return jnp.concatenate([total(occ_blocks, 0), total(vir_blocks, width)], axis=1)

    theirs = side_sums((1 - zh_rank) * PANEL)
    other = lax.ppermute(theirs, "zh", [(0, 1), (1, 0)])
    mine = side_sums(zh_rank * PANEL) + other
    pairs = mine[:, :PANEL] * mine[:, PANEL:]
    cell_count = per_x * N
    gram = pairs[cell_count:]
    factor = jnp.linalg.cholesky(gram)
    lowered = lax.linalg.triangular_solve(factor, jnp.eye(PANEL, dtype=F32), left_side=True, lower=True)
    inverse = mix("km,kn->mn", lowered, lowered)

    basis = real_basis()
    fields = pairs[:cell_count].reshape(per_x, N, PANEL)
    fields = mix("ka,caf->kcf", basis, fields).reshape(16, 5, per_x, PANEL)
    fields = swap(fields, PLANE)
    fields = fields.transpose(1, 0, 2, 3).reshape(5, 5, N, PANEL)
    fields = mix("qc,kbcf->kqbf", basis, fields)
    fields = mix("kqbf,fg->kqbg", fields, inverse).reshape(5 * N, 5, PANEL)
    fields = jnp.pad(fields, ((0, 16), (0, 0), (0, 0))).reshape(32, 13, 5, PANEL)
    fields = swap(fields, RING).reshape(2, 8, 2, 13, 5, PANEL)
    basis_b = basis.reshape(N, 8, 2, 5).transpose(0, 2, 1, 3)
    fields = mix("kyzb,yzhqbf->hqkf", basis_b, fields)

    slot = lax.axis_index(RING) * 13 + jnp.arange(13, dtype=jnp.int32)
    ka = lax.axis_index(PLANE) * 5 + slot // N
    squared = (freq_square(ka) + freq_square(slot % N))[:, None] + freq_square(jnp.arange(N, dtype=jnp.int32))[None, :]
    live = (squared > 0) & (slot < 5 * N)[:, None]
    kernel = jnp.where(live, 32.0 * FOUR_PI / jnp.where(squared > 0, squared, 1.0), 0.0)
    part = mix("qkm,qkn->mn", fields[1], fields[0] * kernel[:, :, None])
    part = jnp.sum(swap(part.reshape(8, 8, PANEL), ORB), axis=0)
    part = swap(jnp.broadcast_to(part[None], (64, 8, PANEL)), GRID)
    return jnp.sum(part, axis=0)


def solution(mesh):
    devices = mesh.devices.reshape(8, 2, 2, 2, 2, 4)
    inner = Mesh(devices, ("zl", "yh", "yl", "c", "zh", "x"))
    in_specs = (P(None, GRID, ORB), P(None, GRID, ORB), P(), P())
    return jax.shard_map(shards, mesh=inner, in_specs=in_specs, out_specs=P(ORB, None), check_vma=False)
```

time: 1220 us -> 340 us (0.28)
  blocking collectives: 933 us -> 77.2 us
  starting transfers between devices: 58.5 us -> 121 us
  local copies, waits for them, and re-layouts: 67.1 us -> 19.3 us
  waiting for transfers between devices: 102 us -> 83.7 us
    psum x2 -> x0, blocking collectives: 726 us -> none  [the longest x1 508 us: shards(): occ_sum, vir_sum = lax.psum((occ_here, vir_here), 'grid')]
    all_gather x2 -> x0, blocking collectives: 116 us -> none  [the longest x1 60.8 us: shards(): lax.all_gather(occ_sum.astype(jnp.bfloat16), 'orb', axis=1, tiled=True)]
    all_to_all x5 -> x3, waiting for transfers between devices: 102 us -> 36.4 us  [swap(): return lax.all_to_all(values, axes, 0, 0, tiled=True)]
    unnamed x1 -> x0, blocking collectives: 65.1 us -> none
    all_to_all x1 -> x3, blocking collectives: 26.5 us -> 77.2 us  [swap(): return lax.all_to_all(values, axes, 0, 0, tiled=True)]
    ppermute x0 -> x7, waiting for transfers between devices: none -> 47.3 us  [the longest x6 25.8 us: spread(): lax.ppermute(out, 'x', [(i, (i + shift) % 4) for i in range(4)])]
    all_to_all x5 -> x3, starting transfers between devices: 58.5 us -> 94.1 us  [swap(): return lax.all_to_all(values, axes, 0, 0, tiled=True)]
    ppermute x0 -> x7, starting transfers between devices: none -> 27 us  [the longest x6 18.8 us: spread(): lax.ppermute(out, 'x', [(i, (i + shift) % 4) for i in range(4)])]
  transfers between devices with their start and end apart: 5 -> 10, of which waited for: 4 -> 9; matrix products, arithmetic and copies ran while one was open for 4% -> 5% of each run, Pallas kernels for 0% -> 0%
where the time goes in v1:
time: 340 us; the launch traced here: 339 us
  starting transfers between devices  121 us (36%)
  waiting for transfers between devices  83.7 us (25%)
  blocking collectives  77.2 us (23%)
  other arithmetic  20 us (6%)
  local copies, waits for them, and re-layouts  19.3 us (6%)
  matrix products  17 us (5%)
    all_to_all x3, starting transfers between devices, swap(): return lax.all_to_all(values, axes, 0, 0, tiled=True)  94.1 us
    all_to_all x3, blocking collectives, swap(): return lax.all_to_all(values, axes, 0, 0, tiled=True)  77.2 us
    all_to_all x3, waiting for transfers between devices, swap(): return lax.all_to_all(values, axes, 0, 0, tiled=True)  36.4 us
    ppermute x6, waiting for transfers between devices, spread(): lax.ppermute(out, 'x', [(i, (i + shift) % 4) for i in range(4)])  25.8 us
    ppermute x1, waiting for transfers between devices, shards(): other = lax.ppermute(theirs, 'zh', [(0, 1), (1, 0)])  21.5 us
    ppermute x6, starting transfers between devices, spread(): lax.ppermute(out, 'x', [(i, (i + shift) % 4) for i in range(4)])  18.8 us
    dot_general x4, matrix products, total(): return jnp.dot(cells, weights.T, preferred_element_type=F32)  10.2 us
    ppermute x1, starting transfers between devices, shards(): other = lax.ppermute(theirs, 'zh', [(0, 1), (1, 0)])  8.12 us
  transfers between devices with their start and end apart: 10, of which 9 were waited for; matrix products, arithmetic and copies ran while one was open for 5% of the time, Pallas kernels for 0%

profile of v1, /device:TPU:1, one launch (start us, length us, event | category | flops | bytes accessed | tf_op | source)
XLA Modules:
  0.0 339.0 jit_solution(17059924420963753273)
XLA Ops:
  2.4 2.0 gather_fusion.2
  4.4 2.0 gather_fusion.1
  6.5 29.9 %all_to_all.30 = bf16[64,2,256]{2,1,0:T(2,128)(2,1)S(1)} all-to-all(bf16[64,2,256]{2,1,0:T(2,128)(2,1)S(1)} %broadcast_select_fusion), channel_id=1, replica_groups=mesh['zl'=8,'yh'=2,'yl'=2,'c'=2,'zh'=2,'x'=4] {'zl','yh','yl','c'}, dimensions={0} | all-to-all | bytes 131072 | tf_op jit(solution)/shard_map/all_to_all | solution.py:42
  37.3 9.6 %all-to-all-start.1 = ((bf16[256,2,256]{2,1,0:T(2,128)(2,1)}), bf16[256,2,256]{2,1,0:T(2,128)(2,1)S(1)}, u32[]{:S(2)}, u32[]{:S(2)}) async-start(bf16[256,2,256]{2,1,0:T(2,128)(2,1)} %broadcast_in_dim.27), calls=%async_computation.1 | async-start | bytes 524288 | tf_op jit(solution)/shard_map/all_to_all | solution.py:42
  48.0 4.8 %collective-permute-start.5 = (bf16[2000,128]{1,0:T(8,128)(2,1)}, bf16[2000,128]{1,0:T(8,128)(2,1)}, u32[]{:S(2)}, u32[]{:S(2)}) collective-permute-start(bf16[2000,128]{1,0:T(8,128)(2,1)} %get-tuple-element.9), channel_id=1, source_target_pairs={{0,2},{1,3},{2,0},{3,1},{4,6},{5,7},{6,4},{7,5},{8,10},{9,11},{10,... | collective-permute-start | bytes 1536008 | tf_op jit(solution)/shard_map/ppermute | solution.py:69
  52.8 2.8 collective-permute-start.4
  55.6 2.5 collective-permute-start.3
  58.3 2.5 collective-permute-start.2
  60.8 4.0 %collective-permute-start.1 = (bf16[2000,128]{1,0:T(8,128)(2,1)S(1)}, bf16[2000,128]{1,0:T(8,128)(2,1)}, u32[]{:S(2)}, u32[]{:S(2)}) collective-permute-start(bf16[2000,128]{1,0:T(8,128)(2,1)S(1)} %get-tuple-element.6), channel_id=1, source_target_pairs={{0,3},{1,0},{2,1},{3,2},{4,7},{5,4},{6,5},{7,6},{8,11},{9,8},{10,9... | collective-permute-start | bytes 1536008 | tf_op jit(solution)/shard_map/ppermute | solution.py:69
  64.9 3.7 %all-to-all-done.1 = bf16[256,2,256]{2,1,0:T(2,128)(2,1)S(1)} async-done(((bf16[256,2,256]{2,1,0:T(2,128)(2,1)}), bf16[256,2,256]{2,1,0:T(2,128)(2,1)S(1)}, u32[]{:S(2)}, u32[]{:S(2)}) %all-to-all-start.1) | async-done | bytes 262176 | tf_op jit(solution)/shard_map/all_to_all | solution.py:42
  69.4 2.3 collective-permute-start
  71.7 5.4 %collective-permute-done.4 = bf16[2000,128]{1,0:T(8,128)(2,1)} collective-permute-done((bf16[2000,128]{1,0:T(8,128)(2,1)}, bf16[2000,128]{1,0:T(8,128)(2,1)}, u32[]{:S(2)}, u32[]{:S(2)}) %collective-permute-start.4) | collective-permute-done | bytes 512032 | tf_op jit(solution)/shard_map/ppermute | solution.py:69
  77.1 2.6 collective-permute-done.3
  79.8 2.1 fusion.16
  81.9 5.0 %collective-permute-done.2 = bf16[2000,128]{1,0:T(8,128)(2,1)} collective-permute-done((bf16[2000,128]{1,0:T(8,128)(2,1)S(1)}, bf16[2000,128]{1,0:T(8,128)(2,1)}, u32[]{:S(2)}, u32[]{:S(2)}) %collective-permute-start.2) | collective-permute-done | bytes 512032 | tf_op jit(solution)/shard_map/ppermute | solution.py:69
  86.9 12.2 %collective-permute-done.1 = bf16[2000,128]{1,0:T(8,128)(2,1)} collective-permute-done((bf16[2000,128]{1,0:T(8,128)(2,1)S(1)}, bf16[2000,128]{1,0:T(8,128)(2,1)}, u32[]{:S(2)}, u32[]{:S(2)}) %collective-permute-start.1) | collective-permute-done | bytes 512032 | tf_op jit(solution)/shard_map/ppermute | solution.py:69
  99.7 2.1 fusion.12
  102.3 8.1 %collective-permute-start.6 = (f32[2064,128]{1,0:T(8,128)S(1)}, f32[2064,128]{1,0:T(8,128)S(1)}, u32[]{:S(2)}, u32[]{:S(2)}) collective-permute-start(f32[2064,128]{1,0:T(8,128)S(1)} %copy.56), channel_id=1, source_target_pairs={{0,4},{4,0},{1,5},{5,1},{2,6},{6,2},{3,7},{7,3},{8,12},{12,8},{9,1... | collective-permute-start | bytes 3170312 | tf_op jit(solution)/shard_map/ppermute | solution.py:89
  110.5 3.2 fusion.18
  113.6 2.8 fusion.14
  116.4 21.5 %collective-permute-done.6 = f32[2064,128]{1,0:T(8,128)S(1)} collective-permute-done((f32[2064,128]{1,0:T(8,128)S(1)}, f32[2064,128]{1,0:T(8,128)S(1)}, u32[]{:S(2)}, u32[]{:S(2)}) %collective-permute-start.6) | collective-permute-done | bytes 1056800 | tf_op jit(solution)/shard_map/ppermute | solution.py:89
  140.5 5.9 %cholesky.17 = f32[64,64]{1,0:T(8,128)S(1)} custom-call(f32[64,64]{1,0:T(8,128)S(1)} %fusion.57), custom_call_target="Cholesky" | custom-call | tf_op jit(solution)/shard_map/jit(cholesky)/cholesky | solution.py:94
  151.7 6.5 %all-to-all-start.2 = ((f32[16,1,8000]{2,1,0:T(1,128)}), f32[16,1,8000]{2,1,0:T(1,128)S(1)}, u32[]{:S(2)}, u32[]{:S(2)}) async-start(f32[16,1,8000]{2,1,0:T(1,128)} %reshape.316), calls=%async_computation.2 | async-start | bytes 1032192 | tf_op jit(solution)/shard_map/all_to_all | solution.py:42
  158.8 4.9 %custom-call.6 = f32[1,64,64]{1,2,0:T(8,128)S(1)} custom-call(f32[1,64,64]{2,1,0:T(8,128)S(1)} %fusion.53), custom_call_target="InvertDiagBlocksLowerTriangular" | custom-call | tf_op jit(solution)/shard_map/triangular_solve | solution.py:95
  164.2 3.9 %all-to-all-done.2 = f32[16,1,8000]{2,1,0:T(1,128)S(1)} async-done(((f32[16,1,8000]{2,1,0:T(1,128)}), f32[16,1,8000]{2,1,0:T(1,128)S(1)}, u32[]{:S(2)}, u32[]{:S(2)}) %all-to-all-start.2) | async-done | bytes 512032 | tf_op jit(solution)/shard_map/all_to_all | solution.py:42
  168.6 1.9 reduce.7
  176.6 78.0 %all-to-all-start.3 = ((f32[32,1,4160]{2,1,0:T(1,128)}), f32[32,1,4160]{2,1,0:T(1,128)S(1)}, u32[]{:S(2)}, u32[]{:S(2)}) async-start(f32[32,1,4160]{2,1,0:T(1,128)} %reshape.318), calls=%async_computation.3 | async-start | bytes 1081344 | tf_op jit(solution)/shard_map/all_to_all | solution.py:42
  254.8 28.8 %all-to-all-done.3 = f32[32,1,4160]{2,1,0:T(1,128)S(1)} async-done(((f32[32,1,4160]{2,1,0:T(1,128)}), f32[32,1,4160]{2,1,0:T(1,128)S(1)}, u32[]{:S(2)}, u32[]{:S(2)}) %all-to-all-start.3) | async-done | bytes 532512 | tf_op jit(solution)/shard_map/all_to_all | solution.py:42
  283.7 1.9 reduce.8
  286.0 2.2 convolution_bitcast_fusion
  288.9 22.1 %all_to_all.31 = f32[8,1,512]{2,1,0:T(1,128)S(1)} all-to-all(f32[8,1,512]{2,1,0:T(1,128)S(1)} %reshape.320), channel_id=1, replica_groups=mesh['zl'=8,'yh'=2,'yl'=2,'c'=2,'zh'=2,'x'=4] {'zh','x'}, dimensions={0} | all-to-all | bytes 32768 | tf_op jit(solution)/shard_map/all_to_all | solution.py:42
  312.0 25.2 %all_to_all.32 = f32[64,1,512]{2,1,0:T(1,128)S(1)} all-to-all(f32[64,1,512]{2,1,0:T(1,128)S(1)} %reshape.322), channel_id=1, replica_groups=mesh['zl'=8,'yh'=2,'yl'=2,'c'=2,'zh'=2,'x'=4] {'zl','yh','yl','c'}, dimensions={0} | all-to-all | bytes 262144 | tf_op jit(solution)/shard_map/all_to_all | solution.py:42
  (98 shorter events, 25.8 us)
Async XLA Ops:
  0.0 0.9 copy-start
  0.0 46.9 %copy-start.1 = (bf16[80,100,128]{2,0,1:T(8,128)(2,1)S(1)}, bf16[80,100,128]{2,0,1:T(8,128)(2,1)}, u32[]{:S(2)}) copy-start(bf16[80,100,128]{2,0,1:T(8,128)(2,1)} %param.8) | copy-start | bytes 6144004
  37.3 31.4 %all-to-all-start.1 = ((bf16[256,2,256]{2,1,0:T(2,128)(2,1)}), bf16[256,2,256]{2,1,0:T(2,128)(2,1)S(1)}, u32[]{:S(2)}, u32[]{:S(2)}) async-start(bf16[256,2,256]{2,1,0:T(2,128)(2,1)} %broadcast_in_dim.27), calls=%async_computation.1 | async-start | bytes 524288 | tf_op jit(solution)/shard_map/all_to_all | solution.py:42
  46.9 11.2 %copy-start.2 = (bf16[80,100,128]{2,0,1:T(8,128)(2,1)S(1)}, bf16[80,100,128]{2,0,1:T(8,128)(2,1)}, u32[]{:S(2)}) copy-start(bf16[80,100,128]{2,0,1:T(8,128)(2,1)} %param.7) | copy-start | bytes 6144004
  48.0 33.9 %copy-start.4 = (bf16[2000,128]{1,0:T(8,128)(2,1)}, bf16[2000,128]{1,0:T(8,128)(2,1)S(1)}, u32[]{:S(2)}) copy-start(bf16[2000,128]{1,0:T(8,128)(2,1)S(1)} %get-tuple-element.12) | copy-start | bytes 1536004
  48.0 21.4 %collective-permute-start.5 = (bf16[2000,128]{1,0:T(8,128)(2,1)}, bf16[2000,128]{1,0:T(8,128)(2,1)}, u32[]{:S(2)}, u32[]{:S(2)}) collective-permute-start(bf16[2000,128]{1,0:T(8,128)(2,1)} %get-tuple-element.9), channel_id=1, source_target_pairs={{0,2},{1,3},{2,0},{3,1},{4,6},{5,7},{6,4},{7,5},{8,10},{9,11},{10,... | collective-permute-start | bytes 1536008 | tf_op jit(solution)/shard_map/ppermute | solution.py:69
  52.8 24.3 %collective-permute-start.4 = (bf16[2000,128]{1,0:T(8,128)(2,1)}, bf16[2000,128]{1,0:T(8,128)(2,1)}, u32[]{:S(2)}, u32[]{:S(2)}) collective-permute-start(bf16[2000,128]{1,0:T(8,128)(2,1)} %get-tuple-element.10), channel_id=1, source_target_pairs={{0,3},{1,0},{2,1},{3,2},{4,7},{5,4},{6,5},{7,6},{8,11},{9,8},{10,9... | collective-permute-start | bytes 1536008 | tf_op jit(solution)/shard_map/ppermute | solution.py:69
  55.6 24.2 %collective-permute-start.3 = (bf16[2000,128]{1,0:T(8,128)(2,1)S(1)}, bf16[2000,128]{1,0:T(8,128)(2,1)}, u32[]{:S(2)}, u32[]{:S(2)}) collective-permute-start(bf16[2000,128]{1,0:T(8,128)(2,1)S(1)} %get-tuple-element.11), channel_id=1, source_target_pairs={{0,1},{1,2},{2,3},{3,0},{4,5},{5,6},{6,7},{7,4},{8,9},{9,10},{10,1... | collective-permute-start | bytes 1536008 | tf_op jit(solution)/shard_map/ppermute | solution.py:69
  58.3 41.4 %copy-start.5 = (bf16[2000,128]{1,0:T(8,128)(2,1)}, bf16[2000,128]{1,0:T(8,128)(2,1)S(1)}, u32[]{:S(2)}) copy-start(bf16[2000,128]{1,0:T(8,128)(2,1)S(1)} %get-tuple-element.8) | copy-start | bytes 1536004
  58.3 28.6 %collective-permute-start.2 = (bf16[2000,128]{1,0:T(8,128)(2,1)S(1)}, bf16[2000,128]{1,0:T(8,128)(2,1)}, u32[]{:S(2)}, u32[]{:S(2)}) collective-permute-start(bf16[2000,128]{1,0:T(8,128)(2,1)S(1)} %get-tuple-element.5), channel_id=1, source_target_pairs={{0,2},{1,3},{2,0},{3,1},{4,6},{5,7},{6,4},{7,5},{8,10},{9,11},{10,... | collective-permute-start | bytes 1536008 | tf_op jit(solution)/shard_map/ppermute | solution.py:69
  60.8 38.3 %collective-permute-start.1 = (bf16[2000,128]{1,0:T(8,128)(2,1)S(1)}, bf16[2000,128]{1,0:T(8,128)(2,1)}, u32[]{:S(2)}, u32[]{:S(2)}) collective-permute-start(bf16[2000,128]{1,0:T(8,128)(2,1)S(1)} %get-tuple-element.6), channel_id=1, source_target_pairs={{0,3},{1,0},{2,1},{3,2},{4,7},{5,4},{6,5},{7,6},{8,11},{9,8},{10,9... | collective-permute-start | bytes 1536008 | tf_op jit(solution)/shard_map/ppermute | solution.py:69
  69.4 30.2 %collective-permute-start = (bf16[2000,128]{1,0:T(8,128)(2,1)S(1)}, bf16[2000,128]{1,0:T(8,128)(2,1)S(1)}, u32[]{:S(2)}, u32[]{:S(2)}) collective-permute-start(bf16[2000,128]{1,0:T(8,128)(2,1)S(1)} %get-tuple-element.7), channel_id=1, source_target_pairs={{0,1},{1,2},{2,3},{3,0},{4,5},{5,6},{6,7},{7,4},{8,9},{9,10},{10,1... | collective-permute-start | bytes 1536008 | tf_op jit(solution)/shard_map/ppermute | solution.py:69
  99.7 2.2 copy-start.9
  102.3 35.6 %collective-permute-start.6 = (f32[2064,128]{1,0:T(8,128)S(1)}, f32[2064,128]{1,0:T(8,128)S(1)}, u32[]{:S(2)}, u32[]{:S(2)}) collective-permute-start(f32[2064,128]{1,0:T(8,128)S(1)} %copy.56), channel_id=1, source_target_pairs={{0,4},{4,0},{1,5},{5,1},{2,6},{6,2},{3,7},{7,3},{8,12},{12,8},{9,1... | collective-permute-start | bytes 3170312 | tf_op jit(solution)/shard_map/ppermute | solution.py:89
  110.4 3.2 copy-start.6
  110.5 3.2 copy-start.10
  137.9 1.1 copy-start.3
  140.3 7.9 %copy-start.7 = (f32[80,80]{1,0:T(8,128)S(1)}, f32[80,80]{1,0:T(8,128)}, u32[]{:S(2)}) copy-start(f32[80,80]{1,0:T(8,128)} %constant.355.clone) | copy-start | bytes 76804
  151.7 16.4 %all-to-all-start.2 = ((f32[16,1,8000]{2,1,0:T(1,128)}), f32[16,1,8000]{2,1,0:T(1,128)S(1)}, u32[]{:S(2)}, u32[]{:S(2)}) async-start(f32[16,1,8000]{2,1,0:T(1,128)} %reshape.316), calls=%async_computation.2 | async-start | bytes 1032192 | tf_op jit(solution)/shard_map/all_to_all | solution.py:42
  171.0 0.8 copy-start.8
  176.6 109.4 %copy-start.11 = (f32[80,2,8,5,1,1]{0,2,1,3,5,4:T(8,128)S(1)}, f32[80,2,8,5,1,1]{0,2,1,3,5,4:T(8,128)}, u32[]{:S(2)}) copy-start(f32[80,2,8,5,1,1]{0,2,1,3,5,4:T(8,128)} %constant.388) | copy-start | bytes 76804
  176.6 107.0 %all-to-all-start.3 = ((f32[32,1,4160]{2,1,0:T(1,128)}), f32[32,1,4160]{2,1,0:T(1,128)S(1)}, u32[]{:S(2)}, u32[]{:S(2)}) async-start(f32[32,1,4160]{2,1,0:T(1,128)} %reshape.318), calls=%async_computation.3 | async-start | bytes 1081344 | tf_op jit(solution)/shard_map/all_to_all | solution.py:42

commit v2 on v1

v2 whole, which is shorter than its diff:
```python
import math

import jax
import jax.numpy as jnp
import numpy as np
from jax import lax
from jax.sharding import Mesh, PartitionSpec as P

N = 80
PANEL = 64
GRID = ("zl", "yh", "yl", "c")
ORB = ("zh", "x")
ROWS = ("yh", "yl", "c")
PLANE = ("yl", "c", "x")
RING = ("yh", "zl", "zh")
BF16 = jnp.bfloat16
F32 = jnp.float32
F16 = jnp.float16
SPAN = 5.21
FOUR_PI = 4.0 * math.pi
TWO_PI = 2.0 * math.pi


def real_basis():
    steps = np.arange(N)
    freqs = np.concatenate([np.arange(N // 2 + 1), np.arange(1, N // 2)])
    angle = TWO_PI / N * (freqs[:, None] * steps[None, :] % N)
    table = np.where(np.arange(N)[:, None] <= N // 2, np.cos(angle), np.sin(angle)) * math.sqrt(2.0 / N)
    table[0] /= math.sqrt(2.0)
    table[N // 2] /= math.sqrt(2.0)
    return table.astype(np.float32)


def freq_square(index):
    freq = jnp.where(index > N // 2, index - N // 2, index).astype(F32)
    wave = TWO_PI / N * freq
    return wave * wave


def mix(form, left, right):
    return jnp.einsum(form, left, right, precision=lax.Precision.HIGHEST, preferred_element_type=F32)


def swap(values, axes):
    return lax.all_to_all(values, axes, 0, 0, tiled=True)


def encode(values):
    square = jnp.mean(values * values, axis=0, keepdims=True)
    power = jnp.ceil(0.5 * jnp.log2(jnp.maximum(square, 1e-37))) - 1.0
    size = jnp.abs(values) * jnp.exp2(-power)
    level = jnp.log(size + jnp.sqrt(size * size + 1.0)) * (29.98 / SPAN)
    whole = jnp.floor(level)
    code = jnp.exp2(whole - 14.0) * (1.0 + (level - whole))
    return jnp.where(values < 0, -code, code).astype(F16), power.astype(F16)


def decode(code, power):
    code = code.astype(F32)
    size = jnp.abs(code)
    whole = jnp.floor(jnp.log2(size) + 2e-4)
    level = whole + (size * jnp.exp2(-whole) - 1.0) + 14.0
    spread = jnp.exp(level * (SPAN / 29.98))
    value = 0.5 * (spread - 1.0 / spread) * jnp.exp2(power.astype(F32))
    return jnp.where(code < 0, -value, value)


def shards(occupied, virtual, points, panels):
    x_rank = lax.axis_index("x")
    zh_rank = lax.axis_index("zh")
    grid_rank = lax.axis_index(GRID)
    columns = occupied.shape[1]
    width = occupied.shape[2]
    per_x = columns // 4

    chosen = points[panels.reshape(-1)]
    plane_of = chosen // (N * N)
    within = chosen % (N * N) - grid_rank * columns
    inside = (within >= 0) & (within < columns)
    column_of = jnp.where(inside, within, 0)
    here = jnp.concatenate([occupied[plane_of, column_of], virtual[plane_of, column_of]], axis=1)
    here = jnp.where(inside[:, None], here, jnp.zeros((), BF16))

    parts = jnp.concatenate([occupied, virtual], axis=2).reshape(N, 4, per_x, 2 * width)
    parts = parts.transpose(1, 2, 0, 3).reshape(4, per_x * N, 2 * width)

    def take(shift):
        return lax.dynamic_index_in_dim(parts, (x_rank + shift) % 4, 0, keepdims=False)

    def spread(block, shift):
        return lax.ppermute(block, "x", [(i, (i + shift) % 4) for i in range(4)])

    far = take(2)
    half = far.shape[0] // 2
    blocks = {0: take(0), 1: spread(take(1), 1), 3: spread(take(3), 3)}
    far_low = spread(far[:half], 2)

    def add(values):
        return jnp.sum(values.astype(F32), axis=0).astype(BF16)

    rows = add(swap(here.reshape(8, 16, 2 * width), ROWS))
    rows = add(swap(jnp.broadcast_to(rows[None], (8, 16, 2 * width)), "zl"))
    rows, blocks[1], blocks[3], far_low = lax.optimization_barrier((rows, blocks[1], blocks[3], far_low))
    blocks[2] = jnp.concatenate([far_low, spread(far[half:], 2)], axis=0)
    gathered = swap(jnp.broadcast_to(rows[None], (32, 16, 2 * width)), ROWS + ("x",))
    pts = gathered.reshape(8, 4, 16, 2 * width).transpose(1, 0, 2, 3).reshape(4, 2 * PANEL, 2 * width)
    shifts = (0, 1, 3, 2)
    pts_blocks = [lax.dynamic_index_in_dim(pts, (x_rank - shift) % 4, 0, keepdims=False) for shift in shifts]

    def side_weights(start):
        heads, tables = [], []
        gap = jnp.zeros((PANEL, width), BF16)
        for block in pts_blocks:
            head = lax.dynamic_slice_in_dim(block, start, PANEL, 0)
            upper = jnp.concatenate([head[:, :width], gap], axis=1)
            lower = jnp.concatenate([gap, head[:, width:]], axis=1)
            heads.append(head)
            tables.append(jnp.concatenate([upper, lower], axis=0))
        return heads, tables

    def side_sums(cells, tables):
        return sum(jnp.dot(c, t.T, preferred_element_type=F32) for c, t in zip(cells, tables))

    def cross(values):
        return lax.ppermute(values, "zh", [(0, 1), (1, 0)])

    their_heads, their_tables = side_weights((1 - zh_rank) * PANEL)
    my_heads, my_tables = side_weights(zh_rank * PANEL)
    cells = [blocks[shift] for shift in shifts]
    gram = side_sums(my_heads, my_tables) + cross(side_sums(their_heads, their_tables))
    factor = jnp.linalg.cholesky(gram[:, :PANEL] * gram[:, PANEL:])
    lowered = lax.linalg.triangular_solve(factor, jnp.eye(PANEL, dtype=F32), left_side=True, lower=True)
    inverse = mix("km,kn->mn", lowered, lowered)

    cell_count = per_x * N
    code, power = encode(side_sums(cells, their_tables))
    sent = jnp.concatenate([code, jnp.broadcast_to(power, (16, 2 * PANEL))], axis=0)
    got = cross(sent)
    mine = side_sums(cells, my_tables)
    got, inverse, mine = lax.optimization_barrier((got, inverse, mine))
    mine = mine + decode(got[:cell_count], got[cell_count : cell_count + 1])
    pairs = mine[:, :PANEL] * mine[:, PANEL:]

    basis = real_basis()
    fields = pairs.reshape(per_x, N, PANEL)
    fields = mix("ka,caf->kcf", basis, fields).reshape(16, 5, per_x, PANEL)
    fields = swap(fields, PLANE)
    fields = fields.transpose(1, 0, 2, 3).reshape(5, 5, N, PANEL)
    fields = mix("qc,kbcf->kqbf", basis, fields)
    fields = mix("kqbf,fg->kqbg", fields, inverse).reshape(25 * N, PANEL)
    code, power = encode(fields)
    code = jnp.concatenate([code, jnp.ones((80, PANEL), F16)], axis=0).reshape(32, 65, PANEL)
    power = jnp.broadcast_to(power[None], (32, 1, PANEL))
    sent = jnp.concatenate([code[:, :33], jnp.concatenate([code[:, 33:], power], axis=1)], axis=2)
    got = swap(sent, RING)
    power = got[:, 32:, PANEL:]
    fields = jnp.concatenate([decode(got[:, :, :PANEL], power), decode(got[:, :32, PANEL:], power)], axis=1)
    fields = fields.reshape(2, 8, 2, 13, 5, PANEL)
    basis_b = basis.reshape(N, 8, 2, 5).transpose(0, 2, 1, 3)
    fields = mix("kyzb,yzhqbf->hqkf", basis_b, fields)

    slot = lax.axis_index(RING) * 13 + jnp.arange(13, dtype=jnp.int32)
    ka = lax.axis_index(PLANE) * 5 + slot // N
    squared = (freq_square(ka) + freq_square(slot % N))[:, None] + freq_square(jnp.arange(N, dtype=jnp.int32))[None, :]
    live = (squared > 0) & (slot < 5 * N)[:, None]
    kernel = jnp.where(live, 32.0 * FOUR_PI / jnp.where(squared > 0, squared, 1.0), 0.0)
    part = mix("qkm,qkn->mn", fields[1], fields[0] * kernel[:, :, None])
    part = part.reshape(2, 4, 8, PANEL).transpose(1, 0, 2, 3)
    part = jnp.broadcast_to(part[None], (8, 4, 2, 8, PANEL)).reshape(32, 16, PANEL)
    part = jnp.sum(swap(part, ROWS + ("x",)), axis=0)
    part = jnp.broadcast_to(part.reshape(1, 2, 8, PANEL), (8, 2, 8, PANEL)).reshape(16, 8, PANEL)
    return jnp.sum(swap(part, ("zl", "zh")), axis=0)


def solution(mesh):
    devices = mesh.devices.reshape(8, 2, 2, 2, 2, 4)
    inner = Mesh(devices, ("zl", "yh", "yl", "c", "zh", "x"))
    in_specs = (P(None, GRID, ORB), P(None, GRID, ORB), P(), P())
    return jax.shard_map(shards, mesh=inner, in_specs=in_specs, out_specs=P(ORB, None), check_vma=False)
```

time: 340 us -> 262 us (0.77)
  starting transfers between devices: 121 us -> 71.8 us
  waiting for transfers between devices: 83.7 us -> 56 us
  blocking collectives: 77.2 us -> 57 us
  local copies, waits for them, and re-layouts: 19.3 us -> 31.3 us
  other arithmetic: 20 us -> 24.4 us
    all_to_all x3, starting transfers between devices: 94.1 us -> 43.7 us  [swap(): return lax.all_to_all(values, axes, 0, 0, tiled=True)]
    ppermute x7 -> x6, waiting for transfers between devices: 47.3 us -> 18.9 us  [the longest x2 18.9 us: cross(): return lax.ppermute(values, 'zh', [(0, 1), (1, 0)])]
    all_to_all x3 -> x4, blocking collectives: 77.2 us -> 57 us  [swap(): return lax.all_to_all(values, axes, 0, 0, tiled=True)]
    dot_general x4 -> x16, matrix products: 10.2 us -> 12.8 us  [side_sums(): jnp.dot(c, t.T, preferred_element_type=F32)]
    unnamed x37 -> x30, local copies, waits for them, and re-layouts: 6.13 us -> 7.29 us
    ppermute x7 -> x6, starting transfers between devices: 27 us -> 28.1 us  [the longest x2 14.2 us: cross(): return lax.ppermute(values, 'zh', [(0, 1), (1, 0)])]
  transfers between devices with their start and end apart: 10 -> 9, of which waited for: 9 -> 4; matrix products, arithmetic and copies ran while one was open for 5% -> 11% of each run, Pallas kernels for 0% -> 0%
where the time goes in v2:
time: 262 us; the launch traced here: 260 us
  starting transfers between devices  71.8 us (27%)
  blocking collectives  57 us (22%)
  waiting for transfers between devices  56 us (21%)
  local copies, waits for them, and re-layouts  31.3 us (12%)
  other arithmetic  24.4 us (9%)
  matrix products  19.1 us (7%)
    all_to_all x4, blocking collectives, swap(): return lax.all_to_all(values, axes, 0, 0, tiled=True)  57 us
    all_to_all x3, starting transfers between devices, swap(): return lax.all_to_all(values, axes, 0, 0, tiled=True)  43.7 us
    all_to_all x3, waiting for transfers between devices, swap(): return lax.all_to_all(values, axes, 0, 0, tiled=True)  37.1 us
    ppermute x2, waiting for transfers between devices, cross(): return lax.ppermute(values, 'zh', [(0, 1), (1, 0)])  18.9 us
    ppermute x2, starting transfers between devices, cross(): return lax.ppermute(values, 'zh', [(0, 1), (1, 0)])  14.2 us
    ppermute x4, starting transfers between devices, spread(): return lax.ppermute(block, 'x', [(i, (i + shift) % 4) for i in range(4)])  13.9 us
    dot_general x16, matrix products, side_sums(): jnp.dot(c, t.T, preferred_element_type=F32)  12.8 us
    unnamed x30, local copies, waits for them, and re-layouts  7.29 us
  transfers between devices with their start and end apart: 9, of which 4 were waited for; matrix products, arithmetic and copies ran while one was open for 11% of the time, Pallas kernels for 0%

profile of v2, /device:TPU:1, one launch (start us, length us, event | category | flops | bytes accessed | tf_op | source)
XLA Modules:
  0.0 260.5 jit_solution(12232542522891155934)
XLA Ops:
  0.0 2.6 %pad_maximum_fusion = bf16[80,100,256]{2,0,1:T(8,128)(2,1)S(1)} fusion(bf16[80,100,128]{2,0,1:T(8,128)(2,1)} %param.8, bf16[80,100,128]{2,0,1:T(8,128)(2,1)} %param.7), kind=kLoop, calls=%fused_computation.3 | loop fusion | flops 8192000 | bytes 8192000 | tf_op jit(solution)/shard_map/concatenate | solution.py:84
  2.7 1.9 copy-done.1
  5.6 5.5 %collective-permute-start.3 = (bf16[1000,256]{1,0:T(8,128)(2,1)}, bf16[1000,256]{1,0:T(8,128)(2,1)}, u32[]{:S(2)}, u32[]{:S(2)}) collective-permute-start(bf16[1000,256]{1,0:T(8,128)(2,1)} %get-tuple-element.39), channel_id=1, source_target_pairs={{0,2},{1,3},{2,0},{3,1},{4,6},{5,7},{6,4},{7,5},{8,10},{9,11},{10,... | collective-permute-start | bytes 1536008 | tf_op jit(solution)/shard_map/ppermute | solution.py:91
  11.1 1.9 collective-permute-start.2
  13.0 2.6 %dynamic-slice_bitcast_fusion = (bf16[2000,256]{1,0:T(8,128)(2,1)}, bf16[2000,256]{1,0:T(8,128)(2,1)S(1)}) fusion(bf16[4,2000,256]{2,1,0:T(8,128)(2,1)} %bitcast.161, s32[]{:T(128)S(6)} %select_n.251, s32[]{:T(128)S(6)} %select_n.249), kind=kLoop, calls=%fused_computation.60 | loop fusion | bytes 4096008 | tf_op jit(solution)/shard_map/jit(dynamic_index_in_dim)/squeeze | solution.py:88
  15.7 4.6 %collective-permute-start.1 = (bf16[2000,256]{1,0:T(8,128)(2,1)}, bf16[2000,256]{1,0:T(8,128)(2,1)S(1)}, u32[]{:S(2)}, u32[]{:S(2)}) collective-permute-start(bf16[2000,256]{1,0:T(8,128)(2,1)} %get-tuple-element.41), channel_id=1, source_target_pairs={{0,3},{1,0},{2,1},{3,2},{4,7},{5,4},{6,5},{7,6},{8,11},{9,8},{10,9... | collective-permute-start | bytes 3072008 | tf_op jit(solution)/shard_map/ppermute | solution.py:91
  20.3 1.9 collective-permute-start
  23.6 2.0 gather_fusion.2
  25.6 2.0 gather_fusion.1
  27.7 13.6 %all_to_all.35 = bf16[8,16,256]{2,1,0:T(8,128)(2,1)S(1)} all-to-all(bf16[8,16,256]{2,1,0:T(8,128)(2,1)S(1)} %maximum_select_fusion), channel_id=1, replica_groups=mesh['zl'=8,'yh'=2,'yl'=2,'c'=2,'zh'=2,'x'=4] {'yh','yl','c'}, dimensions={0} | all-to-all | bytes 131072 | tf_op jit(solution)/shard_map/all_to_all | solution.py:45
  42.0 9.2 %all-to-all-start.1 = ((bf16[8,16,256]{2,1,0:T(8,128)(2,1)}), bf16[8,16,256]{2,1,0:T(8,128)(2,1)S(1)}, u32[]{:S(2)}, u32[]{:S(2)}) async-start(bf16[8,16,256]{2,1,0:T(8,128)(2,1)} %broadcast_in_dim.36), calls=%async_computation.1 | async-start | bytes 131072 | tf_op jit(solution)/shard_map/all_to_all | solution.py:45
  51.3 9.8 %all-to-all-done.1 = bf16[8,16,256]{2,1,0:T(8,128)(2,1)S(1)} async-done(((bf16[8,16,256]{2,1,0:T(8,128)(2,1)}), bf16[8,16,256]{2,1,0:T(8,128)(2,1)S(1)}, u32[]{:S(2)}, u32[]{:S(2)}) %all-to-all-start.1) | async-done | bytes 65568 | tf_op jit(solution)/shard_map/all_to_all | solution.py:45
  61.8 7.5 %all-to-all-start.2 = ((bf16[32,16,256]{2,1,0:T(8,128)(2,1)}), bf16[32,16,256]{2,1,0:T(8,128)(2,1)S(1)}, u32[]{:S(2)}, u32[]{:S(2)}) async-start(bf16[32,16,256]{2,1,0:T(8,128)(2,1)} %broadcast_in_dim.37), calls=%async_computation.2 | async-start | bytes 524288 | tf_op jit(solution)/shard_map/all_to_all | solution.py:45
  71.6 6.6 %all-to-all-done.2 = bf16[32,16,256]{2,1,0:T(8,128)(2,1)S(1)} async-done(((bf16[32,16,256]{2,1,0:T(8,128)(2,1)}), bf16[32,16,256]{2,1,0:T(8,128)(2,1)S(1)}, u32[]{:S(2)}, u32[]{:S(2)}) %all-to-all-start.2) | async-done | bytes 262176 | tf_op jit(solution)/shard_map/all_to_all | solution.py:45
  78.5 1.7 fusion.27
  80.9 2.6 %fusion.25 = f32[2000,128]{1,0:T(8,128)} fusion(bf16[4,2000,256]{2,1,0:T(8,128)(2,1)} %bitcast.163, s32[]{:T(128)S(6)} %select_n.239, bf16[64,128]{1,0:T(8,128)(2,1)S(1)} %slice.136, bf16[64,256]{1,0:T(8,128)(2,1)S(1)} %get-tuple-element.51), kind=kOutput, calls=%fused_computation.55 | convolution fusion | flops 131268608 | bytes 2097156 | tf_op jit(solution)/shard_map/dot_general | solution.py:122
  89.9 11.0 %collective-permute-start.5 = (f32[64,128]{0,1:T(8,128)S(1)}, f32[64,128]{0,1:T(8,128)S(1)}, u32[]{:S(2)}, u32[]{:S(2)}) collective-permute-start(f32[64,128]{0,1:T(8,128)S(1)} %convolution_add_fusion.4), channel_id=1, source_target_pairs={{0,4},{4,0},{1,5},{5,1},{2,6},{6,2},{3,7},{7,3},{8,12},{12,8},{9,1... | collective-permute-start | bytes 98312 | tf_op jit(solution)/shard_map/ppermute | solution.py:125
  100.9 1.6 convolution_add_fusion.1
  105.5 3.2 %collective-permute-start.4 = (f16[2016,128]{1,0:T(8,128)(2,1)S(1)}, f16[2016,128]{1,0:T(8,128)(2,1)S(1)}, u32[]{:S(2)}, u32[]{:S(2)}) collective-permute-start(f16[2016,128]{1,0:T(8,128)(2,1)S(1)} %pad_maximum_fusion.2), channel_id=1, source_target_pairs={{0,4},{4,0},{1,5},{5,1},{2,6},{6,2},{3,7},{7,3},{8,12},{12,8},{9,1... | collective-permute-start | bytes 1548296 | tf_op jit(solution)/shard_map/ppermute | solution.py:125
  110.4 5.8 %cholesky.17 = f32[64,64]{1,0:T(8,128)S(1)} custom-call(f32[64,64]{1,0:T(8,128)S(1)} %fusion.113), custom_call_target="Cholesky" | custom-call | tf_op jit(solution)/shard_map/jit(cholesky)/cholesky | solution.py:131
  117.6 4.9 %custom-call.6 = f32[1,64,64]{1,2,0:T(8,128)S(1)} custom-call(f32[1,64,64]{2,1,0:T(8,128)S(1)} %fusion.92), custom_call_target="InvertDiagBlocksLowerTriangular" | custom-call | tf_op jit(solution)/shard_map/triangular_solve | solution.py:132
  123.0 18.9 %collective-permute-done.4 = f16[2016,128]{1,0:T(8,128)(2,1)S(1)} collective-permute-done((f16[2016,128]{1,0:T(8,128)(2,1)S(1)}, f16[2016,128]{1,0:T(8,128)(2,1)S(1)}, u32[]{:S(2)}, u32[]{:S(2)}) %collective-permute-start.4) | collective-permute-done | bytes 516128 | tf_op jit(solution)/shard_map/ppermute | solution.py:125
  146.2 13.2 %all_to_all.36 = f32[16,1,8000]{2,1,0:T(1,128)S(1)} all-to-all(f32[16,1,8000]{2,1,0:T(1,128)S(1)} %reshape.383), channel_id=1, replica_groups=mesh['zl'=8,'yh'=2,'yl'=2,'c'=2,'zh'=2,'x'=4] {'yl','c','x'}, dimensions={0} | all-to-all | bytes 1024000 | tf_op jit(solution)/shard_map/all_to_all | solution.py:45
  159.8 1.9 reduce.9
  163.1 1.8 convolution_bitcast_fusion.1
  170.7 1.7 reshape.350
  173.3 2.3 copy.131
  175.6 27.0 %all-to-all-start.4 = ((f16[32,33,128]{2,1,0:T(8,128)(2,1)}), f16[32,33,128]{2,1,0:T(8,128)(2,1)S(1)}, u32[]{:S(2)}, u32[]{:S(2)}) async-start(f16[32,33,128]{2,1,0:T(8,128)(2,1)} %copy.131), calls=%async_computation.4 | async-start | bytes 655360 | tf_op jit(solution)/shard_map/all_to_all | solution.py:45
  202.8 20.7 %all-to-all-done.4 = f16[32,33,128]{2,1,0:T(8,128)(2,1)S(1)} async-done(((f16[32,33,128]{2,1,0:T(8,128)(2,1)}), f16[32,33,128]{2,1,0:T(8,128)(2,1)S(1)}, u32[]{:S(2)}, u32[]{:S(2)}) %all-to-all-start.4) | async-done | bytes 270368 | tf_op jit(solution)/shard_map/all_to_all | solution.py:45
  224.9 1.8 convolution_bitcast_fusion
  227.6 16.4 %all_to_all.37 = f32[32,1,1024]{2,1,0:T(1,128)S(1)} all-to-all(f32[32,1,1024]{2,1,0:T(1,128)S(1)} %reshape.385), channel_id=1, replica_groups=mesh['zl'=8,'yh'=2,'yl'=2,'c'=2,'zh'=2,'x'=4] {'yh','yl','c','x'}, dimensions={0} | all-to-all | bytes 262144 | tf_op jit(solution)/shard_map/all_to_all | solution.py:45
  245.2 13.9 %all_to_all.38 = f32[16,1,512]{2,1,0:T(1,128)S(1)} all-to-all(f32[16,1,512]{2,1,0:T(1,128)S(1)} %reshape.387), channel_id=1, replica_groups=mesh['zl'=8,'yh'=2,'yl'=2,'c'=2,'zh'=2,'x'=4] {'zl','zh'}, dimensions={0} | all-to-all | bytes 65536 | tf_op jit(solution)/shard_map/all_to_all | solution.py:45
  (128 shorter events, 37.5 us)
Async XLA Ops:
  0.0 22.3 %copy-start = (s32[128]{0:T(128)S(1)}, s32[128]{0:T(128)}, u32[]{:S(2)}) copy-start(s32[128]{0:T(128)} %param.9) | copy-start | bytes 1540
  2.7 1.9 copy-start.1
  5.6 64.9 %collective-permute-start.3 = (bf16[1000,256]{1,0:T(8,128)(2,1)}, bf16[1000,256]{1,0:T(8,128)(2,1)}, u32[]{:S(2)}, u32[]{:S(2)}) collective-permute-start(bf16[1000,256]{1,0:T(8,128)(2,1)} %get-tuple-element.39), channel_id=1, source_target_pairs={{0,2},{1,3},{2,0},{3,1},{4,6},{5,7},{6,4},{7,5},{8,10},{9,11},{10,... | collective-permute-start | bytes 1536008 | tf_op jit(solution)/shard_map/ppermute | solution.py:91
  11.1 50.0 %collective-permute-start.2 = (bf16[1000,256]{1,0:T(8,128)(2,1)}, bf16[1000,256]{1,0:T(8,128)(2,1)}, u32[]{:S(2)}, u32[]{:S(2)}) collective-permute-start(bf16[1000,256]{1,0:T(8,128)(2,1)} %get-tuple-element.40), channel_id=1, source_target_pairs={{0,2},{1,3},{2,0},{3,1},{4,6},{5,7},{6,4},{7,5},{8,10},{9,11},{10,... | collective-permute-start | bytes 1536008 | tf_op jit(solution)/shard_map/ppermute | solution.py:91
  13.0 9.2 %copy-start.9 = (s32[2,64]{1,0:T(2,128)S(1)}, s32[2,64]{1,0:T(2,128)}, u32[]{:S(2)}) copy-start(s32[2,64]{1,0:T(2,128)} %param.10) | copy-start | bytes 1540
  15.7 45.4 %collective-permute-start.1 = (bf16[2000,256]{1,0:T(8,128)(2,1)}, bf16[2000,256]{1,0:T(8,128)(2,1)S(1)}, u32[]{:S(2)}, u32[]{:S(2)}) collective-permute-start(bf16[2000,256]{1,0:T(8,128)(2,1)} %get-tuple-element.41), channel_id=1, source_target_pairs={{0,3},{1,0},{2,1},{3,2},{4,7},{5,4},{6,5},{7,6},{8,11},{9,8},{10,9... | collective-permute-start | bytes 3072008 | tf_op jit(solution)/shard_map/ppermute | solution.py:91
  20.3 40.8 %collective-permute-start = (bf16[2000,256]{1,0:T(8,128)(2,1)S(1)}, bf16[2000,256]{1,0:T(8,128)(2,1)S(1)}, u32[]{:S(2)}, u32[]{:S(2)}) collective-permute-start(bf16[2000,256]{1,0:T(8,128)(2,1)S(1)} %get-tuple-element.42), channel_id=1, source_target_pairs={{0,1},{1,2},{2,3},{3,0},{4,5},{5,6},{6,7},{7,4},{8,9},{9,10},{10,1... | collective-permute-start | bytes 3072008 | tf_op jit(solution)/shard_map/ppermute | solution.py:91
  27.6 50.6 %copy-start.8 = (pred[256]{0:T(512)(128)(4,1)S(1)}, pred[256]{0:T(512)(128)(4,1)}, u32[]{:S(2)}) copy-start(pred[256]{0:T(512)(128)(4,1)} %constant.376.clone.1) | copy-start | bytes 772
  42.0 19.0 %all-to-all-start.1 = ((bf16[8,16,256]{2,1,0:T(8,128)(2,1)}), bf16[8,16,256]{2,1,0:T(8,128)(2,1)S(1)}, u32[]{:S(2)}, u32[]{:S(2)}) async-start(bf16[8,16,256]{2,1,0:T(8,128)(2,1)} %broadcast_in_dim.36), calls=%async_computation.1 | async-start | bytes 131072 | tf_op jit(solution)/shard_map/all_to_all | solution.py:45
  61.0 8.4 %copy-start.2 = (bf16[2000,256]{1,0:T(8,128)(2,1)}, bf16[2000,256]{1,0:T(8,128)(2,1)S(1)}, u32[]{:S(2)}) copy-start(bf16[2000,256]{1,0:T(8,128)(2,1)S(1)} %collective-permute-done.1) | copy-start | bytes 3072004
  61.8 16.4 %all-to-all-start.2 = ((bf16[32,16,256]{2,1,0:T(8,128)(2,1)}), bf16[32,16,256]{2,1,0:T(8,128)(2,1)S(1)}, u32[]{:S(2)}, u32[]{:S(2)}) async-start(bf16[32,16,256]{2,1,0:T(8,128)(2,1)} %broadcast_in_dim.37), calls=%async_computation.2 | async-start | bytes 524288 | tf_op jit(solution)/shard_map/all_to_all | solution.py:45
  89.9 20.2 %collective-permute-start.5 = (f32[64,128]{0,1:T(8,128)S(1)}, f32[64,128]{0,1:T(8,128)S(1)}, u32[]{:S(2)}, u32[]{:S(2)}) collective-permute-start(f32[64,128]{0,1:T(8,128)S(1)} %convolution_add_fusion.4), channel_id=1, source_target_pairs={{0,4},{4,0},{1,5},{5,1},{2,6},{6,2},{3,7},{7,3},{8,12},{12,8},{9,1... | collective-permute-start | bytes 98312 | tf_op jit(solution)/shard_map/ppermute | solution.py:125
  102.5 1.2 copy-start.3
  105.5 36.4 %collective-permute-start.4 = (f16[2016,128]{1,0:T(8,128)(2,1)S(1)}, f16[2016,128]{1,0:T(8,128)(2,1)S(1)}, u32[]{:S(2)}, u32[]{:S(2)}) collective-permute-start(f16[2016,128]{1,0:T(8,128)(2,1)S(1)} %pad_maximum_fusion.2), channel_id=1, source_target_pairs={{0,4},{4,0},{1,5},{5,1},{2,6},{6,2},{3,7},{7,3},{8,12},{12,8},{9,1... | collective-permute-start | bytes 1548296 | tf_op jit(solution)/shard_map/ppermute | solution.py:125
  109.2 0.8 copy-start.5
  142.7 0.8 copy-start.6
  162.3 0.8 copy-start.7
  168.4 0.9 copy-start.4
  175.6 47.9 %all-to-all-start.4 = ((f16[32,33,128]{2,1,0:T(8,128)(2,1)}), f16[32,33,128]{2,1,0:T(8,128)(2,1)S(1)}, u32[]{:S(2)}, u32[]{:S(2)}) async-start(f16[32,33,128]{2,1,0:T(8,128)(2,1)} %copy.131), calls=%async_computation.4 | async-start | bytes 655360 | tf_op jit(solution)/shard_map/all_to_all | solution.py:45
  223.7 1.3 copy-start.10

commit v3 on v2

v3 whole, which is shorter than its diff:
```python
import math

import jax
import jax.numpy as jnp
import ml_dtypes
import numpy as np
from jax import lax
from jax.experimental import pallas as pl
from jax.experimental.pallas import tpu as pltpu
from jax.sharding import Mesh, PartitionSpec as P

N = 80
PANEL = 64
GRID = ("zl", "yh", "yl", "c")
ORB = ("zh", "x")
ROWS = ("yh", "yl", "c")
PLANE = ("yl", "c", "x")
RING = ("yh", "zl", "zh")
BF16 = jnp.bfloat16
F32 = jnp.float32
LEVELS = 252.9
SPAN = 5.21
SHIFTS = (0, 1, 3, 2)
TILE = 400
CELLS = 2000
FOUR_PI = 4.0 * math.pi
TWO_PI = 2.0 * math.pi


def real_basis():
    steps = np.arange(N)
    freqs = np.concatenate([np.arange(N // 2 + 1), np.arange(1, N // 2)])
    angle = TWO_PI / N * (freqs[:, None] * steps[None, :] % N)
    table = np.where(np.arange(N)[:, None] <= N // 2, np.cos(angle), np.sin(angle)) * math.sqrt(2.0 / N)
    table[0] /= math.sqrt(2.0)
    table[N // 2] /= math.sqrt(2.0)
    return table.astype(np.float32)


def freq_square(index):
    freq = jnp.where(index > N // 2, index - N // 2, index).astype(F32)
    wave = TWO_PI / N * freq
    return wave * wave


def mix(form, left, right):
    return jnp.einsum(form, left, right, precision=lax.Precision.HIGHEST, preferred_element_type=F32)


def swap(values, axes):
    return lax.all_to_all(values, axes, 0, 0, tiled=True)


def lane_power(square_sum, count):
    return jnp.ceil(0.5 * jnp.log2(jnp.maximum(square_sum * (1.0 / count), 1e-37))) - 1.0


def encode(values, power):
    size = jnp.abs(values) * jnp.exp2(-power)
    level = jnp.log(size + jnp.sqrt(size * size + 1.0)) * (LEVELS / SPAN)
    whole = jnp.floor(level)
    code = jnp.exp2(whole - 126.0) * (1.0 + (level - whole))
    return jnp.where(values < 0, -code, code)


def decode(code, power):
    size = jnp.abs(code)
    whole = jnp.floor(jnp.log2(size) + 1e-3)
    level = whole + (size * jnp.exp2(-whole) - 1.0) + 126.0
    spread = jnp.exp(level * (SPAN / LEVELS))
    value = 0.5 * (spread - 1.0 / spread) * jnp.exp2(power)
    return jnp.where(code < 0, -value, value)


def whole_call(kernel, out_shape, scratch, scalars, *arrays):
    vmem = pl.BlockSpec(memory_space=pltpu.VMEM)
    shapes = [a.shape for a in arrays]
    moved = sum(math.prod(shape) * 4 for shape in shapes)
    return pl.pallas_call(
        kernel,
        out_shape=out_shape,
        in_specs=[pl.BlockSpec(memory_space=pltpu.SMEM)] * len(scalars) + [vmem] * len(arrays),
        out_specs=jax.tree.map(lambda _: vmem, out_shape),
        scratch_shapes=scratch,
        compiler_params=pltpu.CompilerParams(vmem_limit_bytes=40 * 2**20),
        cost_estimate=pl.CostEstimate(flops=2 * 10**9, bytes_accessed=moved, transcendentals=0),
    )(*scalars, *arrays)


def head_rows(points_ref, shift, x_rank, panel):
    block = lax.rem(x_rank - shift + 4, 4)
    return jnp.concatenate([points_ref[(panel * 4 + i) * 4 + block] for i in range(4)], axis=0)


def side_table(head):
    half = head.shape[1] // 2
    gap = jnp.zeros((head.shape[0], half), head.dtype)
    upper = jnp.concatenate([head[:, :half], gap], axis=1)
    lower = jnp.concatenate([gap, head[:, half:]], axis=1)
    return jnp.concatenate([upper, lower], axis=0)


def dot_rows(left, right, precision=None):
    return lax.dot_general(left, right, (((1,), (1,)), ((), ())), precision=precision, preferred_element_type=F32)


def split(values):
    high = values.astype(BF16)
    return high, (values - high.astype(F32)).astype(BF16)


def dot_two(table_ref, values):
    high, low = split(values)
    count = table_ref.shape[0] // 2
    top, rest = table_ref[pl.ds(0, count), :], table_ref[pl.ds(count, count), :]
    return dot(top, high) + (dot(top, low) + dot(rest, high))


def dot(left, right):
    return lax.dot_general(left, right, (((1,), (0,)), ((), ())), preferred_element_type=F32)


def two_parts(table):
    high = table.astype(ml_dtypes.bfloat16)
    low = (table - high.astype(np.float32)).astype(ml_dtypes.bfloat16)
    return jnp.asarray(np.concatenate([high, low], axis=0))


def cell_tiles(blocks):
    own, left, right, far_low, far_high = blocks
    for tile in range(5):
        rows = pl.ds(tile * TILE, TILE)
        far = far_low[rows, :] if tile < 3 else far_high[pl.ds((tile - 3) * TILE, TILE), :]
        yield rows, (own[rows, :], left[rows, :], right[rows, :], far)


def sums_kernel(rank_ref, points_ref, own, left, right, far_low, far_high, up_ref, down_ref, sum_ref):
    half = rank_ref[1]
    tables = []
    for shift in SHIFTS:
        heads = [head_rows(points_ref, shift, rank_ref[0], panel) for panel in (half, 1 - half)]
        tables.append(jnp.concatenate([side_table(head) for head in heads], axis=0))
    square = jnp.zeros((1, 4 * PANEL), F32)
    for rows, parts in cell_tiles((own, left, right, far_low, far_high)):
        total = sum(dot_rows(part, table) for part, table in zip(parts, tables))
        sum_ref[rows, :] = total
        square = square + jnp.sum(total * total, axis=0, keepdims=True)
    power = lane_power(square, CELLS)
    for out_ref, low in ((up_ref, 0), (down_ref, 2 * PANEL)):
        lanes = pl.ds(low, 2 * PANEL)
        own_power = power[:, low : low + 2 * PANEL]
        for tile in range(5):
            rows = pl.ds(tile * TILE, TILE)
            out_ref[rows, :] = encode(sum_ref[rows, lanes], own_power).astype(BF16)
        out_ref[pl.ds(CELLS, 16), :] = jnp.broadcast_to(own_power, (16, 2 * PANEL)).astype(BF16)


def gram_kernel(rank_ref, points_ref, gram_ref, other_ref):
    for out_ref, panel in ((gram_ref, rank_ref[2]), (other_ref, 1 - rank_ref[2])):
        heads = [head_rows(points_ref, shift, rank_ref[0], panel) for shift in SHIFTS]
        out_ref[...] = sum(dot_rows(head, side_table(head)) for head in heads)


def first_kernel(below_ref, above_ref, basis_ref, out_ref):
    powers = [ref[pl.ds(CELLS, 16), :].astype(F32)[:1] for ref in (below_ref, above_ref)]
    left_lanes = lax.broadcasted_iota(jnp.int32, (N, 2 * PANEL), 1) < PANEL
    out_ref[...] = jnp.zeros_like(out_ref)

    def product(column):
        rows = pl.ds(column * N, N)
        sums = decode(below_ref[rows, :].astype(F32), powers[0]) + decode(above_ref[rows, :].astype(F32), powers[1])
        return sums * pltpu.roll(sums, PANEL, 1)

    pairs = []
    for pair in range(13):
        right = product(pair + 13) if pair < 12 else 0.0
        pairs.append(jnp.where(left_lanes, product(pair), right))
    moved = dot_two(basis_ref, jnp.concatenate(pairs, axis=1))
    for pair in range(13):
        for k in range(5):
            rows = moved[k * 16 : k * 16 + 16, pair * 2 * PANEL : (pair + 1) * 2 * PANEL]
            out_ref[pl.ds(k * 16 + pair, 16, stride=80), :] = rows


def inverse_kernel(mine_ref, other_ref, out_ref):
    sums = mine_ref[...] + other_ref[...]
    matrix = sums * pltpu.roll(sums, PANEL, 1)
    lane = lax.broadcasted_iota(jnp.int32, (PANEL, 2 * PANEL), 1)
    line = lax.broadcasted_iota(jnp.int32, (PANEL, 2 * PANEL), 0)
    for step in range(PANEL):
        scale = 1.0 / matrix[step : step + 1, step : step + 1]
        row = jnp.where(lane[:1] == step, 1.0, matrix[step : step + 1]) * scale
        column = matrix[:, step : step + 1]
        rest = jnp.where(lane == step, 0.0, matrix) - column * row
        matrix = jnp.where(line == step, row, rest)
    out_ref[pl.ds(0, PANEL), :] = jnp.where(lane < PANEL, matrix, 0.0)
    out_ref[pl.ds(PANEL, PANEL), :] = jnp.where(lane < PANEL, 0.0, pltpu.roll(matrix, PANEL, 1))


def second_kernel(in_ref, table_ref, inverse_ref, out_ref, line_ref, code_ref):
    left_lanes = lax.broadcasted_iota(jnp.int32, (200, 2 * PANEL), 1) < PANEL
    data = [in_ref[:, pl.ds(k * 16, 16), :].reshape(256, 2 * PANEL) for k in range(5)]
    moved = dot_two(table_ref, jnp.concatenate(data, axis=1))
    inverse = split(inverse_ref[...])
    square = jnp.zeros((1, 2 * PANEL), F32)
    for k in range(5):
        part = moved[:, k * 2 * PANEL : (k + 1) * 2 * PANEL]
        low = part[:200] + pltpu.roll(part[200:400], PANEL, 1)
        high = pltpu.roll(part[400:600], PANEL, 1) + part[600:]
        top, rest = split(jnp.where(left_lanes, low, high))
        mixed = dot(top, inverse[0]) + (dot(top, inverse[1]) + dot(rest, inverse[0]))
        line_ref[pl.ds(k * 200, 200), :] = mixed
        square = square + jnp.sum(mixed * mixed, axis=0, keepdims=True)
    power = lane_power(square, 1000)
    line_ref[pl.ds(1000, 120), :] = jnp.zeros((120, 2 * PANEL), F32)
    for tile in range(4):
        rows = pl.ds(tile * 280, 280)
        line_ref[rows, :] = encode(line_ref[rows, :], power)
    for to in range(32):
        code_ref[pl.ds(40 * to, 35), :] = line_ref[pl.ds(35 * to, 35), :]
        code_ref[pl.ds(40 * to + 35, 5), :] = jnp.broadcast_to(power, (5, 2 * PANEL))
    for tile in range(4):
        rows = pl.ds(tile * 320, 320)
        out_ref[rows, :] = code_ref[rows, :].astype(BF16)


def third_kernel(got_ref, table_ref, kernel_ref, out_ref):
    keep = lax.broadcasted_iota(jnp.int32, (40, 2 * PANEL), 0) < 35

    def side(panel):
        parts = []
        for source in range(16):
            block = got_ref[2 * source + (panel + (source % 8 < 4)) % 2].astype(F32)
            parts.append(jnp.where(keep, decode(jnp.where(keep, block, 1.0), block[35:36]), 0.0))
        return jnp.concatenate(parts, axis=0)

    moved = dot_two(table_ref, jnp.concatenate([side(0), side(1)], axis=1))
    fit_top, fit_rest = split(moved[:, : 2 * PANEL] * kernel_ref[...])
    bra_top, bra_rest = split(moved[:, 2 * PANEL :])

    def meet(left, right):
        return lax.dot_general(left, right, (((0,), (0,)), ((), ())), preferred_element_type=F32)

    total = meet(bra_top, fit_top) + (meet(bra_top, fit_rest) + meet(bra_rest, fit_top))
    out_ref[...] = total[:PANEL, :PANEL] + total[PANEL:, PANEL:]


def second_table():
    basis = real_basis().astype(np.float64)
    full = np.zeros((N, 5, 5 * N))
    for row in range(5):
        full[:, row, row * N : (row + 1) * N] = basis
    full = full.reshape(2, 200, 16, 25)
    table = np.zeros((2, 2, 200, 16, 16))
    table[:, 0, :, :, :13] = full[..., :13]
    table[:, 1, :, :, :12] = full[..., 13:]
    return table.reshape(800, 256).astype(np.float32)


def third_table():
    basis = np.roll(real_basis().reshape(N, 8, 2, 5).transpose(0, 2, 1, 3), 4, axis=2)
    table = np.zeros((7, N, 2, 8, 40), np.float32)
    for pair in range(7):
        table[pair, ..., pair * 5 : pair * 5 + 5] = basis
    return table.reshape(7 * N, 640)


def shards(occupied, virtual, points, panels):
    x_rank = lax.axis_index("x")
    zh_rank = lax.axis_index("zh")
    grid_rank = lax.axis_index(GRID)
    columns = occupied.shape[1]
    width = occupied.shape[2]
    per_x = columns // 4

    parts = jnp.concatenate([occupied, virtual], axis=2).reshape(N, 4, per_x, 2 * width)
    parts = parts.transpose(1, 2, 0, 3).reshape(4, per_x * N, 2 * width)

    wanted = panels.reshape(-1, 1) == jnp.arange(2 * PANEL, dtype=jnp.int32)
    chosen = jnp.sum(jnp.where(wanted, points, 0), axis=1)
    within = chosen % (N * N) - grid_rank * columns
    inside = (within >= 0) & (within < columns)
    plane_of = chosen // (N * N)
    column_of = jnp.where(inside, within, 0)
    here = jnp.concatenate([occupied[plane_of, column_of], virtual[plane_of, column_of]], axis=1)
    here = jnp.where(inside[:, None], here, jnp.zeros((), BF16))

    def take(shift):
        return lax.dynamic_index_in_dim(parts, (x_rank + shift) % 4, 0, keepdims=False)

    def spread(block, shift):
        return lax.ppermute(block, "x", [(i, (i + shift) % 4) for i in range(4)])

    far = take(2)
    split = 3 * TILE
    own, left, right = take(0), spread(take(1), 1), spread(take(3), 3)
    far_low = spread(far[:split], 2)

    def add(values):
        return jnp.sum(values.astype(F32), axis=0).astype(BF16)

    rows = add(swap(here.reshape(8, 16, 2 * width), ROWS))
    rows = add(swap(jnp.broadcast_to(rows[None], (8, 16, 2 * width)), "zl"))
    rows, left, right, far_low = lax.optimization_barrier((rows, left, right, far_low))
    far_high = spread(far[split:], 2)
    pts = swap(jnp.broadcast_to(rows[None], (32, 16, 2 * width)), ROWS + ("x",))

    def cross(values):
        return lax.ppermute(values, "zh", [(0, 1), (1, 0)])

    def full(rows, dtype=F32, lanes=2 * PANEL):
        return jax.ShapeDtypeStruct((rows, lanes), dtype)

    panel = ((lax.axis_index("zl") >= 4) == (zh_rank == 1)).astype(jnp.int32)
    ranks = jnp.stack([x_rank, zh_rank, panel]).astype(jnp.int32)
    blocks = (own, left, right, far_low, far_high)
    outs = (full(CELLS + 16, BF16), full(CELLS + 16, BF16))
    up, down = whole_call(sums_kernel, outs, [pltpu.VMEM((CELLS, 4 * PANEL), F32)], (ranks,), pts, *blocks)
    ring = [(z % 8) * 2 + z // 8 for z in range(16)]
    below = lax.ppermute(up, ("zl", "zh"), [(ring[z], ring[(z + 4) % 16]) for z in range(16)])
    above = lax.ppermute(down, ("zl", "zh"), [(ring[z], ring[(z + 12) % 16]) for z in range(16)])
    pts, up = lax.optimization_barrier((pts, up))
    gram, other_gram = whole_call(gram_kernel, (full(PANEL), full(PANEL)), [], (ranks,), pts)
    other_gram = cross(other_gram)

    basis_a = real_basis().reshape(16, 5, N).transpose(1, 0, 2).reshape(N, N)
    fields = whole_call(first_kernel, full(16 * 80), [], (), below, above, two_parts(basis_a))
    fields, gram, other_gram = lax.optimization_barrier((fields, gram, other_gram))
    inverse = whole_call(inverse_kernel, full(2 * PANEL), [], (), gram, other_gram)
    fields = swap(fields.reshape(16, 80, 2 * PANEL), PLANE)
    scratch = [pltpu.VMEM((1120, 2 * PANEL), F32), pltpu.VMEM((1280, 2 * PANEL), F32)]
    fields = whole_call(second_kernel, full(1280, BF16), scratch, (), fields, two_parts(second_table()), inverse)
    fields = swap(fields.reshape(32, 40, 2 * PANEL), RING)

    slot = lax.axis_index(RING) * 7 + jnp.arange(7, dtype=jnp.int32)
    square_a = freq_square(lax.axis_index(PLANE) * 5 + slot // 40)
    square_c = freq_square(slot[:, None] % 40 + jnp.arange(2, dtype=jnp.int32)[None, :] * 40)
    square_b = freq_square(jnp.arange(N, dtype=jnp.int32))
    squared = square_a[:, None, None] + square_b[None, :, None] + square_c[:, None, :]
    live = (squared > 0) & (slot < 200)[:, None, None]
    kernel = jnp.where(live, 32.0 * FOUR_PI / jnp.where(squared > 0, squared, 1.0), 0.0)
    kernel = jnp.broadcast_to(kernel[..., None], (7, N, 2, PANEL)).reshape(7 * N, 2 * PANEL)
    part = whole_call(third_kernel, full(PANEL, F32, PANEL), [], (), fields, two_parts(third_table()), kernel)
    part = part.reshape(2, 4, 8, PANEL).transpose(1, 0, 2, 3)
    part = jnp.broadcast_to(part[None], (8, 4, 2, 8, PANEL)).reshape(32, 16, PANEL)
    part = jnp.sum(swap(part, ROWS + ("x",)), axis=0)
    part = jnp.broadcast_to(part.reshape(1, 2, 8, PANEL), (8, 2, 8, PANEL)).reshape(16, 8, PANEL)
    return jnp.sum(swap(part, ("zl", "zh")), axis=0)


def solution(mesh):
    devices = mesh.devices.reshape(8, 2, 2, 2, 2, 4)
    inner = Mesh(devices, ("zl", "yh", "yl", "c", "zh", "x"))
    in_specs = (P(None, GRID, ORB), P(None, GRID, ORB), P(), P())
    return jax.shard_map(shards, mesh=inner, in_specs=in_specs, out_specs=P(ORB, None), check_vma=False)
```

time: 262 us -> 234 us (0.89)
  waiting for transfers between devices: 56 us -> 85.1 us
  blocking collectives: 57 us -> 30.2 us
  Pallas kernels: 0 us -> 19.5 us
  matrix products: 19.1 us -> 0 us
  local copies, waits for them, and re-layouts: 31.3 us -> 12.3 us
  other arithmetic: 24.4 us -> 6.27 us
  starting transfers between devices: 71.8 us -> 79.1 us
    ppermute x0 -> x2, waiting for transfers between devices: none -> 39.9 us  [the longest x1 33.7 us: shards(): lax.ppermute(up, ('zl', 'zh'), [(ring[z], ring[(z + 4) % 16]) for z in ra...]
    all_to_all x4 -> x2, blocking collectives: 57 us -> 30.2 us  [swap(): return lax.all_to_all(values, axes, 0, 0, tiled=True)]
    pallas_call x0 -> x6, Pallas kernels: none -> 19.5 us  [whole_call(): pl.pallas_call(kernel, out_shape=out_shape, in_specs=[pl.BlockSpec(memory...]
    ppermute x2 -> x1, waiting for transfers between devices: 18.9 us -> 0.01 us  [cross(): return lax.ppermute(values, 'zh', [(0, 1), (1, 0)])]
    dot_general x21 -> x0, matrix products: 18 us -> none  [the longest x16 12.8 us: side_sums(): jnp.dot(c, t.T, preferred_element_type=F32)]
    ppermute x0 -> x2, starting transfers between devices: none -> 17.1 us  [the longest x1 14.3 us: shards(): lax.ppermute(down, ('zl', 'zh'), [(ring[z], ring[(z + 12) % 16]) for z in...]
    another operation x5 -> x1, other arithmetic: 12.1 us -> 0.08 us  [shards(): ranks = jnp.stack([x_rank, zh_rank, panel]).astype(jnp.int32)]
    all_to_all x3 -> x5, waiting for transfers between devices: 37.1 us -> 45.2 us  [swap(): return lax.all_to_all(values, axes, 0, 0, tiled=True)]
  transfers between devices with their start and end apart: 9 -> 12, of which waited for: 4 -> 7; matrix products, arithmetic and copies ran while one was open for 11% -> 5% of each run, Pallas kernels for 0% -> 4%
where the time goes in v3:
time: 234 us; the launch traced here: 233 us
  waiting for transfers between devices  85.1 us (36%)
  starting transfers between devices  79.1 us (34%)
  blocking collectives  30.2 us (13%)
  Pallas kernels  19.5 us (8%)
  local copies, waits for them, and re-layouts  12.3 us (5%)
  other arithmetic  6.27 us (3%)
    all_to_all x5, waiting for transfers between devices, swap(): return lax.all_to_all(values, axes, 0, 0, tiled=True)  45.2 us
    all_to_all x5, starting transfers between devices, swap(): return lax.all_to_all(values, axes, 0, 0, tiled=True)  37.6 us
    ppermute x1, waiting for transfers between devices, shards(): lax.ppermute(up, ('zl', 'zh'), [(ring[z], ring[(z + 4) % 16]) for z in ra...  33.7 us
    all_to_all x2, blocking collectives, swap(): return lax.all_to_all(values, axes, 0, 0, tiled=True)  30.2 us
    pallas_call x6, Pallas kernels, whole_call(): pl.pallas_call(kernel, out_shape=out_shape, in_specs=[pl.BlockSpec(memory...  19.5 us
    ppermute x1, starting transfers between devices, shards(): lax.ppermute(down, ('zl', 'zh'), [(ring[z], ring[(z + 12) % 16]) for z in...  14.3 us
    ppermute x4, starting transfers between devices, spread(): return lax.ppermute(block, 'x', [(i, (i + shift) % 4) for i in range(4)])  14.1 us
    ppermute x1, starting transfers between devices, cross(): return lax.ppermute(values, 'zh', [(0, 1), (1, 0)])  10.3 us
  transfers between devices with their start and end apart: 12, of which 7 were waited for; matrix products, arithmetic and copies ran while one was open for 5% of the time, Pallas kernels for 4%

profile of v3, /device:TPU:1, one launch (start us, length us, event | category | flops | bytes accessed | tf_op | source)
XLA Modules:
  0.0 232.7 jit_solution(15847662740398926172)
XLA Ops:
  0.0 2.6 %pad_maximum_fusion = bf16[80,100,256]{2,0,1:T(8,128)(2,1)S(1)} fusion(bf16[80,100,128]{2,0,1:T(8,128)(2,1)} %param.8, bf16[80,100,128]{2,0,1:T(8,128)(2,1)} %param.7), kind=kLoop, calls=%fused_computation.2 | loop fusion | flops 8192000 | bytes 8192000 | tf_op jit(solution)/shard_map/concatenate | solution.py:276
  2.7 1.7 dynamic-slice_bitcast_fusion
  4.3 3.9 %collective-permute-start = (bf16[2000,256]{1,0:T(8,128)(2,1)}, bf16[2000,256]{1,0:T(8,128)(2,1)S(1)}, u32[]{:S(2)}, u32[]{:S(2)}) collective-permute-start(bf16[2000,256]{1,0:T(8,128)(2,1)} %get-tuple-element.31), channel_id=1, source_target_pairs={{0,1},{1,2},{2,3},{3,0},{4,5},{5,6},{6,7},{7,4},{8,9},{9,10},{10,1... | collective-permute-start | bytes 3072008 | tf_op jit(solution)/shard_map/ppermute | solution.py:292
  8.3 3.2 %collective-permute-start.1 = (bf16[2000,256]{1,0:T(8,128)(2,1)}, bf16[2000,256]{1,0:T(8,128)(2,1)S(1)}, u32[]{:S(2)}, u32[]{:S(2)}) collective-permute-start(bf16[2000,256]{1,0:T(8,128)(2,1)} %get-tuple-element.30), channel_id=1, source_target_pairs={{0,3},{1,0},{2,1},{3,2},{4,7},{5,4},{6,5},{7,6},{8,11},{9,8},{10,9... | collective-permute-start | bytes 3072008 | tf_op jit(solution)/shard_map/ppermute | solution.py:292
  11.5 1.9 dynamic-slice_bitcast_fusion.3
  13.5 3.6 %collective-permute-start.2 = (bf16[1200,256]{1,0:T(8,128)(2,1)}, bf16[1200,256]{1,0:T(8,128)(2,1)}, u32[]{:S(2)}, u32[]{:S(2)}) collective-permute-start(bf16[1200,256]{1,0:T(8,128)(2,1)} %dynamic-slice_bitcast_fusion.3), channel_id=1, source_target_pairs={{0,2},{1,3},{2,0},{3,1},{4,6},{5,7},{6,4},{7,5},{8,10},{9,11},{10,... | collective-permute-start | bytes 1843208 | tf_op jit(solution)/shard_map/ppermute | solution.py:292
  17.5 2.0 gather_fusion
  19.5 2.0 gather_fusion.1
  22.2 8.3 %all-to-all-start = ((bf16[8,16,256]{2,1,0:T(8,128)(2,1)}), bf16[8,16,256]{2,1,0:T(8,128)(2,1)S(1)}, u32[]{:S(2)}, u32[]{:S(2)}) async-start(bf16[8,16,256]{2,1,0:T(8,128)(2,1)} %maximum_select_fusion), calls=%async_computation | async-start | bytes 131072 | tf_op jit(solution)/shard_map/all_to_all | solution.py:51
  30.5 5.3 %all-to-all-done = bf16[8,16,256]{2,1,0:T(8,128)(2,1)S(1)} async-done(((bf16[8,16,256]{2,1,0:T(8,128)(2,1)}), bf16[8,16,256]{2,1,0:T(8,128)(2,1)S(1)}, u32[]{:S(2)}, u32[]{:S(2)}) %all-to-all-start) | async-done | bytes 65568 | tf_op jit(solution)/shard_map/all_to_all | solution.py:51
  36.4 9.5 %all-to-all-start.1 = ((bf16[8,16,256]{2,1,0:T(8,128)(2,1)}), bf16[8,16,256]{2,1,0:T(8,128)(2,1)S(1)}, u32[]{:S(2)}, u32[]{:S(2)}) async-start(bf16[8,16,256]{2,1,0:T(8,128)(2,1)} %broadcast_in_dim.43), calls=%async_computation.1 | async-start | bytes 131072 | tf_op jit(solution)/shard_map/all_to_all | solution.py:51
  45.9 1.8 dynamic-slice_bitcast_fusion.4
  47.7 3.3 %collective-permute-start.3 = (bf16[800,256]{1,0:T(8,128)(2,1)}, bf16[800,256]{1,0:T(8,128)(2,1)}, u32[]{:S(2)}, u32[]{:S(2)}) collective-permute-start(bf16[800,256]{1,0:T(8,128)(2,1)} %dynamic-slice_bitcast_fusion.4), channel_id=1, source_target_pairs={{0,2},{1,3},{2,0},{3,1},{4,6},{5,7},{6,4},{7,5},{8,10},{9,11},{10,... | collective-permute-start | bytes 1228808 | tf_op jit(solution)/shard_map/ppermute | solution.py:292
  51.0 4.6 %all-to-all-done.1 = bf16[8,16,256]{2,1,0:T(8,128)(2,1)S(1)} async-done(((bf16[8,16,256]{2,1,0:T(8,128)(2,1)}), bf16[8,16,256]{2,1,0:T(8,128)(2,1)S(1)}, u32[]{:S(2)}, u32[]{:S(2)}) %all-to-all-start.1) | async-done | bytes 65568 | tf_op jit(solution)/shard_map/all_to_all | solution.py:51
  56.4 6.0 %all-to-all-start.2 = ((bf16[32,16,256]{2,1,0:T(8,128)(2,1)}), bf16[32,16,256]{2,1,0:T(8,128)(2,1)S(1)}, u32[]{:S(2)}, u32[]{:S(2)}) async-start(bf16[32,16,256]{2,1,0:T(8,128)(2,1)} %broadcast_in_dim.44), calls=%async_computation.2 | async-start | bytes 524288 | tf_op jit(solution)/shard_map/all_to_all | solution.py:51
  62.5 8.8 %all-to-all-done.2.points_ref = bf16[32,16,256]{2,1,0:T(8,128)(2,1)S(1)} async-done(((bf16[32,16,256]{2,1,0:T(8,128)(2,1)}), bf16[32,16,256]{2,1,0:T(8,128)(2,1)S(1)}, u32[]{:S(2)}, u32[]{:S(2)}) %all-to-all-start.2) | async-done | bytes 262176 | tf_op jit(solution)/shard_map/all_to_all | solution.py:51
  71.3 5.0 %shard_map.73 = (bf16[2016,128]{1,0:T(8,128)(2,1)S(1)}, bf16[2016,128]{1,0:T(8,128)(2,1)S(1)}) custom-call(s32[3]{0:T(128)S(1)} %pad_add_fusion.rank_ref, bf16[32,16,256]{2,1,0:T(8,128)(2,1)S(1)} %all-to-all-done.2.points_ref, bf16[2000,256]{1,0:T(8,128)(2,1)S(1)} %get-tuple-element.29.own, bf16[2000,256]{1,0:T(8,128)(2,1)S(1)} %collective-permute-done.left, ...), custom_call_target="tpu_custom_call" | custom-call | flops 2000000000 | bytes 8716288 | tf_op jit(solution)/shard_map/pallas_call | solution.py:79
  76.3 2.8 %collective-permute-start.4 = (bf16[2016,128]{1,0:T(8,128)(2,1)S(1)}, bf16[2016,128]{1,0:T(8,128)(2,1)S(1)}, u32[]{:S(2)}, u32[]{:S(2)}) collective-permute-start(bf16[2016,128]{1,0:T(8,128)(2,1)S(1)} %get-tuple-element.21), channel_id=1, source_target_pairs={{0,256},{64,320},{128,384},{192,448},{256,4},{320,68},{384,132},{4... | collective-permute-start | bytes 1548296 | tf_op jit(solution)/shard_map/ppermute | solution.py:320
  79.1 14.3 %collective-permute-start.5 = (bf16[2016,128]{1,0:T(8,128)(2,1)S(1)}, bf16[2016,128]{1,0:T(8,128)(2,1)S(1)}, u32[]{:S(2)}, u32[]{:S(2)}) collective-permute-start(bf16[2016,128]{1,0:T(8,128)(2,1)S(1)} %get-tuple-element.22), channel_id=1, source_target_pairs={{0,260},{64,324},{128,388},{192,452},{256,0},{320,64},{384,128},{4... | collective-permute-start | bytes 1548296 | tf_op jit(solution)/shard_map/ppermute | solution.py:321
  94.3 10.3 %collective-permute-start.6 = (f32[64,128]{1,0:T(8,128)S(1)}, f32[64,128]{1,0:T(8,128)S(1)}, u32[]{:S(2)}, u32[]{:S(2)}) collective-permute-start(f32[64,128]{1,0:T(8,128)S(1)} %get-tuple-element.25), channel_id=1, source_target_pairs={{0,4},{4,0},{1,5},{5,1},{2,6},{6,2},{3,7},{7,3},{8,12},{12,8},{9,1... | collective-permute-start | bytes 98312 | tf_op jit(solution)/shard_map/ppermute | solution.py:309
  104.5 33.7 %collective-permute-done.4.below_ref = bf16[2016,128]{1,0:T(8,128)(2,1)S(1)} collective-permute-done((bf16[2016,128]{1,0:T(8,128)(2,1)S(1)}, bf16[2016,128]{1,0:T(8,128)(2,1)S(1)}, u32[]{:S(2)}, u32[]{:S(2)}) %collective-permute-start.4) | collective-permute-done | bytes 516128 | tf_op jit(solution)/shard_map/ppermute | solution.py:320
  138.2 6.2 %collective-permute-done.5.above_ref = bf16[2016,128]{1,0:T(8,128)(2,1)S(1)} collective-permute-done((bf16[2016,128]{1,0:T(8,128)(2,1)S(1)}, bf16[2016,128]{1,0:T(8,128)(2,1)S(1)}, u32[]{:S(2)}, u32[]{:S(2)}) %collective-permute-start.5) | collective-permute-done | bytes 516128 | tf_op jit(solution)/shard_map/ppermute | solution.py:321
  144.4 2.9 %shard_map.74 = f32[1280,128]{1,0:T(8,128)} custom-call(bf16[2016,128]{1,0:T(8,128)(2,1)S(1)} %collective-permute-done.4.below_ref, bf16[2016,128]{1,0:T(8,128)(2,1)S(1)} %collective-permute-done.5.above_ref, bf16[160,80]{1,0:T(8,128)(2,1)S(1)} %copy-done.2), custom_call_target="tpu_custom_call" | custom-call | flops 2000000000 | bytes 2115584 | tf_op jit(solution)/shard_map/pallas_call | solution.py:79
  147.3 4.4 %all-to-all-start.3 = ((f32[16,80,128]{2,1,0:T(8,128)}), f32[16,80,128]{2,1,0:T(8,128)S(1)}, u32[]{:S(2)}, u32[]{:S(2)}) async-start(f32[16,80,128]{2,1,0:T(8,128)} %bitcast.19), calls=%async_computation.3 | async-start | bytes 1310720 | tf_op jit(solution)/shard_map/all_to_all | solution.py:51
  151.8 5.6 %shard_map.76.inverse_ref = f32[128,128]{1,0:T(8,128)S(1)} custom-call(f32[64,128]{1,0:T(8,128)S(1)} %get-tuple-element.27.mine_ref, f32[64,128]{1,0:T(8,128)S(1)} %collective-permute-done.6.other_ref), custom_call_target="tpu_custom_call" | custom-call | flops 2000000000 | bytes 65536 | tf_op jit(solution)/shard_map/pallas_call | solution.py:79
  157.3 5.8 %all-to-all-done.3.in_ref = f32[16,80,128]{2,1,0:T(8,128)S(1)} async-done(((f32[16,80,128]{2,1,0:T(8,128)}), f32[16,80,128]{2,1,0:T(8,128)S(1)}, u32[]{:S(2)}, u32[]{:S(2)}) %all-to-all-start.3) | async-done | bytes 655392 | tf_op jit(solution)/shard_map/all_to_all | solution.py:51
  163.2 3.4 %shard_map.77 = bf16[1280,128]{1,0:T(8,128)(2,1)} custom-call(f32[16,80,128]{2,1,0:T(8,128)S(1)} %all-to-all-done.3.in_ref, bf16[1600,256]{1,0:T(8,128)(2,1)S(1)} %copy-done.1, f32[128,128]{1,0:T(8,128)S(1)} %shard_map.76.inverse_ref), custom_call_target="tpu_custom_call" | custom-call | flops 2000000000 | bytes 2359296 | tf_op jit(solution)/shard_map/pallas_call | solution.py:79
  166.5 9.4 %all-to-all-start.4 = ((bf16[32,40,128]{2,1,0:T(8,128)(2,1)}), bf16[32,40,128]{2,1,0:T(8,128)(2,1)S(1)}, u32[]{:S(2)}, u32[]{:S(2)}) async-start(bf16[32,40,128]{2,1,0:T(8,128)(2,1)} %bitcast.20), calls=%async_computation.4 | async-start | bytes 655360 | tf_op jit(solution)/shard_map/all_to_all | solution.py:51
  176.6 20.7 %all-to-all-done.4.got_ref = bf16[32,40,128]{2,1,0:T(8,128)(2,1)S(1)} async-done(((bf16[32,40,128]{2,1,0:T(8,128)(2,1)}), bf16[32,40,128]{2,1,0:T(8,128)(2,1)S(1)}, u32[]{:S(2)}, u32[]{:S(2)}) %all-to-all-start.4) | async-done | bytes 327712 | tf_op jit(solution)/shard_map/all_to_all | solution.py:51
  197.3 1.9 shard_map.78
  199.4 16.2 %all_to_all.35 = f32[32,1,1024]{2,1,0:T(1,128)S(1)} all-to-all(f32[32,1,1024]{2,1,0:T(1,128)S(1)} %reshape.272), channel_id=1, replica_groups=mesh['zl'=8,'yh'=2,'yl'=2,'c'=2,'zh'=2,'x'=4] {'yh','yl','c','x'}, dimensions={0} | all-to-all | bytes 262144 | tf_op jit(solution)/shard_map/all_to_all | solution.py:51
  217.4 13.9 %all_to_all.36 = f32[16,1,512]{2,1,0:T(1,128)S(1)} all-to-all(f32[16,1,512]{2,1,0:T(1,128)S(1)} %reshape.274), channel_id=1, replica_groups=mesh['zl'=8,'yh'=2,'yl'=2,'c'=2,'zh'=2,'x'=4] {'zl','zh'}, dimensions={0} | all-to-all | bytes 65536 | tf_op jit(solution)/shard_map/all_to_all | solution.py:51
  (53 shorter events, 7.4 us)
Async XLA Ops:
  2.6 5.7 %copy-start.3 = (bf16[80,100,256]{2,0,1:T(8,128)(2,1)}, bf16[80,100,256]{2,0,1:T(8,128)(2,1)S(1)}, u32[]{:S(2)}) copy-start(bf16[80,100,256]{2,0,1:T(8,128)(2,1)S(1)} %pad_maximum_fusion) | copy-start | bytes 12288004
  2.6 14.4 %copy-start.4 = (s32[2,64]{1,0:T(2,128)S(1)}, s32[2,64]{1,0:T(2,128)}, u32[]{:S(2)}) copy-start(s32[2,64]{1,0:T(2,128)} %param.10) | copy-start | bytes 1540
  2.7 14.5 %copy-start.5 = (s32[128]{0:T(128)S(1)}, s32[128]{0:T(128)}, u32[]{:S(2)}) copy-start(s32[128]{0:T(128)} %param.9) | copy-start | bytes 1540
  4.3 51.3 %collective-permute-start = (bf16[2000,256]{1,0:T(8,128)(2,1)}, bf16[2000,256]{1,0:T(8,128)(2,1)S(1)}, u32[]{:S(2)}, u32[]{:S(2)}) collective-permute-start(bf16[2000,256]{1,0:T(8,128)(2,1)} %get-tuple-element.31), channel_id=1, source_target_pairs={{0,1},{1,2},{2,3},{3,0},{4,5},{5,6},{6,7},{7,4},{8,9},{9,10},{10,1... | collective-permute-start | bytes 3072008 | tf_op jit(solution)/shard_map/ppermute | solution.py:292
  8.3 47.4 %collective-permute-start.1 = (bf16[2000,256]{1,0:T(8,128)(2,1)}, bf16[2000,256]{1,0:T(8,128)(2,1)S(1)}, u32[]{:S(2)}, u32[]{:S(2)}) collective-permute-start(bf16[2000,256]{1,0:T(8,128)(2,1)} %get-tuple-element.30), channel_id=1, source_target_pairs={{0,3},{1,0},{2,1},{3,2},{4,7},{5,4},{6,5},{7,6},{8,11},{9,8},{10,9... | collective-permute-start | bytes 3072008 | tf_op jit(solution)/shard_map/ppermute | solution.py:292
  13.5 42.2 %collective-permute-start.2 = (bf16[1200,256]{1,0:T(8,128)(2,1)}, bf16[1200,256]{1,0:T(8,128)(2,1)}, u32[]{:S(2)}, u32[]{:S(2)}) collective-permute-start(bf16[1200,256]{1,0:T(8,128)(2,1)} %dynamic-slice_bitcast_fusion.3), channel_id=1, source_target_pairs={{0,2},{1,3},{2,0},{3,1},{4,6},{5,7},{6,4},{7,5},{8,10},{9,11},{10,... | collective-permute-start | bytes 1843208 | tf_op jit(solution)/shard_map/ppermute | solution.py:292
  22.2 13.6 %all-to-all-start = ((bf16[8,16,256]{2,1,0:T(8,128)(2,1)}), bf16[8,16,256]{2,1,0:T(8,128)(2,1)S(1)}, u32[]{:S(2)}, u32[]{:S(2)}) async-start(bf16[8,16,256]{2,1,0:T(8,128)(2,1)} %maximum_select_fusion), calls=%async_computation | async-start | bytes 131072 | tf_op jit(solution)/shard_map/all_to_all | solution.py:51
  36.4 19.2 %all-to-all-start.1 = ((bf16[8,16,256]{2,1,0:T(8,128)(2,1)}), bf16[8,16,256]{2,1,0:T(8,128)(2,1)S(1)}, u32[]{:S(2)}, u32[]{:S(2)}) async-start(bf16[8,16,256]{2,1,0:T(8,128)(2,1)} %broadcast_in_dim.43), calls=%async_computation.1 | async-start | bytes 131072 | tf_op jit(solution)/shard_map/all_to_all | solution.py:51
  47.7 14.8 %collective-permute-start.3 = (bf16[800,256]{1,0:T(8,128)(2,1)}, bf16[800,256]{1,0:T(8,128)(2,1)}, u32[]{:S(2)}, u32[]{:S(2)}) collective-permute-start(bf16[800,256]{1,0:T(8,128)(2,1)} %dynamic-slice_bitcast_fusion.4), channel_id=1, source_target_pairs={{0,2},{1,3},{2,0},{3,1},{4,6},{5,7},{6,4},{7,5},{8,10},{9,11},{10,... | collective-permute-start | bytes 1228808 | tf_op jit(solution)/shard_map/ppermute | solution.py:292
  56.4 14.9 %all-to-all-start.2 = ((bf16[32,16,256]{2,1,0:T(8,128)(2,1)}), bf16[32,16,256]{2,1,0:T(8,128)(2,1)S(1)}, u32[]{:S(2)}, u32[]{:S(2)}) async-start(bf16[32,16,256]{2,1,0:T(8,128)(2,1)} %broadcast_in_dim.44), calls=%async_computation.2 | async-start | bytes 524288 | tf_op jit(solution)/shard_map/all_to_all | solution.py:51
  76.2 68.2 %copy-start.2 = (bf16[160,80]{1,0:T(8,128)(2,1)S(1)}, bf16[160,80]{1,0:T(8,128)(2,1)}, u32[]{:S(2)}) copy-start(bf16[160,80]{1,0:T(8,128)(2,1)} %constant.146.clone.basis_ref) | copy-start | bytes 76804
  76.3 62.0 %collective-permute-start.4 = (bf16[2016,128]{1,0:T(8,128)(2,1)S(1)}, bf16[2016,128]{1,0:T(8,128)(2,1)S(1)}, u32[]{:S(2)}, u32[]{:S(2)}) collective-permute-start(bf16[2016,128]{1,0:T(8,128)(2,1)S(1)} %get-tuple-element.21), channel_id=1, source_target_pairs={{0,256},{64,320},{128,384},{192,448},{256,4},{320,68},{384,132},{4... | collective-permute-start | bytes 1548296 | tf_op jit(solution)/shard_map/ppermute | solution.py:320
  79.1 65.4 %collective-permute-start.5 = (bf16[2016,128]{1,0:T(8,128)(2,1)S(1)}, bf16[2016,128]{1,0:T(8,128)(2,1)S(1)}, u32[]{:S(2)}, u32[]{:S(2)}) collective-permute-start(bf16[2016,128]{1,0:T(8,128)(2,1)S(1)} %get-tuple-element.22), channel_id=1, source_target_pairs={{0,260},{64,324},{128,388},{192,452},{256,0},{320,64},{384,128},{4... | collective-permute-start | bytes 1548296 | tf_op jit(solution)/shard_map/ppermute | solution.py:321
  94.3 53.1 %collective-permute-start.6 = (f32[64,128]{1,0:T(8,128)S(1)}, f32[64,128]{1,0:T(8,128)S(1)}, u32[]{:S(2)}, u32[]{:S(2)}) collective-permute-start(f32[64,128]{1,0:T(8,128)S(1)} %get-tuple-element.25), channel_id=1, source_target_pairs={{0,4},{4,0},{1,5},{5,1},{2,6},{6,2},{3,7},{7,3},{8,12},{12,8},{9,1... | collective-permute-start | bytes 98312 | tf_op jit(solution)/shard_map/ppermute | solution.py:309
  147.3 15.8 %copy-start.1 = (bf16[1600,256]{1,0:T(8,128)(2,1)S(1)}, bf16[1600,256]{1,0:T(8,128)(2,1)}, u32[]{:S(2)}) copy-start(bf16[1600,256]{1,0:T(8,128)(2,1)} %constant.147.clone.table_ref) | copy-start | bytes 2457604
  147.3 15.8 %all-to-all-start.3 = ((f32[16,80,128]{2,1,0:T(8,128)}), f32[16,80,128]{2,1,0:T(8,128)S(1)}, u32[]{:S(2)}, u32[]{:S(2)}) async-start(f32[16,80,128]{2,1,0:T(8,128)} %bitcast.19), calls=%async_computation.3 | async-start | bytes 1310720 | tf_op jit(solution)/shard_map/all_to_all | solution.py:51
  157.3 40.0 %copy-start = (bf16[1120,640]{1,0:T(8,128)(2,1)S(1)}, bf16[1120,640]{1,0:T(8,128)(2,1)}, u32[]{:S(2)}) copy-start(bf16[1120,640]{1,0:T(8,128)(2,1)} %constant.148.clone.table_ref) | copy-start | bytes 4300804
  166.5 30.8 %all-to-all-start.4 = ((bf16[32,40,128]{2,1,0:T(8,128)(2,1)}), bf16[32,40,128]{2,1,0:T(8,128)(2,1)S(1)}, u32[]{:S(2)}, u32[]{:S(2)}) async-start(bf16[32,40,128]{2,1,0:T(8,128)(2,1)} %bitcast.20), calls=%async_computation.4 | async-start | bytes 655360 | tf_op jit(solution)/shard_map/all_to_all | solution.py:51

commit v4 on v3

--- a/solution.py
+++ b/solution.py
@@ -21,8 +21,8 @@
 LEVELS = 252.9
 SPAN = 5.21
 SHIFTS = (0, 1, 3, 2)
-TILE = 400
-CELLS = 2000
+ROWS_A = 1280
+ROWS_B = 720
 FOUR_PI = 4.0 * math.pi
 TWO_PI = 2.0 * math.pi
 
@@ -72,7 +72,7 @@
     return jnp.where(code < 0, -value, value)
 
 
-def whole_call(kernel, out_shape, scratch, scalars, *arrays):
+def whole_call(kernel, out_shape, scratch, scalars, *arrays, flops=2 * 10**9):
     vmem = pl.BlockSpec(memory_space=pltpu.VMEM)
     shapes = [a.shape for a in arrays]
     moved = sum(math.prod(shape) * 4 for shape in shapes)
@@ -83,7 +83,7 @@
         out_specs=jax.tree.map(lambda _: vmem, out_shape),
         scratch_shapes=scratch,
         compiler_params=pltpu.CompilerParams(vmem_limit_bytes=40 * 2**20),
-        cost_estimate=pl.CostEstimate(flops=2 * 10**9, bytes_accessed=moved, transcendentals=0),
+        cost_estimate=pl.CostEstimate(flops=flops, bytes_accessed=moved, transcendentals=0),
     )(*scalars, *arrays)
 
 
@@ -120,55 +120,55 @@
     return lax.dot_general(left, right, (((1,), (0,)), ((), ())), preferred_element_type=F32)
 
 
+def dot_three(left, right):
+    (left, left_rest), (right, right_rest) = split(left), split(right)
+    return dot(left, right) + (dot(left, right_rest) + dot(left_rest, right))
+
+
 def two_parts(table):
     high = table.astype(ml_dtypes.bfloat16)
     low = (table - high.astype(np.float32)).astype(ml_dtypes.bfloat16)
     return jnp.asarray(np.concatenate([high, low], axis=0))
 
 
-def cell_tiles(blocks):
-    own, left, right, far_low, far_high = blocks
-    for tile in range(5):
-        rows = pl.ds(tile * TILE, TILE)
-        far = far_low[rows, :] if tile < 3 else far_high[pl.ds((tile - 3) * TILE, TILE), :]
-        yield rows, (own[rows, :], left[rows, :], right[rows, :], far)
-
-
-def sums_kernel(rank_ref, points_ref, own, left, right, far_low, far_high, up_ref, down_ref, sum_ref):
-    half = rank_ref[1]
+def sums_kernel(rank_ref, points_ref, own, left, right, far, one_ref, two_ref, sum_ref):
+    panel_one = rank_ref[1]
+    count = own.shape[0]
     tables = []
     for shift in SHIFTS:
-        heads = [head_rows(points_ref, shift, rank_ref[0], panel) for panel in (half, 1 - half)]
+        heads = [head_rows(points_ref, shift, rank_ref[0], panel) for panel in (panel_one, 1 - panel_one)]
         tables.append(jnp.concatenate([side_table(head) for head in heads], axis=0))
+    tile = 320 if count == ROWS_A else 240
+    tiles = [pl.ds(low, tile) for low in range(0, count, tile)]
     square = jnp.zeros((1, 4 * PANEL), F32)
-    for rows, parts in cell_tiles((own, left, right, far_low, far_high)):
-        total = sum(dot_rows(part, table) for part, table in zip(parts, tables))
+    for rows in tiles:
+        total = sum(dot_rows(block[rows, :], table) for block, table in zip((own, left, right, far), tables))
         sum_ref[rows, :] = total
         square = square + jnp.sum(total * total, axis=0, keepdims=True)
-    power = lane_power(square, CELLS)
-    for out_ref, low in ((up_ref, 0), (down_ref, 2 * PANEL)):
+    power = lane_power(square, count)
+    for out_ref, low in ((one_ref, 0), (two_ref, 2 * PANEL)):
         lanes = pl.ds(low, 2 * PANEL)
         own_power = power[:, low : low + 2 * PANEL]
-        for tile in range(5):
-            rows = pl.ds(tile * TILE, TILE)
+        for rows in tiles:
             out_ref[rows, :] = encode(sum_ref[rows, lanes], own_power).astype(BF16)
-        out_ref[pl.ds(CELLS, 16), :] = jnp.broadcast_to(own_power, (16, 2 * PANEL)).astype(BF16)
-
-
-def gram_kernel(rank_ref, points_ref, gram_ref, other_ref):
-    for out_ref, panel in ((gram_ref, rank_ref[2]), (other_ref, 1 - rank_ref[2])):
+        out_ref[pl.ds(count, 16), :] = jnp.broadcast_to(own_power, (16, 2 * PANEL)).astype(BF16)
+
+
+def gram_kernel(rank_ref, points_ref, gram_ref):
+    for panel in range(2):
         heads = [head_rows(points_ref, shift, rank_ref[0], panel) for shift in SHIFTS]
-        out_ref[...] = sum(dot_rows(head, side_table(head)) for head in heads)
-
-
-def first_kernel(below_ref, above_ref, basis_ref, out_ref):
-    powers = [ref[pl.ds(CELLS, 16), :].astype(F32)[:1] for ref in (below_ref, above_ref)]
+        gram_ref[pl.ds(panel * PANEL, PANEL), :] = sum(dot_rows(head, side_table(head)) for head in heads)
+
+
+def first_kernel(below_a, above_a, below_b, above_b, basis_ref, out_ref):
     left_lanes = lax.broadcasted_iota(jnp.int32, (N, 2 * PANEL), 1) < PANEL
     out_ref[...] = jnp.zeros_like(out_ref)
 
     def product(column):
-        rows = pl.ds(column * N, N)
-        sums = decode(below_ref[rows, :].astype(F32), powers[0]) + decode(above_ref[rows, :].astype(F32), powers[1])
+        refs, count = ((below_a, above_a), ROWS_A) if column < ROWS_A // N else ((below_b, above_b), ROWS_B)
+        rows = pl.ds(column * N % ROWS_A, N)
+        parts = [decode(ref[rows, :].astype(F32), ref[pl.ds(count, 16), :].astype(F32)[:1]) for ref in refs]
+        sums = parts[0] + parts[1]
         return sums * pltpu.roll(sums, PANEL, 1)
 
     pairs = []
@@ -182,33 +182,37 @@
             out_ref[pl.ds(k * 16 + pair, 16, stride=80), :] = rows
 
 
-def inverse_kernel(mine_ref, other_ref, out_ref):
+def inverse_kernel(mine_ref, other_ref, fit_ref, bra_ref):
     sums = mine_ref[...] + other_ref[...]
-    matrix = sums * pltpu.roll(sums, PANEL, 1)
+    both = sums * pltpu.roll(sums, PANEL, 1)
     lane = lax.broadcasted_iota(jnp.int32, (PANEL, 2 * PANEL), 1)
     line = lax.broadcasted_iota(jnp.int32, (PANEL, 2 * PANEL), 0)
+    left = lane < PANEL
+    matrix = jnp.where(left, both[:PANEL], both[PANEL:])
     for step in range(PANEL):
-        scale = 1.0 / matrix[step : step + 1, step : step + 1]
-        row = jnp.where(lane[:1] == step, 1.0, matrix[step : step + 1]) * scale
-        column = matrix[:, step : step + 1]
-        rest = jnp.where(lane == step, 0.0, matrix) - column * row
+        far = PANEL + step
+        here = (lane == step) | (lane == far)
+        row = matrix[step : step + 1]
+        pivot = jnp.where(left[:1], row[:, step : step + 1], row[:, far : far + 1])
+        row = jnp.where(here[:1], 1.0, row) / pivot
+        column = jnp.where(left, matrix[:, step : step + 1], matrix[:, far : far + 1])
+        rest = jnp.where(here, 0.0, matrix) - column * row
         matrix = jnp.where(line == step, row, rest)
-    out_ref[pl.ds(0, PANEL), :] = jnp.where(lane < PANEL, matrix, 0.0)
-    out_ref[pl.ds(PANEL, PANEL), :] = jnp.where(lane < PANEL, 0.0, pltpu.roll(matrix, PANEL, 1))
-
-
-def second_kernel(in_ref, table_ref, inverse_ref, out_ref, line_ref, code_ref):
+    other = pltpu.roll(matrix, PANEL, 1)
+    fit_ref[...] = jnp.where(left, matrix, other)
+    bra_ref[...] = jnp.where(left, other, matrix)
+
+
+def second_kernel(in_ref, table_ref, out_ref, line_ref, code_ref):
     left_lanes = lax.broadcasted_iota(jnp.int32, (200, 2 * PANEL), 1) < PANEL
     data = [in_ref[:, pl.ds(k * 16, 16), :].reshape(256, 2 * PANEL) for k in range(5)]
     moved = dot_two(table_ref, jnp.concatenate(data, axis=1))
-    inverse = split(inverse_ref[...])
     square = jnp.zeros((1, 2 * PANEL), F32)
     for k in range(5):
         part = moved[:, k * 2 * PANEL : (k + 1) * 2 * PANEL]
         low = part[:200] + pltpu.roll(part[200:400], PANEL, 1)
         high = pltpu.roll(part[400:600], PANEL, 1) + part[600:]
-        top, rest = split(jnp.where(left_lanes, low, high))
-        mixed = dot(top, inverse[0]) + (dot(top, inverse[1]) + dot(rest, inverse[0]))
+        mixed = jnp.where(left_lanes, low, high)
         line_ref[pl.ds(k * 200, 200), :] = mixed
         square = square + jnp.sum(mixed * mixed, axis=0, keepdims=True)
     power = lane_power(square, 1000)
@@ -224,7 +228,7 @@
         out_ref[rows, :] = code_ref[rows, :].astype(BF16)
 
 
-def third_kernel(got_ref, table_ref, kernel_ref, out_ref):
+def third_kernel(got_ref, table_ref, kernel_ref, fit_ref, bra_ref, out_ref):
     keep = lax.broadcasted_iota(jnp.int32, (40, 2 * PANEL), 0) < 35
 
     def side(panel):
@@ -242,7 +246,14 @@
         return lax.dot_general(left, right, (((0,), (0,)), ((), ())), preferred_element_type=F32)
 
     total = meet(bra_top, fit_top) + (meet(bra_top, fit_rest) + meet(bra_rest, fit_top))
-    out_ref[...] = total[:PANEL, :PANEL] + total[PANEL:, PANEL:]
+    total = total + pltpu.roll(pltpu.roll(total, PANEL, 0), PANEL, 1)
+    total = dot_three(bra_ref[...][:, :PANEL], total[:PANEL, :PANEL])
+    total = dot_three(total, fit_ref[...])
+    left_lanes = lax.broadcasted_iota(jnp.int32, (8, 2 * PANEL), 1) < PANEL
+    for to in range(4):
+        rows = jnp.where(left_lanes, total[8 * to : 8 * to + 8], total[32 + 8 * to : 40 + 8 * to])
+        for row in range(8):
+            out_ref[row * 4 + to] = rows
 
 
 def second_table():
@@ -291,19 +302,20 @@
     def spread(block, shift):
         return lax.ppermute(block, "x", [(i, (i + shift) % 4) for i in range(4)])
 
-    far = take(2)
-    split = 3 * TILE
-    own, left, right = take(0), spread(take(1), 1), spread(take(3), 3)
-    far_low = spread(far[:split], 2)
+    whole = [take(shift) for shift in SHIFTS]
+    first = [block[:ROWS_A] for block in whole]
+    second = [block[ROWS_A:] for block in whole]
+    first = first[:1] + [spread(block, shift) for block, shift in zip(first[1:], SHIFTS[1:])]
 
     def add(values):
         return jnp.sum(values.astype(F32), axis=0).astype(BF16)
 
     rows = add(swap(here.reshape(8, 16, 2 * width), ROWS))
     rows = add(swap(jnp.broadcast_to(rows[None], (8, 16, 2 * width)), "zl"))
-    rows, left, right, far_low = lax.optimization_barrier((rows, left, right, far_low))
-    far_high = spread(far[split:], 2)
+    rows, first = lax.optimization_barrier((rows, first))
     pts = swap(jnp.broadcast_to(rows[None], (32, 16, 2 * width)), ROWS + ("x",))
+    pts, second = lax.optimization_barrier((pts, second))
+    second = second[:1] + [spread(block, shift) for block, shift in zip(second[1:], SHIFTS[1:])]
 
     def cross(values):
         return lax.ppermute(values, "zh", [(0, 1), (1, 0)])
@@ -311,25 +323,36 @@
     def full(rows, dtype=F32, lanes=2 * PANEL):
         return jax.ShapeDtypeStruct((rows, lanes), dtype)
 
-    panel = ((lax.axis_index("zl") >= 4) == (zh_rank == 1)).astype(jnp.int32)
-    ranks = jnp.stack([x_rank, zh_rank, panel]).astype(jnp.int32)
-    blocks = (own, left, right, far_low, far_high)
-    outs = (full(CELLS + 16, BF16), full(CELLS + 16, BF16))
-    up, down = whole_call(sums_kernel, outs, [pltpu.VMEM((CELLS, 4 * PANEL), F32)], (ranks,), pts, *blocks)
-    ring = [(z % 8) * 2 + z // 8 for z in range(16)]
-    below = lax.ppermute(up, ("zl", "zh"), [(ring[z], ring[(z + 4) % 16]) for z in range(16)])
-    above = lax.ppermute(down, ("zl", "zh"), [(ring[z], ring[(z + 12) % 16]) for z in range(16)])
-    pts, up = lax.optimization_barrier((pts, up))
-    gram, other_gram = whole_call(gram_kernel, (full(PANEL), full(PANEL)), [], (ranks,), pts)
-    other_gram = cross(other_gram)
+    ranks = jnp.stack([x_rank, (zh_rank + lax.axis_index("c")) % 2]).astype(jnp.int32)
+
+    def hops(core_zero):
+        pairs = []
+        for z in range(16):
+            for core, step in ((0, core_zero), (1, 16 - core_zero)):
+                to = (z + step) % 16
+                pairs.append((((z % 8) * 2 + core) * 2 + z // 8, ((to % 8) * 2 + core) * 2 + to // 8))
+        return pairs
+
+    def half_sums(points, blocks):
+        count = blocks[0].shape[0]
+        outs = (full(count + 16, BF16), full(count + 16, BF16))
+        scratch = [pltpu.VMEM((count, 4 * PANEL), F32)]
+        one, two = whole_call(sums_kernel, outs, scratch, (ranks,), points, *blocks)
+        return one, lax.ppermute(one, ("zl", "c", "zh"), hops(4)), lax.ppermute(two, ("zl", "c", "zh"), hops(12))
+
+    one, *got_a = half_sums(pts, first)
+    _, *got_b = half_sums(pts, second)
+    pts, one = lax.optimization_barrier((pts, one))
+    gram = whole_call(gram_kernel, full(2 * PANEL), [], (ranks,), pts, flops=0)
+    other_gram = cross(gram)
 
     basis_a = real_basis().reshape(16, 5, N).transpose(1, 0, 2).reshape(N, N)
-    fields = whole_call(first_kernel, full(16 * 80), [], (), below, above, two_parts(basis_a))
-    fields, gram, other_gram = lax.optimization_barrier((fields, gram, other_gram))
-    inverse = whole_call(inverse_kernel, full(2 * PANEL), [], (), gram, other_gram)
+    fields = whole_call(first_kernel, full(16 * 80), [], (), *got_a, *got_b, two_parts(basis_a))
     fields = swap(fields.reshape(16, 80, 2 * PANEL), PLANE)
     scratch = [pltpu.VMEM((1120, 2 * PANEL), F32), pltpu.VMEM((1280, 2 * PANEL), F32)]
-    fields = whole_call(second_kernel, full(1280, BF16), scratch, (), fields, two_parts(second_table()), inverse)
+    fields = whole_call(second_kernel, full(1280, BF16), scratch, (), fields, two_parts(second_table()))
+    fields, gram, other_gram = lax.optimization_barrier((fields, gram, other_gram))
+    inverses = whole_call(inverse_kernel, (full(PANEL), full(PANEL)), [], (), gram, other_gram)
     fields = swap(fields.reshape(32, 40, 2 * PANEL), RING)
 
     slot = lax.axis_index(RING) * 7 + jnp.arange(7, dtype=jnp.int32)
@@ -340,12 +363,11 @@
     live = (squared > 0) & (slot < 200)[:, None, None]
     kernel = jnp.where(live, 32.0 * FOUR_PI / jnp.where(squared > 0, squared, 1.0), 0.0)
     kernel = jnp.broadcast_to(kernel[..., None], (7, N, 2, PANEL)).reshape(7 * N, 2 * PANEL)
-    part = whole_call(third_kernel, full(PANEL, F32, PANEL), [], (), fields, two_parts(third_table()), kernel)
-    part = part.reshape(2, 4, 8, PANEL).transpose(1, 0, 2, 3)
-    part = jnp.broadcast_to(part[None], (8, 4, 2, 8, PANEL)).reshape(32, 16, PANEL)
+    out_shape = jax.ShapeDtypeStruct((32, 8, 2 * PANEL), F32)
+    part = whole_call(third_kernel, out_shape, [], (), fields, two_parts(third_table()), kernel, *inverses)
     part = jnp.sum(swap(part, ROWS + ("x",)), axis=0)
-    part = jnp.broadcast_to(part.reshape(1, 2, 8, PANEL), (8, 2, 8, PANEL)).reshape(16, 8, PANEL)
-    return jnp.sum(swap(part, ("zl", "zh")), axis=0)
+    part = jnp.sum(swap(jnp.broadcast_to(part[None], (16, 8, 2 * PANEL)), ("zl", "zh")), axis=0)
+    return lax.dynamic_slice_in_dim(part, zh_rank * PANEL, PANEL, 1)
 
 
 def solution(mesh):

time: 234 us -> 227 us (0.970)
  blocking collectives: 30.2 us -> 50.6 us
  starting transfers between devices: 79.1 us -> 67.5 us
  waiting for transfers between devices: 85.1 us -> 73.9 us
  other arithmetic: 6.27 us -> 3.38 us
    all_to_all x2 -> x3, blocking collectives: 30.2 us -> 50.6 us  [swap(): return lax.all_to_all(values, axes, 0, 0, tiled=True)]
    all_to_all x5 -> x4, starting transfers between devices: 37.6 us -> 22.5 us  [swap(): return lax.all_to_all(values, axes, 0, 0, tiled=True)]
    all_to_all x5 -> x4, waiting for transfers between devices: 45.2 us -> 36.5 us  [swap(): return lax.all_to_all(values, axes, 0, 0, tiled=True)]
    ppermute x2 -> x4, waiting for transfers between devices: 39.9 us -> 32.6 us  [the longest x2 31.4 us: half_sums(): lax.ppermute(one, ('zl', 'c', 'zh'), hops(4))]
    ppermute x4 -> x6, starting transfers between devices: 14.1 us -> 19.2 us  [spread(): return lax.ppermute(block, 'x', [(i, (i + shift) % 4) for i in range(4)])]
    ppermute x1, waiting for transfers between devices: 0.01 us -> 4.82 us  [cross(): return lax.ppermute(values, 'zh', [(0, 1), (1, 0)])]
    ppermute x1, starting transfers between devices: 10.3 us -> 7.31 us  [cross(): return lax.ppermute(values, 'zh', [(0, 1), (1, 0)])]
    ppermute x2 -> x4, starting transfers between devices: 17.1 us -> 18.5 us  [the longest x2 12.4 us: half_sums(): lax.ppermute(two, ('zl', 'c', 'zh'), hops(12))]
  transfers between devices with their start and end apart: 12 -> 15, of which waited for: 7 -> 8; matrix products, arithmetic and copies ran while one was open for 5% -> 3% of each run, Pallas kernels for 4% -> 7%
where the time goes in v4:
time: 227 us; the launch traced here: 226 us
  waiting for transfers between devices  73.9 us (33%)
  starting transfers between devices  67.5 us (30%)
  blocking collectives  50.6 us (22%)
  Pallas kernels  20.1 us (9%)
  local copies, waits for them, and re-layouts  10.3 us (5%)
  other arithmetic  3.38 us (1%)
    all_to_all x3, blocking collectives, swap(): return lax.all_to_all(values, axes, 0, 0, tiled=True)  50.6 us
    all_to_all x4, waiting for transfers between devices, swap(): return lax.all_to_all(values, axes, 0, 0, tiled=True)  36.5 us
    ppermute x2, waiting for transfers between devices, half_sums(): lax.ppermute(one, ('zl', 'c', 'zh'), hops(4))  31.4 us
    all_to_all x4, starting transfers between devices, swap(): return lax.all_to_all(values, axes, 0, 0, tiled=True)  22.5 us
    pallas_call x7, Pallas kernels, whole_call(): pl.pallas_call(kernel, out_shape=out_shape, in_specs=[pl.BlockSpec(memory...  20.1 us
    ppermute x6, starting transfers between devices, spread(): return lax.ppermute(block, 'x', [(i, (i + shift) % 4) for i in range(4)])  19.2 us
    ppermute x2, starting transfers between devices, half_sums(): lax.ppermute(two, ('zl', 'c', 'zh'), hops(12))  12.4 us
    ppermute x1, starting transfers between devices, cross(): return lax.ppermute(values, 'zh', [(0, 1), (1, 0)])  7.31 us
  transfers between devices with their start and end apart: 15, of which 8 were waited for; matrix products, arithmetic and copies ran while one was open for 3% of the time, Pallas kernels for 7%

profile of v4, /device:TPU:1, one launch (start us, length us, event | category | flops | bytes accessed | tf_op | source)
XLA Modules:
  0.0 226.1 jit_solution(4408743222756264807)
XLA Ops:
  0.0 2.6 %pad_maximum_fusion = bf16[80,100,256]{2,0,1:T(8,128)(2,1)S(1)} fusion(bf16[80,100,128]{2,0,1:T(8,128)(2,1)} %param.8, bf16[80,100,128]{2,0,1:T(8,128)(2,1)} %param.7), kind=kLoop, calls=%fused_computation.2 | loop fusion | flops 8192000 | bytes 8192000 | tf_op jit(solution)/shard_map/concatenate | solution.py:287
  4.1 3.9 %collective-permute-start = (bf16[1280,256]{1,0:T(8,128)(2,1)}, bf16[1280,256]{1,0:T(8,128)(2,1)S(1)}, u32[]{:S(2)}, u32[]{:S(2)}) collective-permute-start(bf16[1280,256]{1,0:T(8,128)(2,1)} %get-tuple-element.51), channel_id=1, source_target_pairs={{0,1},{1,2},{2,3},{3,0},{4,5},{5,6},{6,7},{7,4},{8,9},{9,10},{10,1... | collective-permute-start | bytes 1966088 | tf_op jit(solution)/shard_map/ppermute | solution.py:303
  8.0 3.2 %collective-permute-start.1 = (bf16[1280,256]{1,0:T(8,128)(2,1)}, bf16[1280,256]{1,0:T(8,128)(2,1)S(1)}, u32[]{:S(2)}, u32[]{:S(2)}) collective-permute-start(bf16[1280,256]{1,0:T(8,128)(2,1)} %get-tuple-element.50), channel_id=1, source_target_pairs={{0,3},{1,0},{2,1},{3,2},{4,7},{5,4},{6,5},{7,6},{8,11},{9,8},{10,9... | collective-permute-start | bytes 1966088 | tf_op jit(solution)/shard_map/ppermute | solution.py:303
  11.2 3.6 %collective-permute-start.2 = (bf16[1280,256]{1,0:T(8,128)(2,1)S(1)}, bf16[1280,256]{1,0:T(8,128)(2,1)S(1)}, u32[]{:S(2)}, u32[]{:S(2)}) collective-permute-start(bf16[1280,256]{1,0:T(8,128)(2,1)S(1)} %get-tuple-element.49), channel_id=1, source_target_pairs={{0,2},{1,3},{2,0},{3,1},{4,6},{5,7},{6,4},{7,5},{8,10},{9,11},{10,... | collective-permute-start | bytes 1966088 | tf_op jit(solution)/shard_map/ppermute | solution.py:303
  19.3 12.6 %all_to_all.35 = bf16[8,16,256]{2,1,0:T(8,128)(2,1)S(1)} all-to-all(bf16[8,16,256]{2,1,0:T(8,128)(2,1)S(1)} %maximum_select_fusion), channel_id=1, replica_groups=mesh['zl'=8,'yh'=2,'yl'=2,'c'=2,'zh'=2,'x'=4] {'yh','yl','c'}, dimensions={0} | all-to-all | bytes 131072 | tf_op jit(solution)/shard_map/all_to_all | solution.py:51
  31.9 20.1 %all_to_all.36 = bf16[8,16,256]{2,1,0:T(8,128)(2,1)S(1)} all-to-all(bf16[8,16,256]{2,1,0:T(8,128)(2,1)S(1)} %broadcast_in_dim.39), channel_id=1, replica_groups=mesh['zl'=8,'yh'=2,'yl'=2,'c'=2,'zh'=2,'x'=4] {'zl'}, dimensions={0} | all-to-all | bytes 131072 | tf_op jit(solution)/shard_map/all_to_all | solution.py:51
  52.9 5.6 %all-to-all-start.2 = ((bf16[32,16,256]{2,1,0:T(8,128)(2,1)}), bf16[32,16,256]{2,1,0:T(8,128)(2,1)S(1)}, u32[]{:S(2)}, u32[]{:S(2)}) async-start(bf16[32,16,256]{2,1,0:T(8,128)(2,1)} %broadcast_in_dim.40), calls=%async_computation.2 | async-start | bytes 524288 | tf_op jit(solution)/shard_map/all_to_all | solution.py:51
  58.5 2.3 %dynamic-slice_bitcast_fusion.4 = (bf16[720,256]{1,0:T(8,128)(2,1)}, bf16[720,256]{1,0:T(8,128)(2,1)}, bf16[720,256]{1,0:T(8,128)(2,1)}, bf16[720,256]{1,0:T(8,128)(2,1)S(1)}) fusion(bf16[4,2000,256]{2,1,0:T(8,128)(2,1)} %bitcast.50, s32[]{:T(128)S(6)} %select_n.185, s32[]{:T(128)S(6)} %add.263, s32[]{:T(128)S(6)} %select_n.183, s32[]{:T(128)S(6)} %select_n.181, ...), kind=kLoop, calls=%fused_computation.7 | loop fusion | bytes 2949140 | tf_op jit(solution)/shard_map/slice | solution.py:307
  60.9 6.6 %all-to-all-done.2.points_ref = bf16[32,16,256]{2,1,0:T(8,128)(2,1)S(1)} async-done(((bf16[32,16,256]{2,1,0:T(8,128)(2,1)}), bf16[32,16,256]{2,1,0:T(8,128)(2,1)S(1)}, u32[]{:S(2)}, u32[]{:S(2)}) %all-to-all-start.2) | async-done | bytes 262176 | tf_op jit(solution)/shard_map/all_to_all | solution.py:51
  67.4 2.2 collective-permute-start.5
  69.6 4.3 %collective-permute-start.6 = (bf16[720,256]{1,0:T(8,128)(2,1)}, bf16[720,256]{1,0:T(8,128)(2,1)}, u32[]{:S(2)}, u32[]{:S(2)}) collective-permute-start(bf16[720,256]{1,0:T(8,128)(2,1)} %get-tuple-element.35), channel_id=1, source_target_pairs={{0,3},{1,0},{2,1},{3,2},{4,7},{5,4},{6,5},{7,6},{8,11},{9,8},{10,9... | collective-permute-start | bytes 1105928 | tf_op jit(solution)/shard_map/ppermute | solution.py:303
  75.9 3.0 %shard_map.73 = (bf16[1296,128]{1,0:T(8,128)(2,1)S(1)}, bf16[1296,128]{1,0:T(8,128)(2,1)S(1)}) custom-call(s32[2]{0:T(128)S(1)} %pad_add_fusion.rank_ref, bf16[32,16,256]{2,1,0:T(8,128)(2,1)S(1)} %all-to-all-done.2.points_ref, bf16[1280,256]{1,0:T(8,128)(2,1)S(1)} %get-tuple-element.27.own, bf16[1280,256]{1,0:T(8,128)(2,1)S(1)} %collective-permute-done.left, ...), custom_call_target="tpu_custom_call" | custom-call | flops 2000000000 | bytes 5767168 | tf_op jit(solution)/shard_map/pallas_call | solution.py:79
  79.0 3.0 %collective-permute-start.3 = (bf16[1296,128]{1,0:T(8,128)(2,1)S(1)}, bf16[1296,128]{1,0:T(8,128)(2,1)S(1)}, u32[]{:S(2)}, u32[]{:S(2)}) collective-permute-start(bf16[1296,128]{1,0:T(8,128)(2,1)S(1)} %get-tuple-element.31), channel_id=1, source_target_pairs={{0,256},{8,268},{64,320},{72,332},{128,384},{136,396},{192,448},{2... | collective-permute-start | bytes 995336 | tf_op jit(solution)/shard_map/ppermute | solution.py:341
  82.0 6.1 %collective-permute-start.4 = (bf16[1296,128]{1,0:T(8,128)(2,1)S(1)}, bf16[1296,128]{1,0:T(8,128)(2,1)S(1)}, u32[]{:S(2)}, u32[]{:S(2)}) collective-permute-start(bf16[1296,128]{1,0:T(8,128)(2,1)S(1)} %get-tuple-element.32), channel_id=1, source_target_pairs={{0,260},{8,264},{64,324},{72,328},{128,388},{136,392},{192,452},{2... | collective-permute-start | bytes 995336 | tf_op jit(solution)/shard_map/ppermute | solution.py:341
  88.2 2.7 %shard_map.74 = (bf16[736,128]{1,0:T(8,128)(2,1)S(1)}, bf16[736,128]{1,0:T(8,128)(2,1)S(1)}) custom-call(s32[2]{0:T(128)S(1)} %pad_add_fusion.rank_ref, bf16[32,16,256]{2,1,0:T(8,128)(2,1)S(1)} %all-to-all-done.2.points_ref, bf16[720,256]{1,0:T(8,128)(2,1)S(1)} %get-tuple-element.33.own, bf16[720,256]{1,0:T(8,128)(2,1)} %collective-permute-done.5.left, ...), custom_call_target="tpu_custom_call" | custom-call | flops 2000000000 | bytes 3473408 | tf_op jit(solution)/shard_map/pallas_call | solution.py:79
  90.9 3.0 %collective-permute-start.8 = (bf16[736,128]{1,0:T(8,128)(2,1)S(1)}, bf16[736,128]{1,0:T(8,128)(2,1)S(1)}, u32[]{:S(2)}, u32[]{:S(2)}) collective-permute-start(bf16[736,128]{1,0:T(8,128)(2,1)S(1)} %get-tuple-element.37), channel_id=1, source_target_pairs={{0,256},{8,268},{64,320},{72,332},{128,384},{136,396},{192,448},{2... | collective-permute-start | bytes 565256 | tf_op jit(solution)/shard_map/ppermute | solution.py:341
  94.0 6.3 %collective-permute-start.9 = (bf16[736,128]{1,0:T(8,128)(2,1)S(1)}, bf16[736,128]{1,0:T(8,128)(2,1)S(1)}, u32[]{:S(2)}, u32[]{:S(2)}) collective-permute-start(bf16[736,128]{1,0:T(8,128)(2,1)S(1)} %get-tuple-element.38), channel_id=1, source_target_pairs={{0,260},{8,264},{64,324},{72,328},{128,388},{136,392},{192,452},{2... | collective-permute-start | bytes 565256 | tf_op jit(solution)/shard_map/ppermute | solution.py:341
  100.2 26.8 %collective-permute-done.3.below_a = bf16[1296,128]{1,0:T(8,128)(2,1)S(1)} collective-permute-done((bf16[1296,128]{1,0:T(8,128)(2,1)S(1)}, bf16[1296,128]{1,0:T(8,128)(2,1)S(1)}, u32[]{:S(2)}, u32[]{:S(2)}) %collective-permute-start.3) | collective-permute-done | bytes 331808 | tf_op jit(solution)/shard_map/ppermute | solution.py:341
  127.0 4.6 %collective-permute-done.8.below_b = bf16[736,128]{1,0:T(8,128)(2,1)S(1)} collective-permute-done((bf16[736,128]{1,0:T(8,128)(2,1)S(1)}, bf16[736,128]{1,0:T(8,128)(2,1)S(1)}, u32[]{:S(2)}, u32[]{:S(2)}) %collective-permute-start.8) | collective-permute-done | bytes 188448 | tf_op jit(solution)/shard_map/ppermute | solution.py:341
  132.8 2.9 %shard_map.75 = f32[1280,128]{1,0:T(8,128)} custom-call(bf16[1296,128]{1,0:T(8,128)(2,1)S(1)} %collective-permute-done.3.below_a, bf16[1296,128]{1,0:T(8,128)(2,1)S(1)} %collective-permute-done.4.above_a, bf16[736,128]{1,0:T(8,128)(2,1)S(1)} %collective-permute-done.8.below_b, bf16[736,128]{1,0:T(8,128)(2,1)S(1)} %collective-permute-done.9.above_b, ...), custom_call_target="tpu_custom_call" | custom-call | flops 2000000000 | bytes 2131968 | tf_op jit(solution)/shard_map/pallas_call | solution.py:79
  135.7 4.7 %all-to-all-start.3 = ((f32[16,80,128]{2,1,0:T(8,128)}), f32[16,80,128]{2,1,0:T(8,128)S(1)}, u32[]{:S(2)}, u32[]{:S(2)}) async-start(f32[16,80,128]{2,1,0:T(8,128)} %bitcast.21), calls=%async_computation.3 | async-start | bytes 1310720 | tf_op jit(solution)/shard_map/all_to_all | solution.py:51
  141.3 7.3 %collective-permute-start.10 = (f32[128,128]{1,0:T(8,128)S(1)}, f32[128,128]{1,0:T(8,128)S(1)}, u32[]{:S(2)}, u32[]{:S(2)}) collective-permute-start(f32[128,128]{1,0:T(8,128)S(1)} %shard_map.77.mine_ref), channel_id=1, source_target_pairs={{0,4},{4,0},{1,5},{5,1},{2,6},{6,2},{3,7},{7,3},{8,12},{12,8},{9,1... | collective-permute-start | bytes 196616 | tf_op jit(solution)/shard_map/ppermute | solution.py:321
  148.6 3.2 %all-to-all-done.3.in_ref = f32[16,80,128]{2,1,0:T(8,128)S(1)} async-done(((f32[16,80,128]{2,1,0:T(8,128)}), f32[16,80,128]{2,1,0:T(8,128)S(1)}, u32[]{:S(2)}, u32[]{:S(2)}) %all-to-all-start.3) | async-done | bytes 655392 | tf_op jit(solution)/shard_map/all_to_all | solution.py:51
  151.8 2.5 %shard_map.76 = bf16[1280,128]{1,0:T(8,128)(2,1)} custom-call(f32[16,80,128]{2,1,0:T(8,128)S(1)} %all-to-all-done.3.in_ref, bf16[1600,256]{1,0:T(8,128)(2,1)S(1)} %copy-done.1), custom_call_target="tpu_custom_call" | custom-call | flops 2000000000 | bytes 2293760 | tf_op jit(solution)/shard_map/pallas_call | solution.py:79
  154.4 4.8 %collective-permute-done.10.other_ref = f32[128,128]{1,0:T(8,128)S(1)} collective-permute-done((f32[128,128]{1,0:T(8,128)S(1)}, f32[128,128]{1,0:T(8,128)S(1)}, u32[]{:S(2)}, u32[]{:S(2)}) %collective-permute-start.10) | collective-permute-done | bytes 65568 | tf_op jit(solution)/shard_map/ppermute | solution.py:321
  159.2 8.6 %all-to-all-start.4 = ((bf16[32,40,128]{2,1,0:T(8,128)(2,1)}), bf16[32,40,128]{2,1,0:T(8,128)(2,1)S(1)}, u32[]{:S(2)}, u32[]{:S(2)}) async-start(bf16[32,40,128]{2,1,0:T(8,128)(2,1)} %bitcast.22), calls=%async_computation.4 | async-start | bytes 655360 | tf_op jit(solution)/shard_map/all_to_all | solution.py:51
  168.5 6.0 %shard_map.78 = (f32[64,128]{1,0:T(8,128)S(1)}, f32[64,128]{1,0:T(8,128)S(1)}) custom-call(f32[128,128]{1,0:T(8,128)S(1)} %shard_map.77.mine_ref, f32[128,128]{1,0:T(8,128)S(1)} %collective-permute-done.10.other_ref), custom_call_target="tpu_custom_call" | custom-call | flops 2000000000 | bytes 131072 | tf_op jit(solution)/shard_map/pallas_call | solution.py:79
  174.5 14.9 %all-to-all-done.4.got_ref = bf16[32,40,128]{2,1,0:T(8,128)(2,1)S(1)} async-done(((bf16[32,40,128]{2,1,0:T(8,128)(2,1)}), bf16[32,40,128]{2,1,0:T(8,128)(2,1)S(1)}, u32[]{:S(2)}, u32[]{:S(2)}) %all-to-all-start.4) | async-done | bytes 327712 | tf_op jit(solution)/shard_map/all_to_all | solution.py:51
  189.4 2.1 shard_map.79
  191.6 17.9 %all_to_all.37 = f32[32,8,128]{2,1,0:T(8,128)S(1)} all-to-all(f32[32,8,128]{2,1,0:T(8,128)S(1)} %shard_map.79), channel_id=1, replica_groups=mesh['zl'=8,'yh'=2,'yl'=2,'c'=2,'zh'=2,'x'=4] {'yh','yl','c','x'}, dimensions={0} | all-to-all | bytes 262144 | tf_op jit(solution)/shard_map/all_to_all | solution.py:51
  210.1 3.5 %all-to-all-start.6 = ((f32[16,8,128]{2,1,0:T(8,128)}), f32[16,8,128]{2,1,0:T(8,128)S(1)}, u32[]{:S(2)}, u32[]{:S(2)}) async-start(f32[16,8,128]{2,1,0:T(8,128)} %broadcast_in_dim.43), calls=%async_computation.6 | async-start | bytes 131072 | tf_op jit(solution)/shard_map/all_to_all | solution.py:51
  213.6 11.8 %all-to-all-done.6 = f32[16,8,128]{2,1,0:T(8,128)S(1)} async-done(((f32[16,8,128]{2,1,0:T(8,128)}), f32[16,8,128]{2,1,0:T(8,128)S(1)}, u32[]{:S(2)}, u32[]{:S(2)}) %all-to-all-start.6) | async-done | bytes 65568 | tf_op jit(solution)/shard_map/all_to_all | solution.py:51
  (52 shorter events, 12.6 us)
Async XLA Ops:
  2.6 8.6 %copy-start.3 = (bf16[80,100,256]{2,0,1:T(8,128)(2,1)}, bf16[80,100,256]{2,0,1:T(8,128)(2,1)S(1)}, u32[]{:S(2)}) copy-start(bf16[80,100,256]{2,0,1:T(8,128)(2,1)S(1)} %pad_maximum_fusion) | copy-start | bytes 12288004
  2.6 12.2 %copy-start.4 = (s32[2,64]{1,0:T(2,128)S(1)}, s32[2,64]{1,0:T(2,128)}, u32[]{:S(2)}) copy-start(s32[2,64]{1,0:T(2,128)} %param.10) | copy-start | bytes 1540
  2.7 12.3 %copy-start.5 = (s32[128]{0:T(128)S(1)}, s32[128]{0:T(128)}, u32[]{:S(2)}) copy-start(s32[128]{0:T(128)} %param.9) | copy-start | bytes 1540
  4.1 48.0 %collective-permute-start = (bf16[1280,256]{1,0:T(8,128)(2,1)}, bf16[1280,256]{1,0:T(8,128)(2,1)S(1)}, u32[]{:S(2)}, u32[]{:S(2)}) collective-permute-start(bf16[1280,256]{1,0:T(8,128)(2,1)} %get-tuple-element.51), channel_id=1, source_target_pairs={{0,1},{1,2},{2,3},{3,0},{4,5},{5,6},{6,7},{7,4},{8,9},{9,10},{10,1... | collective-permute-start | bytes 1966088 | tf_op jit(solution)/shard_map/ppermute | solution.py:303
  8.0 44.1 %collective-permute-start.1 = (bf16[1280,256]{1,0:T(8,128)(2,1)}, bf16[1280,256]{1,0:T(8,128)(2,1)S(1)}, u32[]{:S(2)}, u32[]{:S(2)}) collective-permute-start(bf16[1280,256]{1,0:T(8,128)(2,1)} %get-tuple-element.50), channel_id=1, source_target_pairs={{0,3},{1,0},{2,1},{3,2},{4,7},{5,4},{6,5},{7,6},{8,11},{9,8},{10,9... | collective-permute-start | bytes 1966088 | tf_op jit(solution)/shard_map/ppermute | solution.py:303
  11.2 40.9 %collective-permute-start.2 = (bf16[1280,256]{1,0:T(8,128)(2,1)S(1)}, bf16[1280,256]{1,0:T(8,128)(2,1)S(1)}, u32[]{:S(2)}, u32[]{:S(2)}) collective-permute-start(bf16[1280,256]{1,0:T(8,128)(2,1)S(1)} %get-tuple-element.49), channel_id=1, source_target_pairs={{0,2},{1,3},{2,0},{3,1},{4,6},{5,7},{6,4},{7,5},{8,10},{9,11},{10,... | collective-permute-start | bytes 1966088 | tf_op jit(solution)/shard_map/ppermute | solution.py:303
  52.9 14.5 %all-to-all-start.2 = ((bf16[32,16,256]{2,1,0:T(8,128)(2,1)}), bf16[32,16,256]{2,1,0:T(8,128)(2,1)S(1)}, u32[]{:S(2)}, u32[]{:S(2)}) async-start(bf16[32,16,256]{2,1,0:T(8,128)(2,1)} %broadcast_in_dim.40), calls=%async_computation.2 | async-start | bytes 524288 | tf_op jit(solution)/shard_map/all_to_all | solution.py:51
  67.4 20.8 %collective-permute-start.5 = (bf16[720,256]{1,0:T(8,128)(2,1)}, bf16[720,256]{1,0:T(8,128)(2,1)}, u32[]{:S(2)}, u32[]{:S(2)}) collective-permute-start(bf16[720,256]{1,0:T(8,128)(2,1)} %get-tuple-element.34), channel_id=1, source_target_pairs={{0,1},{1,2},{2,3},{3,0},{4,5},{5,6},{6,7},{7,4},{8,9},{9,10},{10,1... | collective-permute-start | bytes 1105928 | tf_op jit(solution)/shard_map/ppermute | solution.py:303
  69.6 18.6 %collective-permute-start.6 = (bf16[720,256]{1,0:T(8,128)(2,1)}, bf16[720,256]{1,0:T(8,128)(2,1)}, u32[]{:S(2)}, u32[]{:S(2)}) collective-permute-start(bf16[720,256]{1,0:T(8,128)(2,1)} %get-tuple-element.35), channel_id=1, source_target_pairs={{0,3},{1,0},{2,1},{3,2},{4,7},{5,4},{6,5},{7,6},{8,11},{9,8},{10,9... | collective-permute-start | bytes 1105928 | tf_op jit(solution)/shard_map/ppermute | solution.py:303
  73.9 14.3 %collective-permute-start.7 = (bf16[720,256]{1,0:T(8,128)(2,1)}, bf16[720,256]{1,0:T(8,128)(2,1)}, u32[]{:S(2)}, u32[]{:S(2)}) collective-permute-start(bf16[720,256]{1,0:T(8,128)(2,1)} %get-tuple-element.36), channel_id=1, source_target_pairs={{0,2},{1,3},{2,0},{3,1},{4,6},{5,7},{6,4},{7,5},{8,10},{9,11},{10,... | collective-permute-start | bytes 1105928 | tf_op jit(solution)/shard_map/ppermute | solution.py:303
  79.0 53.8 %copy-start.2 = (bf16[160,80]{1,0:T(8,128)(2,1)S(1)}, bf16[160,80]{1,0:T(8,128)(2,1)}, u32[]{:S(2)}) copy-start(bf16[160,80]{1,0:T(8,128)(2,1)} %constant.157.clone.basis_ref) | copy-start | bytes 76804
  79.0 48.0 %collective-permute-start.3 = (bf16[1296,128]{1,0:T(8,128)(2,1)S(1)}, bf16[1296,128]{1,0:T(8,128)(2,1)S(1)}, u32[]{:S(2)}, u32[]{:S(2)}) collective-permute-start(bf16[1296,128]{1,0:T(8,128)(2,1)S(1)} %get-tuple-element.31), channel_id=1, source_target_pairs={{0,256},{8,268},{64,320},{72,332},{128,384},{136,396},{192,448},{2... | collective-permute-start | bytes 995336 | tf_op jit(solution)/shard_map/ppermute | solution.py:341
  82.0 45.0 %collective-permute-start.4 = (bf16[1296,128]{1,0:T(8,128)(2,1)S(1)}, bf16[1296,128]{1,0:T(8,128)(2,1)S(1)}, u32[]{:S(2)}, u32[]{:S(2)}) collective-permute-start(bf16[1296,128]{1,0:T(8,128)(2,1)S(1)} %get-tuple-element.32), channel_id=1, source_target_pairs={{0,260},{8,264},{64,324},{72,328},{128,388},{136,392},{192,452},{2... | collective-permute-start | bytes 995336 | tf_op jit(solution)/shard_map/ppermute | solution.py:341
  90.9 40.8 %collective-permute-start.8 = (bf16[736,128]{1,0:T(8,128)(2,1)S(1)}, bf16[736,128]{1,0:T(8,128)(2,1)S(1)}, u32[]{:S(2)}, u32[]{:S(2)}) collective-permute-start(bf16[736,128]{1,0:T(8,128)(2,1)S(1)} %get-tuple-element.37), channel_id=1, source_target_pairs={{0,256},{8,268},{64,320},{72,332},{128,384},{136,396},{192,448},{2... | collective-permute-start | bytes 565256 | tf_op jit(solution)/shard_map/ppermute | solution.py:341
  93.9 57.9 %copy-start.1 = (bf16[1600,256]{1,0:T(8,128)(2,1)S(1)}, bf16[1600,256]{1,0:T(8,128)(2,1)}, u32[]{:S(2)}) copy-start(bf16[1600,256]{1,0:T(8,128)(2,1)} %constant.158.clone.table_ref) | copy-start | bytes 2457604
  94.0 38.8 %collective-permute-start.9 = (bf16[736,128]{1,0:T(8,128)(2,1)S(1)}, bf16[736,128]{1,0:T(8,128)(2,1)S(1)}, u32[]{:S(2)}, u32[]{:S(2)}) collective-permute-start(bf16[736,128]{1,0:T(8,128)(2,1)S(1)} %get-tuple-element.38), channel_id=1, source_target_pairs={{0,260},{8,264},{64,324},{72,328},{128,388},{136,392},{192,452},{2... | collective-permute-start | bytes 565256 | tf_op jit(solution)/shard_map/ppermute | solution.py:341
  135.7 16.1 %all-to-all-start.3 = ((f32[16,80,128]{2,1,0:T(8,128)}), f32[16,80,128]{2,1,0:T(8,128)S(1)}, u32[]{:S(2)}, u32[]{:S(2)}) async-start(f32[16,80,128]{2,1,0:T(8,128)} %bitcast.21), calls=%async_computation.3 | async-start | bytes 1310720 | tf_op jit(solution)/shard_map/all_to_all | solution.py:51
  141.3 17.9 %collective-permute-start.10 = (f32[128,128]{1,0:T(8,128)S(1)}, f32[128,128]{1,0:T(8,128)S(1)}, u32[]{:S(2)}, u32[]{:S(2)}) collective-permute-start(f32[128,128]{1,0:T(8,128)S(1)} %shard_map.77.mine_ref), channel_id=1, source_target_pairs={{0,4},{4,0},{1,5},{5,1},{2,6},{6,2},{3,7},{7,3},{8,12},{12,8},{9,1... | collective-permute-start | bytes 196616 | tf_op jit(solution)/shard_map/ppermute | solution.py:321
  159.2 30.2 %all-to-all-start.4 = ((bf16[32,40,128]{2,1,0:T(8,128)(2,1)}), bf16[32,40,128]{2,1,0:T(8,128)(2,1)S(1)}, u32[]{:S(2)}, u32[]{:S(2)}) async-start(bf16[32,40,128]{2,1,0:T(8,128)(2,1)} %bitcast.22), calls=%async_computation.4 | async-start | bytes 655360 | tf_op jit(solution)/shard_map/all_to_all | solution.py:51
  168.3 21.1 %copy-start = (bf16[1120,640]{1,0:T(8,128)(2,1)S(1)}, bf16[1120,640]{1,0:T(8,128)(2,1)}, u32[]{:S(2)}) copy-start(bf16[1120,640]{1,0:T(8,128)(2,1)} %constant.159.clone.table_ref) | copy-start | bytes 4300804
  210.1 15.3 %all-to-all-start.6 = ((f32[16,8,128]{2,1,0:T(8,128)}), f32[16,8,128]{2,1,0:T(8,128)S(1)}, u32[]{:S(2)}, u32[]{:S(2)}) async-start(f32[16,8,128]{2,1,0:T(8,128)} %broadcast_in_dim.43), calls=%async_computation.6 | async-start | bytes 131072 | tf_op jit(solution)/shard_map/all_to_all | solution.py:51

commit v5 on v4

--- a/solution.py
+++ b/solution.py
@@ -314,7 +314,6 @@
     rows = add(swap(jnp.broadcast_to(rows[None], (8, 16, 2 * width)), "zl"))
     rows, first = lax.optimization_barrier((rows, first))
     pts = swap(jnp.broadcast_to(rows[None], (32, 16, 2 * width)), ROWS + ("x",))
-    pts, second = lax.optimization_barrier((pts, second))
     second = second[:1] + [spread(block, shift) for block, shift in zip(second[1:], SHIFTS[1:])]
 
     def cross(values):

time: 227 us -> 221 us (0.974)
  blocking collectives: 50.6 us -> 30.7 us
  starting transfers between devices: 67.5 us -> 81.8 us
    all_to_all x3 -> x2, blocking collectives: 50.6 us -> 30.7 us  [swap(): return lax.all_to_all(values, axes, 0, 0, tiled=True)]
    all_to_all x4 -> x5, starting transfers between devices: 22.5 us -> 35.1 us  [swap(): return lax.all_to_all(values, axes, 0, 0, tiled=True)]
    ppermute x2, waiting for transfers between devices: 31.4 us -> 25.9 us  [half_sums(): lax.ppermute(one, ('zl', 'c', 'zh'), hops(4))]
    ppermute x2, waiting for transfers between devices: 1.15 us -> 6.37 us  [half_sums(): lax.ppermute(two, ('zl', 'c', 'zh'), hops(12))]
    ppermute x1, waiting for transfers between devices: 4.82 us -> 1.07 us  [cross(): return lax.ppermute(values, 'zh', [(0, 1), (1, 0)])]
    all_to_all x4 -> x5, waiting for transfers between devices: 36.5 us -> 39.5 us  [swap(): return lax.all_to_all(values, axes, 0, 0, tiled=True)]
  transfers between devices with their start and end apart: 15 -> 16, of which waited for: 8 -> 7; matrix products, arithmetic and copies ran while one was open for 3% -> 4% of each run, Pallas kernels for 7% -> 7%
where the time goes in v5:
time: 221 us; the launch traced here: 220 us
  starting transfers between devices  81.8 us (37%)
  waiting for transfers between devices  72.9 us (33%)
  blocking collectives  30.7 us (14%)
  Pallas kernels  20.1 us (9%)
  local copies, waits for them, and re-layouts  10.9 us (5%)
  other arithmetic  3.38 us (2%)
    all_to_all x5, waiting for transfers between devices, swap(): return lax.all_to_all(values, axes, 0, 0, tiled=True)  39.5 us
    all_to_all x5, starting transfers between devices, swap(): return lax.all_to_all(values, axes, 0, 0, tiled=True)  35.1 us
    all_to_all x2, blocking collectives, swap(): return lax.all_to_all(values, axes, 0, 0, tiled=True)  30.7 us
    ppermute x2, waiting for transfers between devices, half_sums(): lax.ppermute(one, ('zl', 'c', 'zh'), hops(4))  25.9 us
    ppermute x6, starting transfers between devices, spread(): return lax.ppermute(block, 'x', [(i, (i + shift) % 4) for i in range(4)])  20.8 us
    pallas_call x7, Pallas kernels, whole_call(): pl.pallas_call(kernel, out_shape=out_shape, in_specs=[pl.BlockSpec(memory...  20.1 us
    ppermute x2, starting transfers between devices, half_sums(): lax.ppermute(two, ('zl', 'c', 'zh'), hops(12))  12.4 us
    ppermute x1, starting transfers between devices, cross(): return lax.ppermute(values, 'zh', [(0, 1), (1, 0)])  7.3 us
  transfers between devices with their start and end apart: 16, of which 7 were waited for; matrix products, arithmetic and copies ran while one was open for 4% of the time, Pallas kernels for 7%

profile of v5, /device:TPU:1, one launch (start us, length us, event | category | flops | bytes accessed | tf_op | source)
XLA Modules:
  0.0 220.0 jit_solution(4575856712389296651)
XLA Ops:
  0.0 2.6 %pad_maximum_fusion = bf16[80,100,256]{2,0,1:T(8,128)(2,1)S(1)} fusion(bf16[80,100,128]{2,0,1:T(8,128)(2,1)} %param.8, bf16[80,100,128]{2,0,1:T(8,128)(2,1)} %param.7), kind=kLoop, calls=%fused_computation.2 | loop fusion | flops 8192000 | bytes 8192000 | tf_op jit(solution)/shard_map/concatenate | solution.py:287
  4.1 3.9 %collective-permute-start = (bf16[1280,256]{1,0:T(8,128)(2,1)}, bf16[1280,256]{1,0:T(8,128)(2,1)S(1)}, u32[]{:S(2)}, u32[]{:S(2)}) collective-permute-start(bf16[1280,256]{1,0:T(8,128)(2,1)} %get-tuple-element.41), channel_id=1, source_target_pairs={{0,1},{1,2},{2,3},{3,0},{4,5},{5,6},{6,7},{7,4},{8,9},{9,10},{10,1... | collective-permute-start | bytes 1966088 | tf_op jit(solution)/shard_map/ppermute | solution.py:303
  8.0 3.2 %collective-permute-start.1 = (bf16[1280,256]{1,0:T(8,128)(2,1)}, bf16[1280,256]{1,0:T(8,128)(2,1)S(1)}, u32[]{:S(2)}, u32[]{:S(2)}) collective-permute-start(bf16[1280,256]{1,0:T(8,128)(2,1)} %get-tuple-element.40), channel_id=1, source_target_pairs={{0,3},{1,0},{2,1},{3,2},{4,7},{5,4},{6,5},{7,6},{8,11},{9,8},{10,9... | collective-permute-start | bytes 1966088 | tf_op jit(solution)/shard_map/ppermute | solution.py:303
  11.2 3.6 %collective-permute-start.2 = (bf16[1280,256]{1,0:T(8,128)(2,1)S(1)}, bf16[1280,256]{1,0:T(8,128)(2,1)S(1)}, u32[]{:S(2)}, u32[]{:S(2)}) collective-permute-start(bf16[1280,256]{1,0:T(8,128)(2,1)S(1)} %get-tuple-element.39), channel_id=1, source_target_pairs={{0,2},{1,3},{2,0},{3,1},{4,6},{5,7},{6,4},{7,5},{8,10},{9,11},{10,... | collective-permute-start | bytes 1966088 | tf_op jit(solution)/shard_map/ppermute | solution.py:303
  19.3 12.6 %all_to_all.35 = bf16[8,16,256]{2,1,0:T(8,128)(2,1)S(1)} all-to-all(bf16[8,16,256]{2,1,0:T(8,128)(2,1)S(1)} %maximum_select_fusion), channel_id=1, replica_groups=mesh['zl'=8,'yh'=2,'yl'=2,'c'=2,'zh'=2,'x'=4] {'yh','yl','c'}, dimensions={0} | all-to-all | bytes 131072 | tf_op jit(solution)/shard_map/all_to_all | solution.py:51
  32.5 10.6 %all-to-all-start.1 = ((bf16[8,16,256]{2,1,0:T(8,128)(2,1)}), bf16[8,16,256]{2,1,0:T(8,128)(2,1)S(1)}, u32[]{:S(2)}, u32[]{:S(2)}) async-start(bf16[8,16,256]{2,1,0:T(8,128)(2,1)} %broadcast_in_dim.39), calls=%async_computation.1 | async-start | bytes 131072 | tf_op jit(solution)/shard_map/all_to_all | solution.py:51
  43.1 9.8 %all-to-all-done.1 = bf16[8,16,256]{2,1,0:T(8,128)(2,1)S(1)} async-done(((bf16[8,16,256]{2,1,0:T(8,128)(2,1)}), bf16[8,16,256]{2,1,0:T(8,128)(2,1)S(1)}, u32[]{:S(2)}, u32[]{:S(2)}) %all-to-all-start.1) | async-done | bytes 65568 | tf_op jit(solution)/shard_map/all_to_all | solution.py:51
  53.7 5.6 %all-to-all-start.2 = ((bf16[32,16,256]{2,1,0:T(8,128)(2,1)}), bf16[32,16,256]{2,1,0:T(8,128)(2,1)S(1)}, u32[]{:S(2)}, u32[]{:S(2)}) async-start(bf16[32,16,256]{2,1,0:T(8,128)(2,1)} %broadcast_in_dim.40), calls=%async_computation.2 | async-start | bytes 524288 | tf_op jit(solution)/shard_map/all_to_all | solution.py:51
  59.3 2.3 %dynamic-slice_bitcast_fusion.4 = (bf16[720,256]{1,0:T(8,128)(2,1)}, bf16[720,256]{1,0:T(8,128)(2,1)}, bf16[720,256]{1,0:T(8,128)(2,1)}, bf16[720,256]{1,0:T(8,128)(2,1)S(1)}) fusion(bf16[4,2000,256]{2,1,0:T(8,128)(2,1)} %bitcast.50, s32[]{:T(128)S(6)} %select_n.185, s32[]{:T(128)S(6)} %add.263, s32[]{:T(128)S(6)} %select_n.183, s32[]{:T(128)S(6)} %select_n.181, ...), kind=kLoop, calls=%fused_computation.7 | loop fusion | bytes 2949140 | tf_op jit(solution)/shard_map/slice | solution.py:307
  61.7 3.3 %collective-permute-start.5 = (bf16[720,256]{1,0:T(8,128)(2,1)}, bf16[720,256]{1,0:T(8,128)(2,1)}, u32[]{:S(2)}, u32[]{:S(2)}) collective-permute-start(bf16[720,256]{1,0:T(8,128)(2,1)} %get-tuple-element.37), channel_id=1, source_target_pairs={{0,1},{1,2},{2,3},{3,0},{4,5},{5,6},{6,7},{7,4},{8,9},{9,10},{10,1... | collective-permute-start | bytes 1105928 | tf_op jit(solution)/shard_map/ppermute | solution.py:303
  65.0 3.2 %collective-permute-start.6 = (bf16[720,256]{1,0:T(8,128)(2,1)}, bf16[720,256]{1,0:T(8,128)(2,1)}, u32[]{:S(2)}, u32[]{:S(2)}) collective-permute-start(bf16[720,256]{1,0:T(8,128)(2,1)} %get-tuple-element.36), channel_id=1, source_target_pairs={{0,3},{1,0},{2,1},{3,2},{4,7},{5,4},{6,5},{7,6},{8,11},{9,8},{10,9... | collective-permute-start | bytes 1105928 | tf_op jit(solution)/shard_map/ppermute | solution.py:303
  68.2 3.6 %collective-permute-start.7 = (bf16[720,256]{1,0:T(8,128)(2,1)}, bf16[720,256]{1,0:T(8,128)(2,1)}, u32[]{:S(2)}, u32[]{:S(2)}) collective-permute-start(bf16[720,256]{1,0:T(8,128)(2,1)} %get-tuple-element.35), channel_id=1, source_target_pairs={{0,2},{1,3},{2,0},{3,1},{4,6},{5,7},{6,4},{7,5},{8,10},{9,11},{10,... | collective-permute-start | bytes 1105928 | tf_op jit(solution)/shard_map/ppermute | solution.py:303
  71.9 3.0 %shard_map.73 = (bf16[1296,128]{1,0:T(8,128)(2,1)S(1)}, bf16[1296,128]{1,0:T(8,128)(2,1)S(1)}) custom-call(s32[2]{0:T(128)S(1)} %pad_add_fusion.rank_ref, bf16[32,16,256]{2,1,0:T(8,128)(2,1)S(1)} %all-to-all-done.2.points_ref, bf16[1280,256]{1,0:T(8,128)(2,1)S(1)} %get-tuple-element.21.own, bf16[1280,256]{1,0:T(8,128)(2,1)S(1)} %collective-permute-done.left, ...), custom_call_target="tpu_custom_call" | custom-call | flops 2000000000 | bytes 5767168 | tf_op jit(solution)/shard_map/pallas_call | solution.py:79
  74.9 3.0 %collective-permute-start.3 = (bf16[1296,128]{1,0:T(8,128)(2,1)S(1)}, bf16[1296,128]{1,0:T(8,128)(2,1)S(1)}, u32[]{:S(2)}, u32[]{:S(2)}) collective-permute-start(bf16[1296,128]{1,0:T(8,128)(2,1)S(1)} %get-tuple-element.25), channel_id=1, source_target_pairs={{0,256},{8,268},{64,320},{72,332},{128,384},{136,396},{192,448},{2... | collective-permute-start | bytes 995336 | tf_op jit(solution)/shard_map/ppermute | solution.py:340
  78.0 6.1 %collective-permute-start.4 = (bf16[1296,128]{1,0:T(8,128)(2,1)S(1)}, bf16[1296,128]{1,0:T(8,128)(2,1)S(1)}, u32[]{:S(2)}, u32[]{:S(2)}) collective-permute-start(bf16[1296,128]{1,0:T(8,128)(2,1)S(1)} %get-tuple-element.26), channel_id=1, source_target_pairs={{0,260},{8,264},{64,324},{72,328},{128,388},{136,392},{192,452},{2... | collective-permute-start | bytes 995336 | tf_op jit(solution)/shard_map/ppermute | solution.py:340
  84.1 2.7 %shard_map.74 = (bf16[736,128]{1,0:T(8,128)(2,1)S(1)}, bf16[736,128]{1,0:T(8,128)(2,1)S(1)}) custom-call(s32[2]{0:T(128)S(1)} %pad_add_fusion.rank_ref, bf16[32,16,256]{2,1,0:T(8,128)(2,1)S(1)} %all-to-all-done.2.points_ref, bf16[720,256]{1,0:T(8,128)(2,1)S(1)} %get-tuple-element.38.own, bf16[720,256]{1,0:T(8,128)(2,1)} %collective-permute-done.5.left, ...), custom_call_target="tpu_custom_call" | custom-call | flops 2000000000 | bytes 3473408 | tf_op jit(solution)/shard_map/pallas_call | solution.py:79
  86.8 3.0 %collective-permute-start.8 = (bf16[736,128]{1,0:T(8,128)(2,1)S(1)}, bf16[736,128]{1,0:T(8,128)(2,1)S(1)}, u32[]{:S(2)}, u32[]{:S(2)}) collective-permute-start(bf16[736,128]{1,0:T(8,128)(2,1)S(1)} %get-tuple-element.27), channel_id=1, source_target_pairs={{0,256},{8,268},{64,320},{72,332},{128,384},{136,396},{192,448},{2... | collective-permute-start | bytes 565256 | tf_op jit(solution)/shard_map/ppermute | solution.py:340
  89.9 6.3 %collective-permute-start.9 = (bf16[736,128]{1,0:T(8,128)(2,1)S(1)}, bf16[736,128]{1,0:T(8,128)(2,1)S(1)}, u32[]{:S(2)}, u32[]{:S(2)}) collective-permute-start(bf16[736,128]{1,0:T(8,128)(2,1)S(1)} %get-tuple-element.28), channel_id=1, source_target_pairs={{0,260},{8,264},{64,324},{72,328},{128,388},{136,392},{192,452},{2... | collective-permute-start | bytes 565256 | tf_op jit(solution)/shard_map/ppermute | solution.py:340
  96.2 25.9 %collective-permute-done.8.below_b = bf16[736,128]{1,0:T(8,128)(2,1)S(1)} collective-permute-done((bf16[736,128]{1,0:T(8,128)(2,1)S(1)}, bf16[736,128]{1,0:T(8,128)(2,1)S(1)}, u32[]{:S(2)}, u32[]{:S(2)}) %collective-permute-start.8) | collective-permute-done | bytes 188448 | tf_op jit(solution)/shard_map/ppermute | solution.py:340
  122.1 6.4 %collective-permute-done.9.above_b = bf16[736,128]{1,0:T(8,128)(2,1)S(1)} collective-permute-done((bf16[736,128]{1,0:T(8,128)(2,1)S(1)}, bf16[736,128]{1,0:T(8,128)(2,1)S(1)}, u32[]{:S(2)}, u32[]{:S(2)}) %collective-permute-start.9) | collective-permute-done | bytes 188448 | tf_op jit(solution)/shard_map/ppermute | solution.py:340
  128.5 2.9 %shard_map.75 = f32[1280,128]{1,0:T(8,128)} custom-call(bf16[1296,128]{1,0:T(8,128)(2,1)S(1)} %collective-permute-done.3.below_a, bf16[1296,128]{1,0:T(8,128)(2,1)S(1)} %collective-permute-done.4.above_a, bf16[736,128]{1,0:T(8,128)(2,1)S(1)} %collective-permute-done.8.below_b, bf16[736,128]{1,0:T(8,128)(2,1)S(1)} %collective-permute-done.9.above_b, ...), custom_call_target="tpu_custom_call" | custom-call | flops 2000000000 | bytes 2131968 | tf_op jit(solution)/shard_map/pallas_call | solution.py:79
  131.3 4.1 %all-to-all-start.3 = ((f32[16,80,128]{2,1,0:T(8,128)}), f32[16,80,128]{2,1,0:T(8,128)S(1)}, u32[]{:S(2)}, u32[]{:S(2)}) async-start(f32[16,80,128]{2,1,0:T(8,128)} %bitcast.21), calls=%async_computation.3 | async-start | bytes 1310720 | tf_op jit(solution)/shard_map/all_to_all | solution.py:51
  136.3 7.3 %collective-permute-start.10 = (f32[128,128]{1,0:T(8,128)S(1)}, f32[128,128]{1,0:T(8,128)S(1)}, u32[]{:S(2)}, u32[]{:S(2)}) collective-permute-start(f32[128,128]{1,0:T(8,128)S(1)} %shard_map.77.mine_ref), channel_id=1, source_target_pairs={{0,4},{4,0},{1,5},{5,1},{2,6},{6,2},{3,7},{7,3},{8,12},{12,8},{9,1... | collective-permute-start | bytes 196616 | tf_op jit(solution)/shard_map/ppermute | solution.py:320
  143.6 3.2 %all-to-all-done.3.in_ref = f32[16,80,128]{2,1,0:T(8,128)S(1)} async-done(((f32[16,80,128]{2,1,0:T(8,128)}), f32[16,80,128]{2,1,0:T(8,128)S(1)}, u32[]{:S(2)}, u32[]{:S(2)}) %all-to-all-start.3) | async-done | bytes 655392 | tf_op jit(solution)/shard_map/all_to_all | solution.py:51
  146.9 2.5 %shard_map.76 = bf16[1280,128]{1,0:T(8,128)(2,1)} custom-call(f32[16,80,128]{2,1,0:T(8,128)S(1)} %all-to-all-done.3.in_ref, bf16[1600,256]{1,0:T(8,128)(2,1)S(1)} %copy-done.1), custom_call_target="tpu_custom_call" | custom-call | flops 2000000000 | bytes 2293760 | tf_op jit(solution)/shard_map/pallas_call | solution.py:79
  150.5 11.3 %all-to-all-start.4 = ((bf16[32,40,128]{2,1,0:T(8,128)(2,1)}), bf16[32,40,128]{2,1,0:T(8,128)(2,1)S(1)}, u32[]{:S(2)}, u32[]{:S(2)}) async-start(bf16[32,40,128]{2,1,0:T(8,128)(2,1)} %bitcast.22), calls=%async_computation.4 | async-start | bytes 655360 | tf_op jit(solution)/shard_map/all_to_all | solution.py:51
  162.4 6.0 %shard_map.78 = (f32[64,128]{1,0:T(8,128)S(1)}, f32[64,128]{1,0:T(8,128)S(1)}) custom-call(f32[128,128]{1,0:T(8,128)S(1)} %shard_map.77.mine_ref, f32[128,128]{1,0:T(8,128)S(1)} %collective-permute-done.10.other_ref), custom_call_target="tpu_custom_call" | custom-call | flops 2000000000 | bytes 131072 | tf_op jit(solution)/shard_map/pallas_call | solution.py:79
  168.4 14.7 %all-to-all-done.4.got_ref = bf16[32,40,128]{2,1,0:T(8,128)(2,1)S(1)} async-done(((bf16[32,40,128]{2,1,0:T(8,128)(2,1)}), bf16[32,40,128]{2,1,0:T(8,128)(2,1)S(1)}, u32[]{:S(2)}, u32[]{:S(2)}) %all-to-all-start.4) | async-done | bytes 327712 | tf_op jit(solution)/shard_map/all_to_all | solution.py:51
  183.1 2.1 shard_map.79
  185.3 18.1 %all_to_all.36 = f32[32,8,128]{2,1,0:T(8,128)S(1)} all-to-all(f32[32,8,128]{2,1,0:T(8,128)S(1)} %shard_map.79), channel_id=1, replica_groups=mesh['zl'=8,'yh'=2,'yl'=2,'c'=2,'zh'=2,'x'=4] {'yh','yl','c','x'}, dimensions={0} | all-to-all | bytes 262144 | tf_op jit(solution)/shard_map/all_to_all | solution.py:51
  204.0 3.5 %all-to-all-start.6 = ((f32[16,8,128]{2,1,0:T(8,128)}), f32[16,8,128]{2,1,0:T(8,128)S(1)}, u32[]{:S(2)}, u32[]{:S(2)}) async-start(f32[16,8,128]{2,1,0:T(8,128)} %broadcast_in_dim.43), calls=%async_computation.6 | async-start | bytes 131072 | tf_op jit(solution)/shard_map/all_to_all | solution.py:51
  207.5 11.8 %all-to-all-done.6 = f32[16,8,128]{2,1,0:T(8,128)S(1)} async-done(((f32[16,8,128]{2,1,0:T(8,128)}), f32[16,8,128]{2,1,0:T(8,128)S(1)}, u32[]{:S(2)}, u32[]{:S(2)}) %all-to-all-start.6) | async-done | bytes 65568 | tf_op jit(solution)/shard_map/all_to_all | solution.py:51
  (53 shorter events, 11.2 us)
Async XLA Ops:
  2.6 8.6 %copy-start.3 = (bf16[80,100,256]{2,0,1:T(8,128)(2,1)}, bf16[80,100,256]{2,0,1:T(8,128)(2,1)S(1)}, u32[]{:S(2)}) copy-start(bf16[80,100,256]{2,0,1:T(8,128)(2,1)S(1)} %pad_maximum_fusion) | copy-start | bytes 12288004
  2.6 12.2 %copy-start.4 = (s32[2,64]{1,0:T(2,128)S(1)}, s32[2,64]{1,0:T(2,128)}, u32[]{:S(2)}) copy-start(s32[2,64]{1,0:T(2,128)} %param.10) | copy-start | bytes 1540
  2.7 12.3 %copy-start.5 = (s32[128]{0:T(128)S(1)}, s32[128]{0:T(128)}, u32[]{:S(2)}) copy-start(s32[128]{0:T(128)} %param.9) | copy-start | bytes 1540
  4.1 48.8 %collective-permute-start = (bf16[1280,256]{1,0:T(8,128)(2,1)}, bf16[1280,256]{1,0:T(8,128)(2,1)S(1)}, u32[]{:S(2)}, u32[]{:S(2)}) collective-permute-start(bf16[1280,256]{1,0:T(8,128)(2,1)} %get-tuple-element.41), channel_id=1, source_target_pairs={{0,1},{1,2},{2,3},{3,0},{4,5},{5,6},{6,7},{7,4},{8,9},{9,10},{10,1... | collective-permute-start | bytes 1966088 | tf_op jit(solution)/shard_map/ppermute | solution.py:303
  8.0 44.9 %collective-permute-start.1 = (bf16[1280,256]{1,0:T(8,128)(2,1)}, bf16[1280,256]{1,0:T(8,128)(2,1)S(1)}, u32[]{:S(2)}, u32[]{:S(2)}) collective-permute-start(bf16[1280,256]{1,0:T(8,128)(2,1)} %get-tuple-element.40), channel_id=1, source_target_pairs={{0,3},{1,0},{2,1},{3,2},{4,7},{5,4},{6,5},{7,6},{8,11},{9,8},{10,9... | collective-permute-start | bytes 1966088 | tf_op jit(solution)/shard_map/ppermute | solution.py:303
  11.2 41.7 %collective-permute-start.2 = (bf16[1280,256]{1,0:T(8,128)(2,1)S(1)}, bf16[1280,256]{1,0:T(8,128)(2,1)S(1)}, u32[]{:S(2)}, u32[]{:S(2)}) collective-permute-start(bf16[1280,256]{1,0:T(8,128)(2,1)S(1)} %get-tuple-element.39), channel_id=1, source_target_pairs={{0,2},{1,3},{2,0},{3,1},{4,6},{5,7},{6,4},{7,5},{8,10},{9,11},{10,... | collective-permute-start | bytes 1966088 | tf_op jit(solution)/shard_map/ppermute | solution.py:303
  32.5 20.3 %all-to-all-start.1 = ((bf16[8,16,256]{2,1,0:T(8,128)(2,1)}), bf16[8,16,256]{2,1,0:T(8,128)(2,1)S(1)}, u32[]{:S(2)}, u32[]{:S(2)}) async-start(bf16[8,16,256]{2,1,0:T(8,128)(2,1)} %broadcast_in_dim.39), calls=%async_computation.1 | async-start | bytes 131072 | tf_op jit(solution)/shard_map/all_to_all | solution.py:51
  53.7 18.2 %all-to-all-start.2 = ((bf16[32,16,256]{2,1,0:T(8,128)(2,1)}), bf16[32,16,256]{2,1,0:T(8,128)(2,1)S(1)}, u32[]{:S(2)}, u32[]{:S(2)}) async-start(bf16[32,16,256]{2,1,0:T(8,128)(2,1)} %broadcast_in_dim.40), calls=%async_computation.2 | async-start | bytes 524288 | tf_op jit(solution)/shard_map/all_to_all | solution.py:51
  61.7 22.4 %collective-permute-start.5 = (bf16[720,256]{1,0:T(8,128)(2,1)}, bf16[720,256]{1,0:T(8,128)(2,1)}, u32[]{:S(2)}, u32[]{:S(2)}) collective-permute-start(bf16[720,256]{1,0:T(8,128)(2,1)} %get-tuple-element.37), channel_id=1, source_target_pairs={{0,1},{1,2},{2,3},{3,0},{4,5},{5,6},{6,7},{7,4},{8,9},{9,10},{10,1... | collective-permute-start | bytes 1105928 | tf_op jit(solution)/shard_map/ppermute | solution.py:303
  65.0 19.2 %collective-permute-start.6 = (bf16[720,256]{1,0:T(8,128)(2,1)}, bf16[720,256]{1,0:T(8,128)(2,1)}, u32[]{:S(2)}, u32[]{:S(2)}) collective-permute-start(bf16[720,256]{1,0:T(8,128)(2,1)} %get-tuple-element.36), channel_id=1, source_target_pairs={{0,3},{1,0},{2,1},{3,2},{4,7},{5,4},{6,5},{7,6},{8,11},{9,8},{10,9... | collective-permute-start | bytes 1105928 | tf_op jit(solution)/shard_map/ppermute | solution.py:303
  68.2 16.0 %collective-permute-start.7 = (bf16[720,256]{1,0:T(8,128)(2,1)}, bf16[720,256]{1,0:T(8,128)(2,1)}, u32[]{:S(2)}, u32[]{:S(2)}) collective-permute-start(bf16[720,256]{1,0:T(8,128)(2,1)} %get-tuple-element.35), channel_id=1, source_target_pairs={{0,2},{1,3},{2,0},{3,1},{4,6},{5,7},{6,4},{7,5},{8,10},{9,11},{10,... | collective-permute-start | bytes 1105928 | tf_op jit(solution)/shard_map/ppermute | solution.py:303
  74.9 53.6 %copy-start.2 = (bf16[160,80]{1,0:T(8,128)(2,1)S(1)}, bf16[160,80]{1,0:T(8,128)(2,1)}, u32[]{:S(2)}) copy-start(bf16[160,80]{1,0:T(8,128)(2,1)} %constant.157.clone.basis_ref) | copy-start | bytes 76804
  74.9 53.5 %collective-permute-start.3 = (bf16[1296,128]{1,0:T(8,128)(2,1)S(1)}, bf16[1296,128]{1,0:T(8,128)(2,1)S(1)}, u32[]{:S(2)}, u32[]{:S(2)}) collective-permute-start(bf16[1296,128]{1,0:T(8,128)(2,1)S(1)} %get-tuple-element.25), channel_id=1, source_target_pairs={{0,256},{8,268},{64,320},{72,332},{128,384},{136,396},{192,448},{2... | collective-permute-start | bytes 995336 | tf_op jit(solution)/shard_map/ppermute | solution.py:340
  78.0 50.5 %collective-permute-start.4 = (bf16[1296,128]{1,0:T(8,128)(2,1)S(1)}, bf16[1296,128]{1,0:T(8,128)(2,1)S(1)}, u32[]{:S(2)}, u32[]{:S(2)}) collective-permute-start(bf16[1296,128]{1,0:T(8,128)(2,1)S(1)} %get-tuple-element.26), channel_id=1, source_target_pairs={{0,260},{8,264},{64,324},{72,328},{128,388},{136,392},{192,452},{2... | collective-permute-start | bytes 995336 | tf_op jit(solution)/shard_map/ppermute | solution.py:340
  86.8 35.3 %collective-permute-start.8 = (bf16[736,128]{1,0:T(8,128)(2,1)S(1)}, bf16[736,128]{1,0:T(8,128)(2,1)S(1)}, u32[]{:S(2)}, u32[]{:S(2)}) collective-permute-start(bf16[736,128]{1,0:T(8,128)(2,1)S(1)} %get-tuple-element.27), channel_id=1, source_target_pairs={{0,256},{8,268},{64,320},{72,332},{128,384},{136,396},{192,448},{2... | collective-permute-start | bytes 565256 | tf_op jit(solution)/shard_map/ppermute | solution.py:340
  89.9 57.0 %copy-start.1 = (bf16[1600,256]{1,0:T(8,128)(2,1)S(1)}, bf16[1600,256]{1,0:T(8,128)(2,1)}, u32[]{:S(2)}) copy-start(bf16[1600,256]{1,0:T(8,128)(2,1)} %constant.158.clone.table_ref) | copy-start | bytes 2457604
  89.9 38.6 %collective-permute-start.9 = (bf16[736,128]{1,0:T(8,128)(2,1)S(1)}, bf16[736,128]{1,0:T(8,128)(2,1)S(1)}, u32[]{:S(2)}, u32[]{:S(2)}) collective-permute-start(bf16[736,128]{1,0:T(8,128)(2,1)S(1)} %get-tuple-element.28), channel_id=1, source_target_pairs={{0,260},{8,264},{64,324},{72,328},{128,388},{136,392},{192,452},{2... | collective-permute-start | bytes 565256 | tf_op jit(solution)/shard_map/ppermute | solution.py:340
  131.3 15.5 %all-to-all-start.3 = ((f32[16,80,128]{2,1,0:T(8,128)}), f32[16,80,128]{2,1,0:T(8,128)S(1)}, u32[]{:S(2)}, u32[]{:S(2)}) async-start(f32[16,80,128]{2,1,0:T(8,128)} %bitcast.21), calls=%async_computation.3 | async-start | bytes 1310720 | tf_op jit(solution)/shard_map/all_to_all | solution.py:51
  136.3 14.2 %collective-permute-start.10 = (f32[128,128]{1,0:T(8,128)S(1)}, f32[128,128]{1,0:T(8,128)S(1)}, u32[]{:S(2)}, u32[]{:S(2)}) collective-permute-start(f32[128,128]{1,0:T(8,128)S(1)} %shard_map.77.mine_ref), channel_id=1, source_target_pairs={{0,4},{4,0},{1,5},{5,1},{2,6},{6,2},{3,7},{7,3},{8,12},{12,8},{9,1... | collective-permute-start | bytes 196616 | tf_op jit(solution)/shard_map/ppermute | solution.py:320
  150.5 32.7 %all-to-all-start.4 = ((bf16[32,40,128]{2,1,0:T(8,128)(2,1)}), bf16[32,40,128]{2,1,0:T(8,128)(2,1)S(1)}, u32[]{:S(2)}, u32[]{:S(2)}) async-start(bf16[32,40,128]{2,1,0:T(8,128)(2,1)} %bitcast.22), calls=%async_computation.4 | async-start | bytes 655360 | tf_op jit(solution)/shard_map/all_to_all | solution.py:51
  162.3 20.9 %copy-start = (bf16[1120,640]{1,0:T(8,128)(2,1)S(1)}, bf16[1120,640]{1,0:T(8,128)(2,1)}, u32[]{:S(2)}) copy-start(bf16[1120,640]{1,0:T(8,128)(2,1)} %constant.159.clone.table_ref) | copy-start | bytes 4300804
  204.0 15.3 %all-to-all-start.6 = ((f32[16,8,128]{2,1,0:T(8,128)}), f32[16,8,128]{2,1,0:T(8,128)S(1)}, u32[]{:S(2)}, u32[]{:S(2)}) async-start(f32[16,8,128]{2,1,0:T(8,128)} %broadcast_in_dim.43), calls=%async_computation.6 | async-start | bytes 131072 | tf_op jit(solution)/shard_map/all_to_all | solution.py:51

commit v6 on v5

--- a/solution.py
+++ b/solution.py
@@ -249,11 +249,13 @@
     total = total + pltpu.roll(pltpu.roll(total, PANEL, 0), PANEL, 1)
     total = dot_three(bra_ref[...][:, :PANEL], total[:PANEL, :PANEL])
     total = dot_three(total, fit_ref[...])
-    left_lanes = lax.broadcasted_iota(jnp.int32, (8, 2 * PANEL), 1) < PANEL
+    left_lanes = lax.broadcasted_iota(jnp.int32, (4, 2 * PANEL), 1) < PANEL
     for to in range(4):
-        rows = jnp.where(left_lanes, total[8 * to : 8 * to + 8], total[32 + 8 * to : 40 + 8 * to])
-        for row in range(8):
-            out_ref[row * 4 + to] = rows
+        for half in range(2):
+            low = half * 32 + to * 8
+            rows = jnp.where(left_lanes, total[low : low + 4], total[low + 4 : low + 8])
+            for row in range(8):
+                out_ref[row * 4 + to, pl.ds(half * 4, 4), :] = rows
 
 
 def second_table():
@@ -365,8 +367,9 @@
     out_shape = jax.ShapeDtypeStruct((32, 8, 2 * PANEL), F32)
     part = whole_call(third_kernel, out_shape, [], (), fields, two_parts(third_table()), kernel, *inverses)
     part = jnp.sum(swap(part, ROWS + ("x",)), axis=0)
-    part = jnp.sum(swap(jnp.broadcast_to(part[None], (16, 8, 2 * PANEL)), ("zl", "zh")), axis=0)
-    return lax.dynamic_slice_in_dim(part, zh_rank * PANEL, PANEL, 1)
+    part = jnp.broadcast_to(part.reshape(1, 2, 4, 2 * PANEL), (8, 2, 4, 2 * PANEL)).reshape(16, 4, 2 * PANEL)
+    part = jnp.sum(swap(part, ("zl", "zh")), axis=0)
+    return jnp.concatenate([part[:, :PANEL], part[:, PANEL:]], axis=0)
 
 
 def solution(mesh):

time: 221 us -> 219 us (level)
  blocking collectives: 30.7 us -> 44.1 us
  waiting for transfers between devices: 72.9 us -> 60.9 us
  starting transfers between devices: 81.8 us -> 78.4 us
    all_to_all x2 -> x3, blocking collectives: 30.7 us -> 44.1 us  [swap(): return lax.all_to_all(values, axes, 0, 0, tiled=True)]
    all_to_all x5 -> x4, waiting for transfers between devices: 39.5 us -> 26.5 us  [swap(): return lax.all_to_all(values, axes, 0, 0, tiled=True)]
    all_to_all x5 -> x4, starting transfers between devices: 35.1 us -> 31.2 us  [swap(): return lax.all_to_all(values, axes, 0, 0, tiled=True)]
  transfers between devices with their start and end apart: 16 -> 15, of which waited for: 7 -> 6; matrix products, arithmetic and copies ran while one was open for 4% -> 4% of each run, Pallas kernels for 7% -> 7%
where the time goes in v6:
time: 219 us; the launch traced here: 218 us
  starting transfers between devices  78.4 us (36%)
  waiting for transfers between devices  60.9 us (28%)
  blocking collectives  44.1 us (20%)
  Pallas kernels  20.1 us (9%)
  local copies, waits for them, and re-layouts  9.7 us (4%)
  other arithmetic  4 us (2%)
    all_to_all x3, blocking collectives, swap(): return lax.all_to_all(values, axes, 0, 0, tiled=True)  44.1 us
    all_to_all x4, starting transfers between devices, swap(): return lax.all_to_all(values, axes, 0, 0, tiled=True)  31.2 us
    all_to_all x4, waiting for transfers between devices, swap(): return lax.all_to_all(values, axes, 0, 0, tiled=True)  26.5 us
    ppermute x2, waiting for transfers between devices, half_sums(): lax.ppermute(one, ('zl', 'c', 'zh'), hops(4))  25.4 us
    ppermute x6, starting transfers between devices, spread(): return lax.ppermute(block, 'x', [(i, (i + shift) % 4) for i in range(4)])  20.8 us
    pallas_call x7, Pallas kernels, whole_call(): pl.pallas_call(kernel, out_shape=out_shape, in_specs=[pl.BlockSpec(memory...  20.1 us
    ppermute x2, starting transfers between devices, half_sums(): lax.ppermute(two, ('zl', 'c', 'zh'), hops(12))  12.4 us
    ppermute x1, starting transfers between devices, cross(): return lax.ppermute(values, 'zh', [(0, 1), (1, 0)])  7.89 us
  transfers between devices with their start and end apart: 15, of which 6 were waited for; matrix products, arithmetic and copies ran while one was open for 4% of the time, Pallas kernels for 7%

profile of v6, /device:TPU:1, one launch (start us, length us, event | category | flops | bytes accessed | tf_op | source)
XLA Modules:
  0.0 217.6 jit_solution(10956425516461952757)
XLA Ops:
  0.0 2.6 %pad_maximum_fusion = bf16[80,100,256]{2,0,1:T(8,128)(2,1)S(1)} fusion(bf16[80,100,128]{2,0,1:T(8,128)(2,1)} %param.8, bf16[80,100,128]{2,0,1:T(8,128)(2,1)} %param.7), kind=kLoop, calls=%fused_computation.2 | loop fusion | flops 8192000 | bytes 8192000 | tf_op jit(solution)/shard_map/concatenate | solution.py:289
  4.1 3.9 %collective-permute-start = (bf16[1280,256]{1,0:T(8,128)(2,1)}, bf16[1280,256]{1,0:T(8,128)(2,1)S(1)}, u32[]{:S(2)}, u32[]{:S(2)}) collective-permute-start(bf16[1280,256]{1,0:T(8,128)(2,1)} %get-tuple-element.41), channel_id=1, source_target_pairs={{0,1},{1,2},{2,3},{3,0},{4,5},{5,6},{6,7},{7,4},{8,9},{9,10},{10,1... | collective-permute-start | bytes 1966088 | tf_op jit(solution)/shard_map/ppermute | solution.py:305
  8.0 3.2 %collective-permute-start.1 = (bf16[1280,256]{1,0:T(8,128)(2,1)}, bf16[1280,256]{1,0:T(8,128)(2,1)S(1)}, u32[]{:S(2)}, u32[]{:S(2)}) collective-permute-start(bf16[1280,256]{1,0:T(8,128)(2,1)} %get-tuple-element.40), channel_id=1, source_target_pairs={{0,3},{1,0},{2,1},{3,2},{4,7},{5,4},{6,5},{7,6},{8,11},{9,8},{10,9... | collective-permute-start | bytes 1966088 | tf_op jit(solution)/shard_map/ppermute | solution.py:305
  11.2 3.6 %collective-permute-start.2 = (bf16[1280,256]{1,0:T(8,128)(2,1)S(1)}, bf16[1280,256]{1,0:T(8,128)(2,1)S(1)}, u32[]{:S(2)}, u32[]{:S(2)}) collective-permute-start(bf16[1280,256]{1,0:T(8,128)(2,1)S(1)} %get-tuple-element.39), channel_id=1, source_target_pairs={{0,2},{1,3},{2,0},{3,1},{4,6},{5,7},{6,4},{7,5},{8,10},{9,11},{10,... | collective-permute-start | bytes 1966088 | tf_op jit(solution)/shard_map/ppermute | solution.py:305
  19.3 12.6 %all_to_all.35 = bf16[8,16,256]{2,1,0:T(8,128)(2,1)S(1)} all-to-all(bf16[8,16,256]{2,1,0:T(8,128)(2,1)S(1)} %maximum_select_fusion), channel_id=1, replica_groups=mesh['zl'=8,'yh'=2,'yl'=2,'c'=2,'zh'=2,'x'=4] {'yh','yl','c'}, dimensions={0} | all-to-all | bytes 131072 | tf_op jit(solution)/shard_map/all_to_all | solution.py:51
  32.6 10.6 %all-to-all-start.1 = ((bf16[8,16,256]{2,1,0:T(8,128)(2,1)}), bf16[8,16,256]{2,1,0:T(8,128)(2,1)S(1)}, u32[]{:S(2)}, u32[]{:S(2)}) async-start(bf16[8,16,256]{2,1,0:T(8,128)(2,1)} %broadcast_in_dim.41), calls=%async_computation.1 | async-start | bytes 131072 | tf_op jit(solution)/shard_map/all_to_all | solution.py:51
  43.2 9.8 %all-to-all-done.1 = bf16[8,16,256]{2,1,0:T(8,128)(2,1)S(1)} async-done(((bf16[8,16,256]{2,1,0:T(8,128)(2,1)}), bf16[8,16,256]{2,1,0:T(8,128)(2,1)S(1)}, u32[]{:S(2)}, u32[]{:S(2)}) %all-to-all-start.1) | async-done | bytes 65568 | tf_op jit(solution)/shard_map/all_to_all | solution.py:51
  53.7 5.6 %all-to-all-start.2 = ((bf16[32,16,256]{2,1,0:T(8,128)(2,1)}), bf16[32,16,256]{2,1,0:T(8,128)(2,1)S(1)}, u32[]{:S(2)}, u32[]{:S(2)}) async-start(bf16[32,16,256]{2,1,0:T(8,128)(2,1)} %broadcast_in_dim.42), calls=%async_computation.2 | async-start | bytes 524288 | tf_op jit(solution)/shard_map/all_to_all | solution.py:51
  59.4 2.3 %dynamic-slice_bitcast_fusion.4 = (bf16[720,256]{1,0:T(8,128)(2,1)}, bf16[720,256]{1,0:T(8,128)(2,1)}, bf16[720,256]{1,0:T(8,128)(2,1)}, bf16[720,256]{1,0:T(8,128)(2,1)S(1)}) fusion(bf16[4,2000,256]{2,1,0:T(8,128)(2,1)} %bitcast.52, s32[]{:T(128)S(6)} %select_n.182, s32[]{:T(128)S(6)} %add.259, s32[]{:T(128)S(6)} %select_n.180, s32[]{:T(128)S(6)} %select_n.178, ...), kind=kLoop, calls=%fused_computation.7 | loop fusion | bytes 2949140 | tf_op jit(solution)/shard_map/slice | solution.py:309
  61.7 3.3 %collective-permute-start.5 = (bf16[720,256]{1,0:T(8,128)(2,1)}, bf16[720,256]{1,0:T(8,128)(2,1)}, u32[]{:S(2)}, u32[]{:S(2)}) collective-permute-start(bf16[720,256]{1,0:T(8,128)(2,1)} %get-tuple-element.37), channel_id=1, source_target_pairs={{0,1},{1,2},{2,3},{3,0},{4,5},{5,6},{6,7},{7,4},{8,9},{9,10},{10,1... | collective-permute-start | bytes 1105928 | tf_op jit(solution)/shard_map/ppermute | solution.py:305
  65.0 3.2 %collective-permute-start.6 = (bf16[720,256]{1,0:T(8,128)(2,1)}, bf16[720,256]{1,0:T(8,128)(2,1)}, u32[]{:S(2)}, u32[]{:S(2)}) collective-permute-start(bf16[720,256]{1,0:T(8,128)(2,1)} %get-tuple-element.36), channel_id=1, source_target_pairs={{0,3},{1,0},{2,1},{3,2},{4,7},{5,4},{6,5},{7,6},{8,11},{9,8},{10,9... | collective-permute-start | bytes 1105928 | tf_op jit(solution)/shard_map/ppermute | solution.py:305
  68.2 3.6 %collective-permute-start.7 = (bf16[720,256]{1,0:T(8,128)(2,1)}, bf16[720,256]{1,0:T(8,128)(2,1)}, u32[]{:S(2)}, u32[]{:S(2)}) collective-permute-start(bf16[720,256]{1,0:T(8,128)(2,1)} %get-tuple-element.35), channel_id=1, source_target_pairs={{0,2},{1,3},{2,0},{3,1},{4,6},{5,7},{6,4},{7,5},{8,10},{9,11},{10,... | collective-permute-start | bytes 1105928 | tf_op jit(solution)/shard_map/ppermute | solution.py:305
  71.9 3.0 %shard_map.73 = (bf16[1296,128]{1,0:T(8,128)(2,1)S(1)}, bf16[1296,128]{1,0:T(8,128)(2,1)S(1)}) custom-call(s32[2]{0:T(128)S(1)} %pad_add_fusion.rank_ref, bf16[32,16,256]{2,1,0:T(8,128)(2,1)S(1)} %all-to-all-done.2.points_ref, bf16[1280,256]{1,0:T(8,128)(2,1)S(1)} %get-tuple-element.21.own, bf16[1280,256]{1,0:T(8,128)(2,1)S(1)} %collective-permute-done.left, ...), custom_call_target="tpu_custom_call" | custom-call | flops 2000000000 | bytes 5767168 | tf_op jit(solution)/shard_map/pallas_call | solution.py:79
  74.9 3.0 %collective-permute-start.3 = (bf16[1296,128]{1,0:T(8,128)(2,1)S(1)}, bf16[1296,128]{1,0:T(8,128)(2,1)S(1)}, u32[]{:S(2)}, u32[]{:S(2)}) collective-permute-start(bf16[1296,128]{1,0:T(8,128)(2,1)S(1)} %get-tuple-element.25), channel_id=1, source_target_pairs={{0,256},{8,268},{64,320},{72,332},{128,384},{136,396},{192,448},{2... | collective-permute-start | bytes 995336 | tf_op jit(solution)/shard_map/ppermute | solution.py:342
  78.0 6.1 %collective-permute-start.4 = (bf16[1296,128]{1,0:T(8,128)(2,1)S(1)}, bf16[1296,128]{1,0:T(8,128)(2,1)S(1)}, u32[]{:S(2)}, u32[]{:S(2)}) collective-permute-start(bf16[1296,128]{1,0:T(8,128)(2,1)S(1)} %get-tuple-element.26), channel_id=1, source_target_pairs={{0,260},{8,264},{64,324},{72,328},{128,388},{136,392},{192,452},{2... | collective-permute-start | bytes 995336 | tf_op jit(solution)/shard_map/ppermute | solution.py:342
  84.2 2.7 %shard_map.74 = (bf16[736,128]{1,0:T(8,128)(2,1)S(1)}, bf16[736,128]{1,0:T(8,128)(2,1)S(1)}) custom-call(s32[2]{0:T(128)S(1)} %pad_add_fusion.rank_ref, bf16[32,16,256]{2,1,0:T(8,128)(2,1)S(1)} %all-to-all-done.2.points_ref, bf16[720,256]{1,0:T(8,128)(2,1)S(1)} %get-tuple-element.38.own, bf16[720,256]{1,0:T(8,128)(2,1)} %collective-permute-done.5.left, ...), custom_call_target="tpu_custom_call" | custom-call | flops 2000000000 | bytes 3473408 | tf_op jit(solution)/shard_map/pallas_call | solution.py:79
  86.8 3.0 %collective-permute-start.8 = (bf16[736,128]{1,0:T(8,128)(2,1)S(1)}, bf16[736,128]{1,0:T(8,128)(2,1)S(1)}, u32[]{:S(2)}, u32[]{:S(2)}) collective-permute-start(bf16[736,128]{1,0:T(8,128)(2,1)S(1)} %get-tuple-element.27), channel_id=1, source_target_pairs={{0,256},{8,268},{64,320},{72,332},{128,384},{136,396},{192,448},{2... | collective-permute-start | bytes 565256 | tf_op jit(solution)/shard_map/ppermute | solution.py:342
  89.9 6.3 %collective-permute-start.9 = (bf16[736,128]{1,0:T(8,128)(2,1)S(1)}, bf16[736,128]{1,0:T(8,128)(2,1)S(1)}, u32[]{:S(2)}, u32[]{:S(2)}) collective-permute-start(bf16[736,128]{1,0:T(8,128)(2,1)S(1)} %get-tuple-element.28), channel_id=1, source_target_pairs={{0,260},{8,264},{64,324},{72,328},{128,388},{136,392},{192,452},{2... | collective-permute-start | bytes 565256 | tf_op jit(solution)/shard_map/ppermute | solution.py:342
  96.2 25.4 %collective-permute-done.8.below_b = bf16[736,128]{1,0:T(8,128)(2,1)S(1)} collective-permute-done((bf16[736,128]{1,0:T(8,128)(2,1)S(1)}, bf16[736,128]{1,0:T(8,128)(2,1)S(1)}, u32[]{:S(2)}, u32[]{:S(2)}) %collective-permute-start.8) | collective-permute-done | bytes 188448 | tf_op jit(solution)/shard_map/ppermute | solution.py:342
  121.6 6.9 %collective-permute-done.9.above_b = bf16[736,128]{1,0:T(8,128)(2,1)S(1)} collective-permute-done((bf16[736,128]{1,0:T(8,128)(2,1)S(1)}, bf16[736,128]{1,0:T(8,128)(2,1)S(1)}, u32[]{:S(2)}, u32[]{:S(2)}) %collective-permute-start.9) | collective-permute-done | bytes 188448 | tf_op jit(solution)/shard_map/ppermute | solution.py:342
  128.5 2.9 %shard_map.75 = f32[1280,128]{1,0:T(8,128)} custom-call(bf16[1296,128]{1,0:T(8,128)(2,1)S(1)} %collective-permute-done.3.below_a, bf16[1296,128]{1,0:T(8,128)(2,1)S(1)} %collective-permute-done.4.above_a, bf16[736,128]{1,0:T(8,128)(2,1)S(1)} %collective-permute-done.8.below_b, bf16[736,128]{1,0:T(8,128)(2,1)S(1)} %collective-permute-done.9.above_b, ...), custom_call_target="tpu_custom_call" | custom-call | flops 2000000000 | bytes 2131968 | tf_op jit(solution)/shard_map/pallas_call | solution.py:79
  131.4 3.5 %all-to-all-start.3 = ((f32[16,80,128]{2,1,0:T(8,128)}), f32[16,80,128]{2,1,0:T(8,128)S(1)}, u32[]{:S(2)}, u32[]{:S(2)}) async-start(f32[16,80,128]{2,1,0:T(8,128)} %bitcast.21), calls=%async_computation.3 | async-start | bytes 1310720 | tf_op jit(solution)/shard_map/all_to_all | solution.py:51
  135.7 7.9 %collective-permute-start.10 = (f32[128,128]{1,0:T(8,128)S(1)}, f32[128,128]{1,0:T(8,128)S(1)}, u32[]{:S(2)}, u32[]{:S(2)}) collective-permute-start(f32[128,128]{1,0:T(8,128)S(1)} %shard_map.77.mine_ref), channel_id=1, source_target_pairs={{0,4},{4,0},{1,5},{5,1},{2,6},{6,2},{3,7},{7,3},{8,12},{12,8},{9,1... | collective-permute-start | bytes 196616 | tf_op jit(solution)/shard_map/ppermute | solution.py:322
  143.6 2.0 all-to-all-done.3.in_ref
  145.6 2.5 %shard_map.76 = bf16[1280,128]{1,0:T(8,128)(2,1)} custom-call(f32[16,80,128]{2,1,0:T(8,128)S(1)} %all-to-all-done.3.in_ref, bf16[1600,256]{1,0:T(8,128)(2,1)S(1)} %copy-done.1), custom_call_target="tpu_custom_call" | custom-call | flops 2000000000 | bytes 2293760 | tf_op jit(solution)/shard_map/pallas_call | solution.py:79
  148.2 2.1 collective-permute-done.10.other_ref
  150.3 11.5 %all-to-all-start.4 = ((bf16[32,40,128]{2,1,0:T(8,128)(2,1)}), bf16[32,40,128]{2,1,0:T(8,128)(2,1)S(1)}, u32[]{:S(2)}, u32[]{:S(2)}) async-start(bf16[32,40,128]{2,1,0:T(8,128)(2,1)} %bitcast.22), calls=%async_computation.4 | async-start | bytes 655360 | tf_op jit(solution)/shard_map/all_to_all | solution.py:51
  162.5 6.0 %shard_map.78 = (f32[64,128]{1,0:T(8,128)S(1)}, f32[64,128]{1,0:T(8,128)S(1)}) custom-call(f32[128,128]{1,0:T(8,128)S(1)} %shard_map.77.mine_ref, f32[128,128]{1,0:T(8,128)S(1)} %collective-permute-done.10.other_ref), custom_call_target="tpu_custom_call" | custom-call | flops 2000000000 | bytes 131072 | tf_op jit(solution)/shard_map/pallas_call | solution.py:79
  168.5 14.7 %all-to-all-done.4.got_ref = bf16[32,40,128]{2,1,0:T(8,128)(2,1)S(1)} async-done(((bf16[32,40,128]{2,1,0:T(8,128)(2,1)}), bf16[32,40,128]{2,1,0:T(8,128)(2,1)S(1)}, u32[]{:S(2)}, u32[]{:S(2)}) %all-to-all-start.4) | async-done | bytes 327712 | tf_op jit(solution)/shard_map/all_to_all | solution.py:51
  183.2 2.2 shard_map.79
  185.3 17.1 %all_to_all.36 = f32[32,8,128]{2,1,0:T(8,128)S(1)} all-to-all(f32[32,8,128]{2,1,0:T(8,128)S(1)} %shard_map.79), channel_id=1, replica_groups=mesh['zl'=8,'yh'=2,'yl'=2,'c'=2,'zh'=2,'x'=4] {'yh','yl','c','x'}, dimensions={0} | all-to-all | bytes 262144 | tf_op jit(solution)/shard_map/all_to_all | solution.py:51
  202.5 14.4 %all_to_all.37 = f32[16,4,128]{2,1,0:T(4,128)S(1)} all-to-all(f32[16,4,128]{2,1,0:T(4,128)S(1)} %bitcast.53), channel_id=1, replica_groups=mesh['zl'=8,'yh'=2,'yl'=2,'c'=2,'zh'=2,'x'=4] {'zl','zh'}, dimensions={0} | all-to-all | bytes 65536 | tf_op jit(solution)/shard_map/all_to_all | solution.py:51
  (53 shorter events, 9.6 us)
Async XLA Ops:
  2.6 8.6 %copy-start.3 = (bf16[80,100,256]{2,0,1:T(8,128)(2,1)}, bf16[80,100,256]{2,0,1:T(8,128)(2,1)S(1)}, u32[]{:S(2)}) copy-start(bf16[80,100,256]{2,0,1:T(8,128)(2,1)S(1)} %pad_maximum_fusion) | copy-start | bytes 12288004
  2.6 12.2 %copy-start.4 = (s32[2,64]{1,0:T(2,128)S(1)}, s32[2,64]{1,0:T(2,128)}, u32[]{:S(2)}) copy-start(s32[2,64]{1,0:T(2,128)} %param.10) | copy-start | bytes 1540
  2.7 12.3 %copy-start.5 = (s32[128]{0:T(128)S(1)}, s32[128]{0:T(128)}, u32[]{:S(2)}) copy-start(s32[128]{0:T(128)} %param.9) | copy-start | bytes 1540
  4.1 48.9 %collective-permute-start = (bf16[1280,256]{1,0:T(8,128)(2,1)}, bf16[1280,256]{1,0:T(8,128)(2,1)S(1)}, u32[]{:S(2)}, u32[]{:S(2)}) collective-permute-start(bf16[1280,256]{1,0:T(8,128)(2,1)} %get-tuple-element.41), channel_id=1, source_target_pairs={{0,1},{1,2},{2,3},{3,0},{4,5},{5,6},{6,7},{7,4},{8,9},{9,10},{10,1... | collective-permute-start | bytes 1966088 | tf_op jit(solution)/shard_map/ppermute | solution.py:305
  8.0 44.9 %collective-permute-start.1 = (bf16[1280,256]{1,0:T(8,128)(2,1)}, bf16[1280,256]{1,0:T(8,128)(2,1)S(1)}, u32[]{:S(2)}, u32[]{:S(2)}) collective-permute-start(bf16[1280,256]{1,0:T(8,128)(2,1)} %get-tuple-element.40), channel_id=1, source_target_pairs={{0,3},{1,0},{2,1},{3,2},{4,7},{5,4},{6,5},{7,6},{8,11},{9,8},{10,9... | collective-permute-start | bytes 1966088 | tf_op jit(solution)/shard_map/ppermute | solution.py:305
  11.2 41.7 %collective-permute-start.2 = (bf16[1280,256]{1,0:T(8,128)(2,1)S(1)}, bf16[1280,256]{1,0:T(8,128)(2,1)S(1)}, u32[]{:S(2)}, u32[]{:S(2)}) collective-permute-start(bf16[1280,256]{1,0:T(8,128)(2,1)S(1)} %get-tuple-element.39), channel_id=1, source_target_pairs={{0,2},{1,3},{2,0},{3,1},{4,6},{5,7},{6,4},{7,5},{8,10},{9,11},{10,... | collective-permute-start | bytes 1966088 | tf_op jit(solution)/shard_map/ppermute | solution.py:305
  32.6 20.3 %all-to-all-start.1 = ((bf16[8,16,256]{2,1,0:T(8,128)(2,1)}), bf16[8,16,256]{2,1,0:T(8,128)(2,1)S(1)}, u32[]{:S(2)}, u32[]{:S(2)}) async-start(bf16[8,16,256]{2,1,0:T(8,128)(2,1)} %broadcast_in_dim.41), calls=%async_computation.1 | async-start | bytes 131072 | tf_op jit(solution)/shard_map/all_to_all | solution.py:51
  53.7 18.2 %all-to-all-start.2 = ((bf16[32,16,256]{2,1,0:T(8,128)(2,1)}), bf16[32,16,256]{2,1,0:T(8,128)(2,1)S(1)}, u32[]{:S(2)}, u32[]{:S(2)}) async-start(bf16[32,16,256]{2,1,0:T(8,128)(2,1)} %broadcast_in_dim.42), calls=%async_computation.2 | async-start | bytes 524288 | tf_op jit(solution)/shard_map/all_to_all | solution.py:51
  61.7 22.4 %collective-permute-start.5 = (bf16[720,256]{1,0:T(8,128)(2,1)}, bf16[720,256]{1,0:T(8,128)(2,1)}, u32[]{:S(2)}, u32[]{:S(2)}) collective-permute-start(bf16[720,256]{1,0:T(8,128)(2,1)} %get-tuple-element.37), channel_id=1, source_target_pairs={{0,1},{1,2},{2,3},{3,0},{4,5},{5,6},{6,7},{7,4},{8,9},{9,10},{10,1... | collective-permute-start | bytes 1105928 | tf_op jit(solution)/shard_map/ppermute | solution.py:305
  65.0 19.2 %collective-permute-start.6 = (bf16[720,256]{1,0:T(8,128)(2,1)}, bf16[720,256]{1,0:T(8,128)(2,1)}, u32[]{:S(2)}, u32[]{:S(2)}) collective-permute-start(bf16[720,256]{1,0:T(8,128)(2,1)} %get-tuple-element.36), channel_id=1, source_target_pairs={{0,3},{1,0},{2,1},{3,2},{4,7},{5,4},{6,5},{7,6},{8,11},{9,8},{10,9... | collective-permute-start | bytes 1105928 | tf_op jit(solution)/shard_map/ppermute | solution.py:305
  68.2 16.0 %collective-permute-start.7 = (bf16[720,256]{1,0:T(8,128)(2,1)}, bf16[720,256]{1,0:T(8,128)(2,1)}, u32[]{:S(2)}, u32[]{:S(2)}) collective-permute-start(bf16[720,256]{1,0:T(8,128)(2,1)} %get-tuple-element.35), channel_id=1, source_target_pairs={{0,2},{1,3},{2,0},{3,1},{4,6},{5,7},{6,4},{7,5},{8,10},{9,11},{10,... | collective-permute-start | bytes 1105928 | tf_op jit(solution)/shard_map/ppermute | solution.py:305
  74.9 53.5 %copy-start.2 = (bf16[160,80]{1,0:T(8,128)(2,1)S(1)}, bf16[160,80]{1,0:T(8,128)(2,1)}, u32[]{:S(2)}) copy-start(bf16[160,80]{1,0:T(8,128)(2,1)} %constant.153.clone.basis_ref) | copy-start | bytes 76804
  74.9 53.5 %collective-permute-start.3 = (bf16[1296,128]{1,0:T(8,128)(2,1)S(1)}, bf16[1296,128]{1,0:T(8,128)(2,1)S(1)}, u32[]{:S(2)}, u32[]{:S(2)}) collective-permute-start(bf16[1296,128]{1,0:T(8,128)(2,1)S(1)} %get-tuple-element.25), channel_id=1, source_target_pairs={{0,256},{8,268},{64,320},{72,332},{128,384},{136,396},{192,448},{2... | collective-permute-start | bytes 995336 | tf_op jit(solution)/shard_map/ppermute | solution.py:342
  78.0 50.5 %collective-permute-start.4 = (bf16[1296,128]{1,0:T(8,128)(2,1)S(1)}, bf16[1296,128]{1,0:T(8,128)(2,1)S(1)}, u32[]{:S(2)}, u32[]{:S(2)}) collective-permute-start(bf16[1296,128]{1,0:T(8,128)(2,1)S(1)} %get-tuple-element.26), channel_id=1, source_target_pairs={{0,260},{8,264},{64,324},{72,328},{128,388},{136,392},{192,452},{2... | collective-permute-start | bytes 995336 | tf_op jit(solution)/shard_map/ppermute | solution.py:342
  86.8 34.7 %collective-permute-start.8 = (bf16[736,128]{1,0:T(8,128)(2,1)S(1)}, bf16[736,128]{1,0:T(8,128)(2,1)S(1)}, u32[]{:S(2)}, u32[]{:S(2)}) collective-permute-start(bf16[736,128]{1,0:T(8,128)(2,1)S(1)} %get-tuple-element.27), channel_id=1, source_target_pairs={{0,256},{8,268},{64,320},{72,332},{128,384},{136,396},{192,448},{2... | collective-permute-start | bytes 565256 | tf_op jit(solution)/shard_map/ppermute | solution.py:342
  89.9 55.8 %copy-start.1 = (bf16[1600,256]{1,0:T(8,128)(2,1)S(1)}, bf16[1600,256]{1,0:T(8,128)(2,1)}, u32[]{:S(2)}) copy-start(bf16[1600,256]{1,0:T(8,128)(2,1)} %constant.154.clone.table_ref) | copy-start | bytes 2457604
  89.9 38.6 %collective-permute-start.9 = (bf16[736,128]{1,0:T(8,128)(2,1)S(1)}, bf16[736,128]{1,0:T(8,128)(2,1)S(1)}, u32[]{:S(2)}, u32[]{:S(2)}) collective-permute-start(bf16[736,128]{1,0:T(8,128)(2,1)S(1)} %get-tuple-element.28), channel_id=1, source_target_pairs={{0,260},{8,264},{64,324},{72,328},{128,388},{136,392},{192,452},{2... | collective-permute-start | bytes 565256 | tf_op jit(solution)/shard_map/ppermute | solution.py:342
  131.4 14.3 %all-to-all-start.3 = ((f32[16,80,128]{2,1,0:T(8,128)}), f32[16,80,128]{2,1,0:T(8,128)S(1)}, u32[]{:S(2)}, u32[]{:S(2)}) async-start(f32[16,80,128]{2,1,0:T(8,128)} %bitcast.21), calls=%async_computation.3 | async-start | bytes 1310720 | tf_op jit(solution)/shard_map/all_to_all | solution.py:51
  135.7 14.6 %collective-permute-start.10 = (f32[128,128]{1,0:T(8,128)S(1)}, f32[128,128]{1,0:T(8,128)S(1)}, u32[]{:S(2)}, u32[]{:S(2)}) collective-permute-start(f32[128,128]{1,0:T(8,128)S(1)} %shard_map.77.mine_ref), channel_id=1, source_target_pairs={{0,4},{4,0},{1,5},{5,1},{2,6},{6,2},{3,7},{7,3},{8,12},{12,8},{9,1... | collective-permute-start | bytes 196616 | tf_op jit(solution)/shard_map/ppermute | solution.py:322
  150.3 32.8 %all-to-all-start.4 = ((bf16[32,40,128]{2,1,0:T(8,128)(2,1)}), bf16[32,40,128]{2,1,0:T(8,128)(2,1)S(1)}, u32[]{:S(2)}, u32[]{:S(2)}) async-start(bf16[32,40,128]{2,1,0:T(8,128)(2,1)} %bitcast.22), calls=%async_computation.4 | async-start | bytes 655360 | tf_op jit(solution)/shard_map/all_to_all | solution.py:51
  162.3 20.8 %copy-start = (bf16[1120,640]{1,0:T(8,128)(2,1)S(1)}, bf16[1120,640]{1,0:T(8,128)(2,1)}, u32[]{:S(2)}) copy-start(bf16[1120,640]{1,0:T(8,128)(2,1)} %constant.155.clone.table_ref) | copy-start | bytes 4300804
